TPU v7x, 128 devices: a whole 4x4x4 slice. The times are simulated.
128 devices in a mesh: dp: 8 (over y, core), seq: 16 (over x, z).
Axes of the slice: x: 4, y: 4, z: 4, core: 2. Of those that a mesh axis runs over, the one named last changes fastest.
Arguments:
- tokens: bfloat16 [8, 4096, 768], P('dp', 'seq'), may hold values from -6 to 6
- starts: int32 [8, 16], P('dp', 'seq'), may hold values from 0 to 1, as said below
- g_in: float32 [768], replicated, may hold values from 0.5 to 1.5
- w_in: bfloat16 [768, 3328], P('dp'), may hold values from -0.21875 to 0.21875
- w_dt: bfloat16 [768, 48], P('dp'), may hold values from -0.21875 to 0.21875
- conv_w: float32 [4, 1792], replicated, may hold values from -3 to 3
- conv_b: float32 [1792], replicated, may hold values from -3 to 3
- dt_bias: float32 [48], replicated, may hold values from -4.5 to -2.5
- a_log: float32 [24], replicated, as said below
- dskip: float32 [24], replicated, may hold values from 0.5 to 1.5
- g_out: float32 [1536], replicated, may hold values from 0.5 to 1.5
- w_out: bfloat16 [1536, 768], P('dp'), may hold values from -0.15625 to 0.15625
- d_out: bfloat16 [8, 4096, 768], P('dp', 'seq'), may hold values from -6 to 6
Outputs:
- out: bfloat16 [8, 4096, 768], P('dp', 'seq')
- d_tokens: float32 [8, 4096, 768], P('dp', 'seq')
- d_g_in: float32 [768], replicated
- d_w_in: float32 [768, 3328], P('dp')
- d_w_dt: float32 [768, 48], P('dp')
- d_conv_w: float32 [4, 1792], replicated
- d_conv_b: float32 [1792], replicated
- d_dt_bias: float32 [48], replicated
- d_a_log: float32 [24], replicated
- d_dskip: float32 [24], replicated
- d_g_out: float32 [1536], replicated
- d_w_out: float32 [1536, 768], P('dp')
Inputs may be any that keep to these rules, and one draw needn't show every extreme that they name: `starts`: the first block of every group is 1; a 1 stands only at block indices that are multiples of 4; in one group, drawn from the seed, only the first block is 1. `a_log`: each value lies between log(0.5 / (0.03 * 4096)) and 4 above it.
All inputs are finite; a program needn't handle non-finite values.
Results may differ from a plain program's by a relative error of at most 0.025.
Values may be sent and summed in bfloat16 or wider, within the bound.
No kernel may reach another device: no remote copies, remote signals or barrier semaphores. Data moves between devices by JAX's collectives and lax.ppermute only.
A program may use at most 192 MiB of HBM per device.

v0:
```python
from functools import partial

import jax
import jax.numpy as jnp
from jax import lax
from jax.sharding import PartitionSpec as P

EPSILON = 1e-05
EXACT = lax.Precision.HIGHEST
span_rows = 128


def from_behind(value, axis, steps):
    count = lax.axis_size(axis)
    leading, last = (max(0, -steps), min(count, count - steps))
    return lax.ppermute(value, axis, [(source, source + steps) for source in range(leading, last)])


def carried_in(x, axis, combine, identity, reverse):
    size, index = (lax.axis_size(axis), lax.axis_index(axis))
    everything = jax.tree.map(
        lambda part, kind: lax.all_gather(part.astype(kind), axis), x, (jnp.bfloat16, jnp.bfloat16)
    )
    start = jax.tree.map(
        lambda part, zero: jnp.broadcast_to(jnp.asarray(zero, part.dtype), part.shape), x, identity
    )

    def lap(k, before):
        at = size - 1 - k if reverse else k
        reached = at > index if reverse else at < index
        new = combine(
            before, jax.tree.map(lambda part, own: part[at].astype(own.dtype), everything, x)
        )
        return jax.tree.map(lambda a, b: jnp.where(reached, a, b), new, before)

    return lax.fori_loop(0, size, lap, start)


def entering_2(x, axis, join, neutral, backward):
    count = lax.axis_size(axis)
    place = lax.axis_index(axis)
    ahead = count - 1 - place if backward else place
    gathered = jax.tree.map(
        lambda a, kind: lax.all_gather(a.astype(kind), axis),
        x,
        jax.tree.map(lambda a: jnp.bfloat16 if a.dtype == jnp.float32 else a.dtype, x),
    )
    state = jax.tree.map(lambda a, e: jnp.zeros_like(a) + jnp.asarray(e, a.dtype), x, neutral)

    def one(lap, state):
        source = count - 1 - lap if backward else lap
        return join(
            state,
            jax.tree.map(
                lambda a, own: lax.dynamic_index_in_dim(a, source, 0, False).astype(own.dtype),
                gathered,
                x,
            ),
        )

    return lax.fori_loop(0, ahead, one, state)


def rms_scale(values, scale_gain):
    return (
        values * lax.rsqrt(jnp.mean(values * values, axis=-1, keepdims=True) + EPSILON) * scale_gain
    )


def decay_matrix(gaps, mask):
    return jnp.where(mask, jnp.exp(jnp.where(mask, gaps, 0.0)), 0.0)


def conv_inner(
    conv_input,
    halo_rows,
    step_raw,
    conv_w,
    conv_b,
    dt_bias,
    a_log,
    continued,
    inner_width,
    state_width,
):
    conv_width = conv_w.shape[0]
    block_len = conv_input.shape[0]
    num_heads = a_log.shape[0]
    extended = jnp.concatenate([halo_rows * continued, conv_input], axis=0)
    conv_sum = conv_b + conv_w[0] * extended[0:block_len]
    for tap in range(1, conv_width):
        conv_sum = conv_sum + conv_w[tap] * extended[tap : tap + block_len]
    activated = jax.nn.silu(conv_sum)
    x_heads = activated[:, :inner_width].reshape(block_len, num_heads, -1)
    b_fwd = activated[:, inner_width : inner_width + state_width]
    c_fwd = activated[:, inner_width + state_width : inner_width + 2 * state_width]
    b_rev = activated[:, inner_width + 2 * state_width : inner_width + 3 * state_width]
    c_rev = activated[:, inner_width + 3 * state_width : inner_width + 4 * state_width]
    dt_all = jax.nn.softplus(step_raw + dt_bias)
    rates = jnp.exp(a_log)
    dt_fwd = dt_all[:, :num_heads]
    dt_rev = dt_all[:, num_heads:]
    return (x_heads, b_fwd, c_fwd, b_rev, c_rev, dt_fwd, dt_rev, -dt_fwd * rates, -dt_rev * rates)


def reverse_cumsum(values):
    return jnp.flip(jnp.cumsum(jnp.flip(values, 0), axis=0), 0)


def block_states(inner_vals, continued):
    x_heads, b_fwd, c_fwd, b_rev, c_rev, dt_fwd, dt_rev, la_fwd, la_rev = inner_vals
    cum_fwd = jnp.cumsum(la_fwd, axis=0)
    last_cum = cum_fwd[-1]
    scaled_fwd = (jnp.exp(last_cum[None] - cum_fwd) * dt_fwd)[..., None] * x_heads
    state_fwd = jnp.einsum("sn,shp->hnp", b_fwd, scaled_fwd, precision=EXACT)
    cum_rev = reverse_cumsum(la_rev)
    first_cum = cum_rev[0]
    scaled_rev = (jnp.exp(first_cum[None] - cum_rev) * dt_rev)[..., None] * x_heads
    state_rev = jnp.einsum("sn,shp->hnp", b_rev, scaled_rev, precision=EXACT)
    return (
        continued * jnp.exp(last_cum),
        state_fwd,
        continued * jnp.exp(first_cum),
        state_rev * continued,
    )


def local_mix(x_heads, b_mat, c_mat, dt_mat, cum_mat):
    positions = jnp.arange(x_heads.shape[0])
    cum_heads = cum_mat.T
    decays = decay_matrix(
        cum_heads[:, :, None] - cum_heads[:, None, :], positions[:, None] > positions[None, :]
    )
    c_dot_b = jnp.dot(c_mat, b_mat.T, precision=EXACT)
    weights = decays * c_dot_b[None] * dt_mat.T[:, None, :]
    return jnp.einsum("hts,shp->thp", weights, x_heads, precision=EXACT)


def forward_spans(x_heads, b_mat, c_mat, dt_mat, la_mat, incoming):
    block_len, num_heads, head_size = x_heads.shape
    span = min(span_rows, block_len)
    count = block_len // span
    x_parts = x_heads.reshape(count, span, num_heads, head_size)
    b_parts = b_mat.reshape(count, span, -1)
    c_parts = c_mat.reshape(count, span, -1)
    dt_parts = dt_mat.reshape(count, span, num_heads)
    cum_parts = jnp.cumsum(la_mat.reshape(count, span, num_heads), axis=1)
    inside = jax.vmap(local_mix)(x_parts, b_parts, c_parts, dt_parts, cum_parts)
    last_cum = cum_parts[:, -1, :]
    scaled_parts = (jnp.exp(last_cum[:, None, :] - cum_parts) * dt_parts)[..., None] * x_parts
    span_states = jnp.einsum("csn,cshp->chnp", b_parts, scaled_parts, precision=EXACT)
    running = incoming
    entering_list = []
    for span_index in range(count):
        entering_list.append(running)
        running = jnp.exp(last_cum[span_index])[:, None, None] * running + span_states[span_index]
    entering = jnp.stack(entering_list)
    result = inside + jnp.exp(cum_parts)[..., None] * jnp.einsum(
        "ctn,chnp->cthp", c_parts, entering, precision=EXACT
    )
    return result.reshape(block_len, num_heads, head_size)


def mix_tokens(inner_vals, incoming_left, incoming_right, gate_in, dskip, g_out, continued):
    x_heads, b_fwd, c_fwd, b_rev, c_rev, dt_fwd, dt_rev, la_fwd, la_rev = inner_vals
    block_len = x_heads.shape[0]
    fwd_part = forward_spans(x_heads, b_fwd, c_fwd, dt_fwd, la_fwd, incoming_left * continued)
    rev_part = jnp.flip(
        forward_spans(
            jnp.flip(x_heads, 0),
            jnp.flip(b_rev, 0),
            jnp.flip(c_rev, 0),
            jnp.flip(dt_rev, 0),
            jnp.flip(la_rev, 0),
            incoming_right,
        ),
        0,
    )
    mix_all = (fwd_part + rev_part + x_heads * dskip[:, None]).reshape(block_len, -1)
    gated = mix_all * jax.nn.silu(gate_in)
    return rms_scale(gated, g_out)


def combine(earlier, later):
    return (later[0] * earlier[0], later[0][:, None, None] * earlier[1] + later[1])


def contract_rows(left, right):
    return lax.dot_general(
        left, right, (((0,), (0,)), ((), ())), preferred_element_type=jnp.float32
    )


def contract_cols(left, right):
    return lax.dot_general(
        left, right, (((1,), (1,)), ((), ())), preferred_element_type=jnp.float32
    )


def local(
    tokens, starts, g_in, w_in, w_dt, conv_w, conv_b, dt_bias, a_log, dskip, g_out, w_out, d_out
):
    inner_width = g_out.shape[0]
    num_heads = a_log.shape[0]
    state_width = (conv_b.shape[0] - inner_width) // 4
    head_size = inner_width // num_heads
    conv_width = conv_w.shape[0]
    continued = (1 - starts[0, 0]).astype(jnp.float32)
    x_float = tokens[0].astype(jnp.float32)
    full_in, full_dt, full_out = (
        lax.all_gather(w_in, "dp", axis=0, tiled=True),
        lax.all_gather(w_dt, "dp", axis=0, tiled=True),
        lax.all_gather(w_out, "dp", axis=0, tiled=True),
    )
    normed_float, front_pull = jax.vjp(rms_scale, x_float, g_in)
    normed_in = normed_float.astype(jnp.bfloat16)
    projected = jnp.dot(normed_in, full_in, preferred_element_type=jnp.float32)
    step_raw = jnp.dot(normed_in, full_dt, preferred_element_type=jnp.float32)
    gate_in = projected[:, :inner_width]
    conv_input = projected[:, inner_width:].astype(jnp.bfloat16)
    halo_rows = from_behind(conv_input[-(conv_width - 1) :], "seq", 1)
    conv_fn = partial(
        conv_inner, continued=continued, inner_width=inner_width, state_width=state_width
    )
    inner_vals, conv_pull = jax.vjp(
        conv_fn,
        conv_input.astype(jnp.float32),
        halo_rows.astype(jnp.float32),
        step_raw,
        conv_w,
        conv_b,
        dt_bias,
        a_log,
    )
    block_ends, ends_pull = jax.vjp(partial(block_states, continued=continued), inner_vals)
    identity = (
        jnp.ones((num_heads,), jnp.float32),
        jnp.zeros((num_heads, state_width, head_size), jnp.float32),
    )
    incoming_left = carried_in((block_ends[0], block_ends[1]), "seq", combine, identity, False)[1]
    incoming_right = carried_in((block_ends[2], block_ends[3]), "seq", combine, identity, True)[1]
    normed_out, mix_pull = jax.vjp(
        partial(mix_tokens, continued=continued),
        inner_vals,
        incoming_left,
        incoming_right,
        gate_in,
        dskip,
        g_out,
    )
    mixed_low = normed_out.astype(jnp.bfloat16)
    branch = jnp.dot(mixed_low, full_out, preferred_element_type=jnp.float32)
    output = (x_float + branch).astype(jnp.bfloat16)[None]
    upstream = d_out[0]
    d_mixed = contract_cols(upstream, full_out)
    grad_out_w = contract_rows(mixed_low, upstream)
    d_inner, d_left, d_right, d_gate, d_dskip, d_gout = mix_pull(d_mixed)
    carry_back = entering_2((block_ends[0], d_left), "seq", combine, identity, True)[1]
    carry_ahead = entering_2((block_ends[2], d_right), "seq", combine, identity, False)[1]
    d_ends = (
        jnp.sum(carry_back * incoming_left, axis=(1, 2)),
        carry_back,
        jnp.sum(carry_ahead * incoming_right, axis=(1, 2)),
        carry_ahead,
    )
    (d_inner_ends,) = ends_pull(d_ends)
    d_inner = jax.tree.map(jnp.add, d_inner, d_inner_ends)
    d_conv_input, d_halo, d_step, d_conv_w, d_conv_b, d_dt_bias, d_a_log = conv_pull(d_inner)
    d_tail = from_behind(d_halo, "seq", -1)
    d_conv_input = jnp.concatenate(
        [d_conv_input[: -(conv_width - 1)], d_conv_input[-(conv_width - 1) :] + d_tail], axis=0
    )
    d_projected = jnp.concatenate([d_gate, d_conv_input], axis=1).astype(jnp.bfloat16)
    d_step_low = d_step.astype(jnp.bfloat16)
    d_normed = contract_cols(d_projected, full_in) + contract_cols(d_step_low, full_dt)
    grad_in_w = contract_rows(normed_in, d_projected)
    grad_dt_w = contract_rows(normed_in, d_step_low)
    d_x, d_gin = front_pull(d_normed)
    d_tokens = (upstream.astype(jnp.float32) + d_x)[None]
    summed = (
        lax.psum(grad_in_w.astype(jnp.bfloat16), "seq").astype(jnp.float32),
        lax.psum(grad_dt_w.astype(jnp.bfloat16), "seq").astype(jnp.float32),
        lax.psum(grad_out_w.astype(jnp.bfloat16), "seq").astype(jnp.float32),
        lax.psum(d_gin.astype(jnp.bfloat16), "seq").astype(jnp.float32),
        lax.psum(d_conv_w.astype(jnp.bfloat16), "seq").astype(jnp.float32),
        lax.psum(d_conv_b.astype(jnp.bfloat16), "seq").astype(jnp.float32),
        lax.psum(d_dt_bias.astype(jnp.bfloat16), "seq").astype(jnp.float32),
        lax.psum(d_a_log.astype(jnp.bfloat16), "seq").astype(jnp.float32),
        lax.psum(d_dskip.astype(jnp.bfloat16), "seq").astype(jnp.float32),
        lax.psum(d_gout.astype(jnp.bfloat16), "seq").astype(jnp.float32),
    )
    shard_in, shard_dt, shard_out = (
        lax.psum_scatter(
            summed[0].astype(jnp.bfloat16), "dp", scatter_dimension=0, tiled=True
        ).astype(jnp.float32),
        lax.psum_scatter(
            summed[1].astype(jnp.bfloat16), "dp", scatter_dimension=0, tiled=True
        ).astype(jnp.float32),
        lax.psum_scatter(
            summed[2].astype(jnp.bfloat16), "dp", scatter_dimension=0, tiled=True
        ).astype(jnp.float32),
    )
    small_grads = summed[3:]
    totals = (
        lax.psum(small_grads[0].astype(jnp.bfloat16), "dp").astype(jnp.float32),
        lax.psum(small_grads[1].astype(jnp.bfloat16), "dp").astype(jnp.float32),
        lax.psum(small_grads[2].astype(jnp.bfloat16), "dp").astype(jnp.float32),
        lax.psum(small_grads[3].astype(jnp.bfloat16), "dp").astype(jnp.float32),
        lax.psum(small_grads[4].astype(jnp.bfloat16), "dp").astype(jnp.float32),
        lax.psum(small_grads[5].astype(jnp.bfloat16), "dp").astype(jnp.float32),
        lax.psum(small_grads[6].astype(jnp.bfloat16), "dp").astype(jnp.float32),
    )
    return (
        output,
        d_tokens,
        totals[0],
        shard_in,
        shard_dt,
        totals[1],
        totals[2],
        totals[3],
        totals[4],
        totals[5],
        totals[6],
        shard_out,
    )


def solution(mesh):
    return jax.shard_map(
        local,
        mesh=mesh,
        in_specs=(
            P("dp", "seq", None),
            P("dp", "seq"),
            P(),
            P("dp", None),
            P("dp", None),
            P(),
            P(),
            P(),
            P(),
            P(),
            P(),
            P("dp", None),
            P("dp", "seq", None),
        ),
        out_specs=(
            P("dp", "seq", None),
            P("dp", "seq", None),
            P(),
            P("dp", None),
            P("dp", None),
            P(),
            P(),
            P(),
            P(),
            P(),
            P(),
            P("dp", None),
        ),
        check_vma=False,
    )
```

profile of v0, /device:TPU:0, one launch (start us, length us, event | category | flops | bytes accessed | tf_op | source)
XLA Modules:
  0.0 683.4 jit_solution(7616835533709243600)
XLA Ops:
  9.3 13.5 %all-gather.2 = bf16[8,96,48]{1,2,0:T(8,128)(2,1)S(1)} all-gather(bf16[1,96,48]{1,2,0:T(8,128)(2,1)} %bitcast.516), channel_id=1, replica_groups=mesh['dp'=8,'seq'=16] {'dp'}, dimensions={0}, use_global_device_ids=true | all-gather | bytes 82944 | tf_op jit(solution)/shard_map/all_gather | solution.py:212
  31.3 16.8 %all-gather.12.cloned.1.call-done = bf16[768,3328]{1,0:T(8,128)(2,1)} async-done(((bf16[96,3328]{1,0:T(8,128)(2,1)}), bf16[768,3328]{1,0:T(8,128)(2,1)}) %all-gather.12.cloned.1.call-update) | async-done | bytes 5111824 | tf_op jit(solution)/shard_map/all_gather | solution.py:211
  48.2 5.7 fusion.252
  64.8 4.0 fusion.119
  81.0 22.8 %all-gather.3 = bf16[16,1,24]{2,1,0:T(2,128)(2,1)S(1)} all-gather(bf16[1,1,24]{2,1,0:T(2,128)(2,1)} %get-tuple-element.566), channel_id=1, replica_groups=mesh['dp'=8,'seq'=16] {'seq'}, dimensions={0}, use_global_device_ids=true | all-gather | bytes 816 | tf_op jit(solution)/shard_map/all_gather | solution.py:22
  104.3 19.5 %all-gather.4 = bf16[16,1,24]{2,1,0:T(2,128)(2,1)S(1)} all-gather(bf16[1,1,24]{2,1,0:T(2,128)(2,1)} %get-tuple-element.568), channel_id=1, replica_groups=mesh['dp'=8,'seq'=16] {'seq'}, dimensions={0}, use_global_device_ids=true | all-gather | bytes 816 | tf_op jit(solution)/shard_map/all_gather | solution.py:22
  151.7 47.5 %while.59 = (s32[]{:T(128)}, f32[24,64,64]{2,1,0:T(8,128)}, s32[]{:T(128)}, bf16[16,24]{1,0:T(8,128)(2,1)}, bf16[16,24,64,64]{3,2,1,0:T(8,128)(2,1)}, /*index=5*/s32[]{:T(128)}, s32[]{:T(128)}, s32[]{:T(128)}, s32[]{:T(128)}) while((s32[]{:T(128)}, f32[24,64,64]{2,1,0:T(8,128)}, s32[]{:T(128)}, bf16[16,24]{1,0:T(8,128)(2,1)}, ...), condition=%wide.region_10.11_spmd.clone, body=%wide.region_9.10_spmd.clone.sunk | while | flops 491552 | bytes 983455 | solution.py:36
  199.2 47.5 %while.58 = (s32[]{:T(128)}, f32[24,64,64]{2,1,0:T(8,128)}, s32[]{:T(128)}, bf16[16,24]{1,0:T(8,128)(2,1)}, bf16[16,24,64,64]{3,2,1,0:T(8,128)(2,1)}, /*index=5*/s32[]{:T(128)}, s32[]{:T(128)}) while((s32[]{:T(128)}, f32[24,64,64]{2,1,0:T(8,128)}, s32[]{:T(128)}, bf16[16,24]{1,0:T(8,128)(2,1)}, bf16[16,24,64,64]{3,2,1,0:T(8,128)(2,1)}, ...), condition=%wide.region_5.6_spmd.clone, body=%wide.region_4.5_spmd.clone.sunk | while | flops 491548 | bytes 983393 | solution.py:36
  255.3 6.4 fusion.49
  263.0 4.3 rev.58
  272.7 6.4 fusion.50
  287.7 4.6 multiply_reduce_fusion.9
  324.5 4.1 rev.62
  328.6 4.3 fusion.147
  333.1 5.3 fusion.78
  338.5 10.9 %fusion.22 = (f32[2,24,128]{2,1,0:T(8,128)}, f32[2,24,128]{2,1,0:T(8,128)}, f32[2,24,128]{2,1,0:T(8,128)}, f32[2,128,128]{2,1,0:T(8,128)S(1)}, f32[2,128,128]{2,...) fusion(f32[2,24,128]{2,1,0:T(8,128)S(1)} %copy-done.122, ...), kind=kOutput, calls=%fused_computation.51 | convolution fusion | flops 627470336 | bytes 7077888 | tf_op jit(solution)/shard_map/transpose(jvp(vmap(hts,shp->thp)))/dot_general | solution.py:136
  360.0 4.2 fusion.146
  372.8 5.1 multiply_reduce_fusion.12
  380.2 6.3 fusion.35
  386.7 28.8 %while.57 = (s32[]{:T(128)}, f32[24,64,64]{2,1,0:T(8,128)S(1)}, s32[]{:T(128)}, bf16[16,24]{1,0:T(8,128)(2,1)}, bf16[16,24,64,64]{3,2,1,0:T(8,128)(2,1)}, /*index=5*/s32[]{:T(128)}, s32[]{:T(128)}, s32[]{:T(128)}, s32[]{:T(128)}) while((s32[]{:T(128)}, f32[24,64,64]{2,1,0:T(8,128)S(1)}, s32[]{:T(128)}, bf16[16,24]{1,0:T(8,128)(2,1)}, ...), condition=%wide.region_18.19_spmd, body=%wide.region_17.18_spmd.sunk | while | flops 294942 | bytes 983435 | solution.py:61
  415.5 10.3 %all-gather.16.cloned.1.call-done = bf16[16,24,64,64]{3,2,1,0:T(8,128)(2,1)} async-done(((bf16[1,24,64,64]{3,2,1,0:T(8,128)(2,1)}), bf16[16,24,64,64]{3,2,1,0:T(8,128)(2,1)}) %all-gather.16.cloned.1.call-update) | async-done | bytes 3145744 | tf_op jit(solution)/shard_map/all_gather | solution.py:44
  429.8 5.7 multiply_reduce_fusion.13
  438.7 3.9 fusion.140
  442.7 6.0 fusion.143
  448.8 4.1 multiply_reduce_fusion.6
  455.7 4.6 collective-permute-done.1
  460.4 3.9 convolution_convert_fusion
  512.1 17.2 %reduce-scatter.6.cloned.1.call-done = bf16[96,3328]{1,0:T(8,128)(2,1)} async-done(((bf16[768,3328]{1,0:T(8,128)(2,1)}), bf16[96,3328]{1,0:T(8,128)(2,1)}) %reduce-scatter.6.cloned.1.call-update) | async-done | bytes 638992 | tf_op jit(solution)/shard_map/reduce_scatter | solution.py:293
  529.4 4.2 fusion.159
  534.8 33.0 %reduce-scatter.10.cloned.1.call-done = bf16[96,48]{1,0:T(8,128)(2,1)} async-done(((bf16[768,48]{1,0:T(8,128)(2,1)}), bf16[96,48]{1,0:T(8,128)(2,1)}) %reduce-scatter.10.cloned.1.call-update) | async-done | bytes 9232
  568.6 74.7 %all-reduce.23 = (bf16[768]{0:T(1024)(128)(2,1)S(1)}, bf16[96,48]{0,1:T(8,128)(2,1)S(1)}, bf16[4,1792]{1,0:T(4,128)(2,1)S(1)}, bf16[1792]{0:T(1024)(128)(2,1)S(1...) all-reduce(bf16[768]{0:T(1024)(128)(2,1)S(1)} %get-tuple-element.45, ...), channel_id=1, replica_groups=mesh['dp'=8,'seq'=16] {'seq'}, use_global_device_ids=true, to_apply=%region_47.48 | all-reduce | flops 15968 | bytes 63872 | tf_op jit(solution)/shard_map/psum | solution.py:284
  643.3 24.2 %all-reduce.25 = (bf16[768]{0:T(1024)(128)(2,1)S(1)}, bf16[4,1792]{1,0:T(4,128)(2,1)S(1)}, bf16[1792]{0:T(1024)(128)(2,1)S(1)}, bf16[48]{0:T(256)(128)(2,1)S(1)}...) all-reduce(bf16[768]{0:T(1024)(128)(2,1)S(1)} %get-tuple-element.50, ...), channel_id=1, replica_groups=mesh['dp'=8,'seq'=16] {'dp'}, use_global_device_ids=true, to_apply=%region_48.49 | all-reduce | flops 11360 | bytes 45440 | tf_op jit(solution)/shard_map/psum | solution.py:305
  (639 shorter events, 329.3 us)
Async XLA Ops:
  7.2 41.0 %all-gather.12.cloned.1.call-start = ((), (), s32[]{:S(2)}) async-start(), calls=%async_computation.3 | async-start | bytes 5750784 | tf_op jit(solution)/shard_map/all_gather | solution.py:211
  7.9 143.8 %all-gather.22.cloned.1.call-start = ((), (), s32[]{:S(2)}) async-start(), calls=%async_computation.8 | async-start | bytes 6684672 | tf_op jit(solution)/shard_map/all_gather | solution.py:22
  24.2 24.0 %copy-start.127 = (f32[256]{0:T(256)}, f32[256]{0:T(256)S(1)}, u32[]{:S(2)}) copy-start(f32[256]{0:T(256)S(1)} %fusion.216) | copy-start | bytes 3076
  26.2 21.9 %copy-start.23 = (bf16[1,256,768]{2,1,0:T(8,128)(2,1)S(1)}, bf16[1,256,768]{2,1,0:T(8,128)(2,1)}, u32[]{:S(2)}) copy-start(bf16[1,256,768]{2,1,0:T(8,128)(2,1)} %param.21) | copy-start | bytes 1179652
  26.2 21.9 %copy-start.94 = (f32[768]{0:T(1024)S(1)}, f32[768]{0:T(1024)}, u32[]{:S(2)}) copy-start(f32[768]{0:T(1024)} %param.23) | copy-start | bytes 9220
  26.4 27.5 %copy-start.54 = (f32[256,24]{1,0:T(8,128)}, f32[256,24]{1,0:T(8,128)S(1)}, u32[]{:S(2)}) copy-start(f32[256,24]{1,0:T(8,128)S(1)} %get-tuple-element.557) | copy-start | bytes 73732
  28.4 25.5 %copy-start.46 = (f32[24,2,128]{0,2,1:T(8,128)}, f32[24,2,128]{0,2,1:T(8,128)S(1)}, u32[]{:S(2)}) copy-start(f32[24,2,128]{0,2,1:T(8,128)S(1)} %copy.559) | copy-start | bytes 73732
  28.5 25.4 %copy-start.60 = (f32[24,2,128]{0,2,1:T(8,128)}, f32[24,2,128]{0,2,1:T(8,128)S(1)}, u32[]{:S(2)}) copy-start(f32[24,2,128]{0,2,1:T(8,128)S(1)} %copy.579) | copy-start | bytes 73732
  28.6 25.3 %copy-start.48 = (f32[256,24]{1,0:T(8,128)}, f32[256,24]{1,0:T(8,128)S(1)}, u32[]{:S(2)}) copy-start(f32[256,24]{1,0:T(8,128)S(1)} %rev.57) | copy-start | bytes 73732
  31.3 27.6 %copy-start.99 = (f32[1792]{0:T(1024)}, f32[1792]{0:T(1024)S(1)}, u32[]{:S(2)}) copy-start(f32[1792]{0:T(1024)S(1)} %get-tuple-element.457) | copy-start | bytes 21508
  31.3 27.6 %copy-start.101 = (f32[1792]{0:T(1024)}, f32[1792]{0:T(1024)S(1)}, u32[]{:S(2)}) copy-start(f32[1792]{0:T(1024)S(1)} %get-tuple-element.458) | copy-start | bytes 21508
  31.3 27.6 %copy-start.103 = (f32[1792]{0:T(1024)}, f32[1792]{0:T(1024)S(1)}, u32[]{:S(2)}) copy-start(f32[1792]{0:T(1024)S(1)} %get-tuple-element.459) | copy-start | bytes 21508
  31.3 27.6 %copy-start.105 = (f32[1792]{0:T(1024)}, f32[1792]{0:T(1024)S(1)}, u32[]{:S(2)}) copy-start(f32[1792]{0:T(1024)S(1)} %get-tuple-element.460) | copy-start | bytes 21508
  54.0 4.9 collective-permute-start
  61.4 76.0 %copy-start.15 = (f32[256,1792]{1,0:T(8,128)}, f32[256,1792]{1,0:T(8,128)S(1)}, u32[]{:S(2)}) copy-start(f32[256,1792]{1,0:T(8,128)S(1)} %get-tuple-element.537) | copy-start | bytes 5505028
  68.8 130.4 %all-gather.20.cloned.1.call-start = ((), (), s32[]{:S(2)}) async-start(), calls=%async_computation.7 | async-start | bytes 6684672 | tf_op jit(solution)/shard_map/all_gather | solution.py:22
  74.4 209.9 %all-gather.14.cloned.1.call-start = ((), (), s32[]{:S(2)}) async-start(), calls=%async_computation.4 | async-start | bytes 2654208 | tf_op jit(solution)/shard_map/all_gather | solution.py:213
  74.9 311.7 %all-gather.18.cloned.1.call-start = ((), (), s32[]{:S(2)}) async-start(), calls=%async_computation.6 | async-start | bytes 6684672 | tf_op jit(solution)/shard_map/all_gather | solution.py:44
  77.4 63.2 %copy-start.137 = (f32[2,1,24]{2,1,0:T(1,128)}, f32[2,1,24]{2,1,0:T(1,128)S(1)}, u32[]{:S(2)}) copy-start(f32[2,1,24]{2,1,0:T(1,128)S(1)} %slice.163) | copy-start | bytes 580
  79.1 56.8 %copy-start.52 = (f32[2,128,24]{2,1,0:T(8,128)}, f32[2,128,24]{2,1,0:T(8,128)S(1)}, u32[]{:S(2)}) copy-start(f32[2,128,24]{2,1,0:T(8,128)S(1)} %reduce_window_sum.87) | copy-start | bytes 73732
  141.3 130.2 %copy-start.5 = (f32[2,128,24,64]{1,0,3,2:T(2,128)}, f32[2,128,24,64]{1,0,3,2:T(2,128)S(1)}, u32[]{:S(2)}) copy-start(f32[2,128,24,64]{1,0,3,2:T(2,128)S(1)} %reshape.448) | copy-start | bytes 4718596
  142.5 111.2 %copy-start.39 = (f32[256,64]{1,0:T(8,128)}, f32[256,64]{1,0:T(8,128)S(1)}, u32[]{:S(2)}) copy-start(f32[256,64]{1,0:T(8,128)S(1)} %rev.54) | copy-start | bytes 196612
  303.8 122.0 %all-gather.16.cloned.1.call-start = ((), (), s32[]{:S(2)}) async-start(), calls=%async_computation.5 | async-start | bytes 6684672 | tf_op jit(solution)/shard_map/all_gather | solution.py:44
  306.7 21.9 %copy-start = (f32[256,24,64]{0,2,1:T(8,128)}, f32[256,24,64]{0,2,1:T(8,128)S(1)}, u32[]{:S(2)}) copy-start(f32[256,24,64]{0,2,1:T(8,128)S(1)} %rev.59) | copy-start | bytes 4718596
  313.6 198.5 %reduce-scatter.8.cloned.1.call-start = ((), (), s32[]{:S(2)}) async-start(), calls=%async_computation.10 | async-start | bytes 2654208 | tf_op jit(solution)/shard_map/reduce_scatter | solution.py:299
  386.5 142.8 %reduce-scatter.6.cloned.1.call-start = ((), (), s32[]{:S(2)}) async-start(), calls=%async_computation.9 | async-start | bytes 5750784 | tf_op jit(solution)/shard_map/reduce_scatter | solution.py:293
  453.5 6.8 collective-permute-start.1
  464.3 103.4 %reduce-scatter.10.cloned.1.call-start = ((), (), s32[]{:S(2)}) async-start(), calls=%async_computation.11 | async-start | bytes 221184
  511.9 160.1 %all-reduce.28.cloned.1.call-start = ((), (), s32[]{:S(2)}) async-start(), calls=%async_computation.12 | async-start | bytes 1867776 | tf_op jit(solution)/shard_map/psum | solution.py:281
  533.6 35.0 %copy-start.130 = (bf16[1536]{0:T(1024)(128)(2,1)S(1)}, bf16[1536]{0:T(1024)(128)(2,1)}, u32[]{:S(2)}) copy-start(bf16[1536]{0:T(1024)(128)(2,1)} %get-tuple-element.447) | copy-start | bytes 9220
  533.6 35.0 %copy-start.131 = (bf16[1792]{0:T(1024)(128)(2,1)S(1)}, bf16[1792]{0:T(1024)(128)(2,1)}, u32[]{:S(2)}) copy-start(bf16[1792]{0:T(1024)(128)(2,1)} %get-tuple-element.449) | copy-start | bytes 10756
  533.6 35.0 %copy-start.160 = (bf16[24]{0:T(256)(128)(2,1)S(1)}, bf16[24]{0:T(256)(128)(2,1)}, u32[]{:S(2)}) copy-start(bf16[24]{0:T(256)(128)(2,1)} %reduce_sum.412) | copy-start | bytes 148
  (142 other events, 615.8 us)
Sparse Core Ops, SparseCore 0:
  9.7 38.4 all-gather.11
  68.9 62.2 all-gather.21
  134.0 60.8 all-gather.19
  196.4 25.1 all-gather.13
  304.0 58.7 all-gather.17
  364.8 60.9 all-gather.15
  428.3 33.7 reduce-scatter.7
  464.5 64.7 reduce-scatter.5
  532.3 35.3 reduce-scatter.9
  571.1 85.2 all-reduce.27
where the time goes:
time: 696 us; the launch traced here: 683 us
  other arithmetic  193 us (28%)
  blocking collectives  155 us (22%)
  matrix products  135 us (19%)
  local copies, waits for them, and re-layouts  92.4 us (13%)
  waiting for transfers between devices  84.6 us (12%)
  between operations  17.4 us (2%)
    psum x1, blocking collectives, local(): lax.psum(d_gin.astype(jnp.bfloat16), 'seq').astype(jnp.float32)  74.7 us
    select_n x32, other arithmetic, lap(): return jax.tree.map(lambda a, b: jnp.where(reached, a, b), new, before)  72.9 us
    all_gather x2, blocking collectives, carried_in(): lax.all_gather(part.astype(kind), axis)  42.3 us
    dot_general x6, matrix products, local_mix(): return jnp.einsum('hts,shp->thp', weights, x_heads, precision=EXACT)  39 us
    unnamed x11, waiting for transfers between devices  34.3 us
    psum x1, blocking collectives, local(): lax.psum(small_grads[0].astype(jnp.bfloat16), 'dp').astype(jnp.float32)  24.2 us
    convert_element_type x32, other arithmetic, lap(): part[at].astype(own.dtype)  22 us
    dot_general x6, matrix products, forward_spans(): jnp.einsum('csn,cshp->chnp', b_parts, scaled_parts, precision=EXACT)  21.8 us
  transfers between devices with their start and end apart: 12, of which 6 were waited for; matrix products, arithmetic and copies ran while one was open for 55% of the time, Pallas kernels for 0%

commit v1 on v0

v1 whole, which is shorter than its diff:
```python
import jax
import jax.numpy as jnp
from jax import lax
from jax.experimental import pallas as pl
from jax.experimental.pallas import tpu as pltpu
from jax.sharding import PartitionSpec as P

F32, BF = jnp.float32, jnp.bfloat16
EPS = 1e-05
LOG2E = 1.4426950408889634
D, H, E, N, T = 768, 24, 1536, 64, 256
C = E + 4 * N
CD = C + 128
HALO = 16
TILES = E // 128
DP, SEQ = 8, 16
VMEM = 56 * 1024 * 1024


def iota(shape, dim):
    return lax.broadcasted_iota(jnp.int32, shape, dim)


def mm(a, b):
    return jnp.dot(a, b, preferred_element_type=F32)


def mm_nt(a, b):
    return lax.dot_general(a, b, (((1,), (1,)), ((), ())), preferred_element_type=F32)


def flip(v):
    return v.astype(F32).T.astype(v.dtype)


def sigmoid(v):
    return 1.0 / (1.0 + jnp.exp(-v))


def silu(v):
    return v * sigmoid(v)


def split2(v):
    hi = v.astype(BF)
    return hi, (v - hi.astype(F32)).astype(BF)


def pair(v):
    return jnp.concatenate(split2(v), axis=1)


def onehot(cond):
    return jnp.where(cond, 1.0, 0.0).astype(BF)


def spread(v, tile, base):
    head = iota((256, 128), 0) & 127
    column = (iota((256, 128), 1) >> 6) + (2 * tile + base)
    return mm(v, onehot(head == column))


def head_sum(v, tile, base):
    head = (iota((128, 128), 0) >> 6) + (2 * tile + base)
    mark = onehot(head == iota((128, 128), 1))
    hi, lo = split2(v)
    return mm(hi, mark) + mm(lo, mark)


def head_sum1(v, tile, base):
    head = (iota((128, 128), 0) >> 6) + (2 * tile + base)
    return mm(v.astype(BF), onehot(head == iota((128, 128), 1)))


def tri_sum(mask, v):
    hi = v.astype(BF)
    rest = v - hi.astype(F32)
    mid = rest.astype(BF)
    low = (rest - mid.astype(F32)).astype(BF)
    return mm(mask, hi) + mm(mask, mid) + mm(mask, low)


def tri(cond):
    return onehot(cond(iota((T, T), 0), iota((T, T), 1)))


def lanes(rows=T):
    return iota((rows, 128), 1)


def tile_at(i):
    return pl.ds(pl.multiple_of(i * 128, 128), 128)


def bc_parts(cs, at):
    both = silu(cs[:, at : at + 128])
    return both[:, :N].astype(BF), both[:, N:].astype(BF)


def ends(cum):
    return jnp.where(lanes(1) < H, cum[T - 1 : T], cum[0:1])


def decay_rows(dec, i, first, second):
    a, b = spread(dec, i, first), spread(dec, i, second)
    ah, bh = a.astype(BF).astype(F32), b.astype(BF).astype(F32)
    row = iota((16, 128), 0)
    out = jnp.where(row == 0, ah, jnp.where(row == 1, a - ah, jnp.where(row == 2, bh, b - bh)))
    return jnp.where(row < 4, out, 0.0).astype(BF)


def put_slices(pay, i, first, second, dec):
    group, at = i // 3, tile_at(lax.rem(i, 3))
    for q in range(4):
        j = 4 * group + q
        pay[j, 0:16, at] = first[16 * q : 16 * q + 16].astype(BF)
        pay[j, 16:32, at] = second[16 * q : 16 * q + 16].astype(BF)
        pay[j, 32:48, at] = dec


def take_slices(recv, first, second, first_scale):
    for j in range(SEQ):
        rows, at = pl.ds(16 * (j % 4), 16), pl.ds(384 * (j // 4), 384)
        first[rows, at] = (recv[j, 0:16].astype(F32) * first_scale).astype(BF)
        second[rows, at] = recv[j, 16:32]


def front(ids, cont, tok, halo, gin, cw, cb, dtb, alog, *refs):
    parts, (u_out, ci_out, cs, sraw_out, dt_out, cum_out, pay), (w, cif, sem) = (
        refs[:8],
        refs[8:15],
        refs[15:],
    )
    copies = [
        pltpu.make_async_copy(
            parts[k], w.at[pl.ds(pl.multiple_of(ids[k] * 96, 16), 96)], sem.at[k]
        )
        for k in range(8)
    ]
    for copy in copies:
        copy.start()
    x = jnp.concatenate([halo[...], tok[...]], axis=0).astype(F32)
    u = x * lax.rsqrt(jnp.mean(x * x, axis=1, keepdims=True) + EPS) * gin[...]
    u_out[...] = u.astype(BF)
    for copy in copies:
        copy.wait()
    keep = cont[0]
    mask = jnp.where(iota((HALO + T, 1), 0) < HALO, keep, 1.0)
    for j in range(7):
        at = slice(256 * j, 256 * j + 256)
        ci = (mm(u_out[...], w[:, at]) * mask).astype(BF)
        ci_out[:, at] = ci
        cif[...] = ci.astype(F32)
        total = cb[:, at]
        for k in range(4):
            total = total + cw[k : k + 1, at] * cif[HALO - 3 + k : HALO - 3 + k + T, :]
        cs[:, at] = total
    sraw = mm(u_out[HALO:, :], w[:, C:]) + dtb[...]
    sraw_out[...] = sraw
    e = jnp.exp(-jnp.abs(sraw))
    dt = jnp.maximum(sraw, 0.0) + jnp.log1p(e)
    dt = jnp.where(lanes() < 2 * H, dt, 0.0)
    dt_out[...] = dt
    rate = jnp.where(lanes(1) < 2 * H, jnp.exp(alog[...]), 0.0)
    la = -dt * rate
    cum = jnp.where(
        lanes() < H,
        tri_sum(tri(lambda r, c: r >= c), la),
        tri_sum(tri(lambda r, c: r <= c), la),
    )
    cum_out[...] = cum
    last = ends(cum)
    tail = pair(jnp.exp(last - cum) * dt)
    dec = pair(jnp.broadcast_to(jnp.exp(last) * keep, (16, 128)))
    bf_t = flip(bc_parts(cs, E)[0])
    br_t = flip(bc_parts(cs, E + 128)[0])

    def tile(i, _):
        x_act = silu(cs[:, tile_at(i)])
        sf = mm(bf_t, (spread(tail, i, 0) * x_act).astype(BF))
        sr = mm(br_t, (spread(tail, i, H) * x_act).astype(BF)) * keep
        put_slices(pay, i, sf, sr, decay_rows(dec, i, 0, H))
        return 0

    lax.fori_loop(0, TILES, tile, 0)


def scan_blocks(recv, out):
    carry = jnp.zeros((16, 384), F32)
    back = jnp.zeros((16, 384), F32)
    for i in range(SEQ):
        k = SEQ - 1 - i
        out[i, 0:16] = carry.astype(BF)
        out[k, 16:32] = back.astype(BF)
        dec = recv[i, 32:48].astype(F32)
        carry = (dec[0:1] + dec[1:2]) * carry + recv[i, 0:16].astype(F32)
        dec = recv[k, 32:48].astype(F32)
        back = (dec[2:3] + dec[3:4]) * back + recv[k, 16:32].astype(F32)


def lower_blocks(e_left, e_right, g):
    left = e_left * g[:, :128]
    right = e_right * g[128:, 128:]
    return left, right


def columns_of(cum2, col):
    for h in range(2 * H):
        col[h] = jnp.broadcast_to(cum2[:, h : h + 1], (T, 128))


def halves(v):
    first = lanes() < 64
    return jnp.where(first, v, 0.0).astype(BF), jnp.where(first, 0.0, v).astype(BF)


def low_full(left, right):
    right = jnp.concatenate([jnp.zeros((128, 128), right.dtype), right], axis=0)
    return jnp.concatenate([left, right], axis=1)


def up_full(left, right):
    left = jnp.concatenate([left, jnp.zeros((128, 128), left.dtype)], axis=0)
    return jnp.concatenate([left, right], axis=1)


def local_mix(cs, dt, cum, yf, yr, col, row, gf, gr):
    cum2 = cum[...] * LOG2E
    row[...] = cum2.T
    columns_of(cum2, col)
    r, c = iota((T, T), 0), iota((T, T), 1)
    b, cc = bc_parts(cs, E)
    gf[...] = jnp.where(r > c, mm_nt(cc, b), 0.0)
    b, cc = bc_parts(cs, E + 128)
    gr[...] = jnp.where(r < c, mm_nt(cc, b), 0.0)
    dt2 = pair(dt[...])

    def weights(h, forward):
        at, along = col[h], row[pl.ds(h, 1), :]
        if forward:
            left = jnp.exp2(jnp.minimum(at - along[:, :128], 0.0)) * gf[:, :128]
            right = jnp.exp2(jnp.minimum(at[128:] - along[:, 128:], 0.0)) * gf[128:, 128:]
            return low_full(left.astype(BF), right.astype(BF))
        left = jnp.exp2(jnp.minimum(at[:128] - along[:, :128], 0.0)) * gr[:128, :128]
        right = jnp.exp2(jnp.minimum(at - along[:, 128:], 0.0)) * gr[:, 128:]
        return up_full(left.astype(BF), right.astype(BF))

    def tile(i, _):
        at = tile_at(i)
        x = silu(cs[:, at])
        x0, x1 = halves(x * spread(dt2, i, 0))
        yf[:, at] = mm(weights(2 * i, True), x0) + mm(weights(2 * i + 1, True), x1)
        x0, x1 = halves(x * spread(dt2, i, H))
        yr[:, at] = mm(weights(H + 2 * i, False), x0) + mm(weights(H + 2 * i + 1, False), x1)
        return 0

    lax.fori_loop(0, TILES, tile, 0)


def load_rest(rest, wg, wo, sem):
    copies = []
    for p in range(DP):
        at = 384 * p
        if wg is not None:
            copies.append((rest.at[pl.ds(at, 96)], wg.at[0, pl.ds(96 * p, 96)]))
            copies.append((rest.at[pl.ds(at + 96, 96)], wg.at[1, pl.ds(96 * p, 96)]))
        if wo is not None:
            copies.append((rest.at[pl.ds(at + 192, 192)], wo.at[pl.ds(192 * p, 192)]))
    copies = [pltpu.make_async_copy(a, b, sem.at[k]) for k, (a, b) in enumerate(copies)]
    for copy in copies:
        copy.start()
    return copies


def gate_products(u, dout, rest, gate, dn, wg, wo, sem):
    copies = load_rest(rest, wg, wo, sem)
    for copy in copies:
        copy.wait()
    gate[:, :D] = mm(u[HALO:, :], wg[0])
    gate[:, D:] = mm(u[HALO:, :], wg[1])
    dn[...] = mm_nt(dout[...], wo[...])


def gated_norm(cont, cs, cum, ylf, ylr, recv, gate, dn, gout, dsk, *refs):
    (n16, dg16, dm16, row, dgout, ddsk, pay), (sf, sr, yfs, yrs, mix, xdm) = refs[:7], refs[7:]
    keep = cont[0]
    take_slices(recv, sf, sr, keep)
    cumv = cum[...]
    ef2 = pair(jnp.exp(cumv))
    dec = pair(jnp.broadcast_to(jnp.exp(ends(cumv)) * keep, (16, 128)))
    _, cf = bc_parts(cs, E)
    _, cr = bc_parts(cs, E + 128)
    zero = jnp.zeros((T, 128), F32)

    def first(i, sums):
        at = tile_at(i)
        yf = ylf[:, at] + spread(ef2, i, 0) * mm(cf, sf[:, at])
        yr = ylr[:, at] + spread(ef2, i, H) * mm(cr, sr[:, at])
        yfs[:, at] = yf
        yrs[:, at] = yr
        m = yf + yr + dsk[:, at] * silu(cs[:, at])
        mix[:, at] = m
        gd = m * silu(gate[:, at])
        return sums[0] + gd * gd, sums[1] + dn[:, at] * gout[:, at] * gd

    squares, crossed = lax.fori_loop(0, TILES, first, (zero, zero))
    rs = lax.rsqrt(jnp.sum(squares, axis=1, keepdims=True) / E + EPS)
    pull = jnp.sum(crossed, axis=1, keepdims=True) / E * (rs * rs * rs)
    cf_t, cr_t = flip(cf), flip(cr)

    def second(i, rows):
        at = tile_at(i)
        g, m = gate[:, at], mix[:, at]
        sg = sigmoid(g)
        sl = g * sg
        gd = m * sl
        gdr = gd * rs
        n16[:, at] = (gdr * gout[:, at]).astype(BF)
        dgout[:, at] = jnp.sum(dn[:, at] * gdr, axis=0, keepdims=True)
        dgd = rs * (dn[:, at] * gout[:, at]) - gd * pull
        dg16[:, at] = (dgd * m * sg * (1.0 + g * (1.0 - sg))).astype(BF)
        dm = dgd * sl
        low = dm.astype(BF)
        dm16[:, at] = low
        dmr = low.astype(F32)
        xdm[:, at] = jnp.sum(dm * silu(cs[:, at]), axis=0, keepdims=True)
        lf = mm(cf_t, (spread(ef2, i, 0) * dm).astype(BF)) * keep
        lr = mm(cr_t, (spread(ef2, i, H) * dm).astype(BF))
        put_slices(pay, i, lr, lf, decay_rows(dec, i, H, 0))
        return (
            rows + head_sum(dmr * yfs[:, at], i, 0) + head_sum(dmr * yrs[:, at], i, H)
        )

    row[...] = lax.fori_loop(0, TILES, second, zero)
    total = jnp.zeros((8, 128), F32)
    for i in range(TILES):
        total = total + head_sum(
            jnp.broadcast_to(xdm[:, 128 * i : 128 * i + 128], (8, 128)), i, 0
        )
    ddsk[...] = total[0:1]


def out_and_grads(ids, tok, u, n16, dg16, dout, rest, out, keep, send, wo, n_t, u_t, sem):
    copies = load_rest(rest, None, wo, sem)
    n_t[...] = flip(n16[...])
    u_t[...] = flip(u[HALO:, :])
    for ref, base in ((send, 4), (keep, 0)):
        for k in range(4):
            d = ids[base + k]
            ref[k, 192:384] = mm(
                n_t[pl.ds(pl.multiple_of(d * 192, 64), 192), :], dout[...]
            ).astype(BF)
            rows = u_t[pl.ds(pl.multiple_of(d * 96, 32), 96), :]
            ref[k, 0:96] = mm(rows, dg16[:, :D]).astype(BF)
            ref[k, 96:192] = mm(rows, dg16[:, D:]).astype(BF)
    for copy in copies:
        copy.wait()
    out[...] = (tok[...].astype(F32) + mm(n16[...], wo[...])).astype(BF)


def local_back(cs, dt, cum, dm16, zf, zr, dgf, dgr, col, row, gf, gr, dm_t):
    cum2 = cum[...] * LOG2E
    row[...] = cum2.T
    columns_of(cum2, col)
    dm_t[...] = flip(dm16[...])
    s, t = iota((T, T), 0), iota((T, T), 1)
    b, cc = bc_parts(cs, E)
    gf[...] = jnp.where(t > s, mm_nt(b, cc), 0.0)
    b, cc = bc_parts(cs, E + 128)
    gr[...] = jnp.where(t < s, mm_nt(b, cc), 0.0)
    dgf[...] = jnp.zeros((T, T), F32)
    dgr[...] = jnp.zeros((T, T), F32)
    dt2 = pair(dt[...])

    def tile(i, _):
        at = tile_at(i)
        x = silu(cs[:, at])
        d0, d1 = halves(dm16[:, at].astype(F32))
        dms = dm_t[at, :]
        for forward in (True, False):
            base = 0 if forward else H
            xs = halves(x * spread(dt2, i, base))
            total = jnp.zeros((T, 128), F32)
            small = jnp.zeros((128, 128), F32)
            large = jnp.zeros((T, 128), F32)
            for e in range(2):
                h = base + 2 * i + e
                at_s, along = col[h], row[pl.ds(h, 1), :]
                if forward:
                    ea = jnp.exp2(jnp.minimum(along[:, :128] - at_s[:128], 0.0))
                    eb = jnp.exp2(jnp.minimum(along[:, 128:] - at_s, 0.0))
                    w = up_full((ea * gf[:128, :128]).astype(BF), (eb * gf[:, 128:]).astype(BF))
                    small = small + ea * mm(xs[e][:128], dms[:, :128])
                    large = large + eb * mm(xs[e], dms[:, 128:])
                else:
                    ea = jnp.exp2(jnp.minimum(along[:, :128] - at_s, 0.0))
                    eb = jnp.exp2(jnp.minimum(along[:, 128:] - at_s[128:], 0.0))
                    w = low_full((ea * gr[:, :128]).astype(BF), (eb * gr[128:, 128:]).astype(BF))
                    large = large + ea * mm(xs[e], dms[:, :128])
                    small = small + eb * mm(xs[e][128:], dms[:, 128:])
                total = total + mm(w, (d0, d1)[e])
            if forward:
                zf[:, at] = total
                dgf[:128, :128] += small
                dgf[:, 128:] += large
            else:
                zr[:, at] = total
                dgr[:, :128] += large
                dgr[128:, 128:] += small
        return 0

    lax.fori_loop(0, TILES, tile, 0)
    dgf[...] = jnp.where(t > s, dgf[...], 0.0)
    dgr[...] = jnp.where(t < s, dgr[...], 0.0)


def last_back(
    ids, cont, tok, halo, gin, cw, alog, dsk, cs, sraw, dt, cum, ci, u, dout, dm16, dg16, zf, zr,
    dgf, dgr, back, fore, row, dgout, ddsk, rest, *refs
):
    parts, (dtok, dhalo, keep_out, send_out), scratch = refs[:8], refs[8:12], refs[12:]
    w, wg, sf, sr, kf, kr, dcs, cif, dall, u_t, small, srow, sem, sem2 = scratch
    copies = [
        pltpu.make_async_copy(
            parts[k], w.at[pl.ds(pl.multiple_of(ids[k] * 96, 16), 96)], sem2.at[k]
        )
        for k in range(8)
    ]
    for copy in copies:
        copy.start()
    copies += load_rest(rest, wg, None, sem)
    keep = cont[0]
    take_slices(back, kr, kf, keep)
    take_slices(fore, sf, sr, keep)
    u_t[...] = flip(u[...])
    cumv, dtv = cum[...], dt[...]
    last = ends(cumv)
    te2, ef2, dt2 = pair(jnp.exp(last - cumv)), pair(jnp.exp(cumv)), pair(dtv)
    bf, cf = bc_parts(cs, E)
    br, cr = bc_parts(cs, E + 128)
    dcs[0:HALO] = jnp.zeros((HALO, C), F32)
    dcs[HALO + T :] = jnp.zeros((16, C), F32)
    zero = jnp.zeros((T, 128), F32)

    def silu_slope(v):
        sg = sigmoid(v)
        return sg * (1.0 + v * (1.0 - sg))

    def tile(i, sums):
        inner, tails, direct, dbf, dcf, dbr, dcr, dots = sums
        at = tile_at(i)
        x = silu(cs[:, at])
        dm = dm16[:, at].astype(F32)
        dx = dsk[:, at] * dm
        new = []
        for base, z, k, s, b in ((0, zf, kf, sf, bf), (H, zr, kr, sr, br)):
            dts, te, ef = spread(dt2, i, base), spread(te2, i, base), spread(ef2, i, base)
            xd = (x * dts).astype(BF).astype(F32)
            zi, zt = z[:, at], te * mm(b, k[:, at])
            zs = zi + zt
            dx = dx + dts * zs
            inner = inner + head_sum(xd * zi, i, base)
            tails = tails + head_sum1(xd * zt, i, base)
            direct = direct + head_sum1(x * zs, i, base)
            new.append(mm_nt((te * xd).astype(BF), k[:, at]))
            new.append(mm_nt((ef * dm).astype(BF), s[:, at]))
            both = jnp.sum(s[:, at].astype(F32) * k[:, at].astype(F32), axis=0, keepdims=True)
            dots = dots + head_sum(jnp.broadcast_to(both, (8, 128)), i, base)
        dcs[HALO : HALO + T, at] = dx * silu_slope(cs[:, at])
        return (inner, tails, direct, dbf + new[0], dcf + new[1], dbr + new[2], dcr + new[3], dots)

    zn = jnp.zeros((T, N), F32)
    inner, tails, direct, dbf, dcf, dbr, dcr, dots = lax.fori_loop(
        0, TILES, tile, (zero, zero, zero, zn, zn, zn, zn, jnp.zeros((8, 128), F32))
    )
    gf16, gr16 = dgf[...].astype(BF), dgr[...].astype(BF)
    dbf = dbf + mm(gf16, cf)
    dcf = dcf + mm(flip(gf16), bf)
    dbr = dbr + mm(gr16, cr)
    dcr = dcr + mm(flip(gr16), br)
    for at, b, c in ((E, dbf, dcf), (E + 128, dbr, dcr)):
        dcs[HALO : HALO + T, at : at + 128] = jnp.concatenate([b, c], axis=1) * silu_slope(
            cs[:, at : at + 128]
        )
    rate = jnp.where(lanes(1) < 2 * H, jnp.exp(alog[...]), 0.0)
    v = row[...] - inner
    forward = lanes() < H
    dla = jnp.where(
        forward,
        tri_sum(tri(lambda r, c: r <= c), v) + tri_sum(tri(lambda r, c: r > c), tails),
        tri_sum(tri(lambda r, c: r >= c), v) + tri_sum(tri(lambda r, c: r < c), tails),
    ) + jnp.exp(last) * dots[0:1]
    dstep = (direct - dla * rate) * sigmoid(sraw[...])
    dstep = jnp.where(lanes() < 2 * H, dstep, 0.0)
    dall[0:HALO, C:] = jnp.zeros((HALO, 128), BF)
    dall[HALO:, C:] = dstep.astype(BF)
    dal = jnp.sum(dla * (-dtv * rate), axis=0, keepdims=True)
    small[...] = jnp.zeros((96, 128), F32)
    small[88:89] = jnp.sum(dstep, axis=0, keepdims=True)
    srow[...] = jnp.broadcast_to(dal, (8, 128))
    small[89:90, 0:H] = srow[0:1, 0:H] + srow[0:1, H : 2 * H]
    small[90:91] = ddsk[...]
    mask = jnp.where(iota((HALO + T, 1), 0) < HALO, keep, 1.0)
    for j in range(7):
        at = slice(256 * j, 256 * j + 256)
        g = dcs[HALO : HALO + T, at]
        cif[...] = ci[:, at].astype(F32)
        grads = [jnp.sum(g, axis=0, keepdims=True)]
        total = jnp.zeros((HALO + T, 256), F32)
        for k in range(4):
            grads.append(
                jnp.sum(g * cif[HALO - 3 + k : HALO - 3 + k + T, :], axis=0, keepdims=True)
            )
            total = total + cw[k : k + 1, at] * dcs[3 - k : 3 - k + HALO + T, at]
        dall[:, at] = (total * mask).astype(BF)
        for half in range(2):
            tile_no, cut = 2 * j + half, slice(128 * half, 128 * half + 128)
            small[56 + tile_no : 57 + tile_no] = grads[0][:, cut]
            for k in range(4):
                at_row = 14 * k + tile_no
                small[at_row : at_row + 1] = grads[k + 1][:, cut]
    for j in range(TILES):
        small[70 + j : 71 + j] = dgout[:, 128 * j : 128 * j + 128]
    for copy in copies:
        copy.wait()
    du = mm_nt(dall[...], w[...])
    dg = mm_nt(dg16[:, :D], wg[0]) + mm_nt(dg16[:, D:], wg[1])
    du = du + jnp.concatenate([jnp.zeros((HALO, D), F32), dg], axis=0)
    x = jnp.concatenate([halo[...], tok[...]], axis=0).astype(F32)
    r = lax.rsqrt(jnp.mean(x * x, axis=1, keepdims=True) + EPS)
    duxr = du * x * r
    for j in range(6):
        small[82 + j : 83 + j] = jnp.sum(duxr[:, 128 * j : 128 * j + 128], axis=0, keepdims=True)
    dxh = du * gin[...]
    dx = r * dxh - x * (r * r * r * jnp.mean(dxh * x, axis=1, keepdims=True))
    dhalo[...] = dx[:HALO]
    dtok[...] = dout[...].astype(F32) + dx[HALO:]
    low = small[...].astype(BF)
    for ref, base in ((send_out, 12), (keep_out, 8)):
        for k in range(4):
            rows = u_t[pl.ds(pl.multiple_of(ids[base + k] * 96, 32), 96), :]
            ref[k, :, :CD] = mm(rows, dall[...]).astype(BF)
            ref[k, :, CD:] = low


def add_pairs(a, b, *outs):
    for k in range(4):
        outs[k][...] = (a[k].astype(F32) + b[k].astype(F32)).astype(BF)


def add_four(a, b, c, d, out):
    total = a[...].astype(F32) + b[...].astype(F32) + c[...].astype(F32) + d[...].astype(F32)
    for j in range(total.shape[1] // 128):
        out[j] = total[:, 128 * j : 128 * j + 128].astype(BF)


def add_blocks(recv, out):
    total = recv[0].astype(F32)
    for i in range(1, SEQ):
        total = total + recv[i].astype(F32)
    low = total.astype(BF)
    for i in range(SEQ):
        out[i] = low


def finish(rest, tail, dwin, dwdt, dwout, dcw, dcb, dgout, dgin, ddtb, dal, ddsk):
    for j in range(6):
        at = slice(128 * j, 128 * j + 128)
        dwin[:, at] = rest[j, 0:96].astype(F32)
        dwin[:, D + 128 * j : D + 128 * j + 128] = rest[j, 96:192].astype(F32)
        dwout[:, at] = rest[j, 192:384].astype(F32)
    for j in range(14):
        dwin[:, E + 128 * j : E + 128 * j + 128] = tail[j].astype(F32)
    dwdt[...] = tail[14, :, 0 : 2 * H].astype(F32)
    small = tail[15].astype(F32)
    for j in range(14):
        at = slice(128 * j, 128 * j + 128)
        for k in range(4):
            dcw[k : k + 1, at] = small[14 * k + j : 14 * k + j + 1]
        dcb[:, at] = small[56 + j : 57 + j]
    for j in range(TILES):
        dgout[:, 128 * j : 128 * j + 128] = small[70 + j : 71 + j]
    for j in range(6):
        dgin[:, 128 * j : 128 * j + 128] = small[82 + j : 83 + j]
    ddtb[...] = small[88:89, 0 : 2 * H]
    dal[...] = small[89:90, 0:H]
    ddsk[...] = small[90:91, 0:H]


V = pl.BlockSpec(memory_space=pltpu.VMEM)
S = pl.BlockSpec(memory_space=pltpu.SMEM)
ANY = pl.BlockSpec(memory_space=pl.ANY)


def shape(*dims, dtype=F32):
    return jax.ShapeDtypeStruct(dims, dtype)


def call(kernel, name, ins, outs, scratch=(), flops=0, **more):
    specs, args = zip(*ins)
    moved = sum(a.size * a.dtype.itemsize for a in args)
    moved += sum(o.size * o.dtype.itemsize for o in outs)
    return pl.pallas_call(
        kernel,
        name=name,
        out_shape=tuple(outs),
        in_specs=list(specs),
        out_specs=tuple(V for _ in outs),
        scratch_shapes=list(scratch),
        cost_estimate=pl.CostEstimate(flops=flops, bytes_accessed=moved, transcendentals=0),
        compiler_params=pltpu.CompilerParams(vmem_limit_bytes=VMEM),
        **more,
    )(*args)


def vm(*dims, dtype=F32):
    return pltpu.VMEM(dims, dtype)


def shift_y(k):
    return [(2 * y + c, 2 * ((y + k) % 4) + c) for y in range(4) for c in range(2)]


SWAP = [(i, i ^ 1) for i in range(DP)]


def exchange(value):
    return lax.all_to_all(value, "seq", 0, 0, tiled=True)


def add_swapped(keep, send, name):
    recv = lax.ppermute(send, "dp", SWAP)
    rows, cols = keep.shape[1:]
    step = rows // 3
    return pl.pallas_call(
        add_pairs,
        name=name,
        grid=(3,),
        out_shape=tuple(shape(rows, cols, dtype=BF) for _ in range(4)),
        in_specs=[pl.BlockSpec((4, step, cols), lambda i: (0, i, 0))] * 2,
        out_specs=tuple(pl.BlockSpec((step, cols), lambda i: (i, 0)) for _ in range(4)),
        compiler_params=pltpu.CompilerParams(vmem_limit_bytes=VMEM),
    )(keep, recv)


def over_y(parts, name):
    got = [lax.ppermute(parts[k], "dp", shift_y(k)) for k in (1, 2, 3)]
    rows, cols = parts[0].shape
    return call(
        add_four,
        name,
        [(V, parts[0])] + [(V, g) for g in got],
        [shape(cols // 128, rows, 128, dtype=BF)],
    )[0]


def over_seq(tiles, rows, name):
    got = exchange(tiles.reshape(SEQ, rows, 128))
    total = call(add_blocks, name, [(V, got)], [shape(SEQ, rows, 128, dtype=BF)])[0]
    return exchange(total)


def local(
    tokens, starts, g_in, w_in, w_dt, conv_w, conv_b, dt_bias, a_log, dskip, g_out, w_out, d_out
):
    dp = lax.axis_index("dp")
    y, core = dp // 2, dp % 2
    tok, dout = tokens[0], d_out[0]
    cont = (1 - starts[0]).astype(F32)

    own = jnp.concatenate([w_in[:, E:], jnp.pad(w_dt, ((0, 0), (0, 128 - 2 * H)))], axis=1)
    halo = lax.ppermute(tok[-HALO:], "seq", [(i, i + 1) for i in range(SEQ - 1)])
    column = [own] + [lax.ppermute(own, "dp", shift_y(k)) for k in (1, 2, 3)]
    parts = column + [lax.ppermute(part, "dp", SWAP) for part in column]
    from_y = [2 * ((y - k) % 4) + core for k in range(4)]
    to_y = [(y + k) % 4 for k in range(4)]
    mine = [2 * t + core for t in to_y]
    other = [2 * t + 1 - core for t in to_y]
    ids = jnp.stack(from_y + [2 * ((y - k) % 4) + 1 - core for k in range(4)] + mine + other)
    rest_own = jnp.concatenate([w_in[:, :D], w_in[:, D:E], w_out], axis=0)
    rest_own = lax.optimization_barrier([rest_own] + column[1:])[0]
    rest = lax.all_gather(rest_own, "dp", axis=0, tiled=True)

    row = lambda v: v.reshape(1, -1)
    pad = lambda v: jnp.pad(v, (0, 128 - v.shape[0])).reshape(1, 128)
    alog = pad(jnp.concatenate([a_log, a_log]))
    dsk = row(jnp.repeat(dskip, N))
    gin, gout = row(g_in), row(g_out)
    part_ins = [(ANY, part) for part in parts]
    w_scratch = vm(D, CD, dtype=BF)
    dma = pltpu.SemaphoreType.DMA

    u, ci, cs, sraw, dt, cum, pay = call(
        front,
        "front",
        [(S, ids), (S, cont), (V, tok), (V, halo), (V, gin), (V, conv_w), (V, row(conv_b))]
        + [(V, pad(dt_bias)), (V, alog)]
        + part_ins,
        [shape(HALO + T, D, dtype=BF), shape(HALO + T, C, dtype=BF), shape(T, C)]
        + [shape(T, 128)] * 3
        + [shape(SEQ, 48, 384, dtype=BF)],
        [w_scratch, vm(HALO + T, 256), dma((8,))],
        flops=2 * T * D * CD,
    )

    def across(payload, name):
        got = exchange(payload)
        out = call(scan_blocks, name, [(V, got)], [shape(SEQ, 32, 384, dtype=BF)])[0]
        return exchange(out)

    mix_scratch = [vm(2 * H, T, 128), vm(128, T), vm(T, T), vm(T, T)]
    fore = across(pay, "scan_states")
    ylf, ylr = call(
        local_mix,
        "local_mix",
        [(V, cs), (V, dt), (V, cum)],
        [shape(T, E)] * 2,
        mix_scratch,
        flops=2 * 48 * T * T * 256,
    )
    rest_scratch = [vm(2, D, D, dtype=BF), vm(E, D, dtype=BF), dma((24,))]
    gate, dn = call(
        gate_products,
        "gate_products",
        [(V, u), (V, dout), (ANY, rest)],
        [shape(T, E)] * 2,
        rest_scratch,
        flops=4 * T * D * E,
    )
    n16, dg16, dm16, rows, dgout, ddsk, pay_back = call(
        gated_norm,
        "gated_norm",
        [(S, cont), (V, cs), (V, cum), (V, ylf), (V, ylr), (V, fore), (V, gate), (V, dn)]
        + [(V, gout), (V, dsk)],
        [shape(T, E, dtype=BF)] * 3
        + [shape(T, 128), shape(1, E), shape(1, 128), shape(SEQ, 48, 384, dtype=BF)],
        [vm(N, E, dtype=BF)] * 2 + [vm(T, E)] * 3 + [vm(1, E)],
        flops=12 * T * N * E,
    )
    back = across(pay_back, "scan_adjoints")
    out, rest_keep, rest_send = call(
        out_and_grads,
        "out_and_grads",
        [(S, ids[8:]), (V, tok), (V, u), (V, n16), (V, dg16), (V, dout), (ANY, rest)],
        [shape(T, D, dtype=BF)] + [shape(4, 384, D, dtype=BF)] * 2,
        [vm(E, D, dtype=BF), vm(E, T, dtype=BF), vm(D, T, dtype=BF), dma((8,))],
        flops=6 * T * D * E,
    )
    zf, zr, dgf, dgr = call(
        local_back,
        "local_back",
        [(V, cs), (V, dt), (V, cum), (V, dm16)],
        [shape(T, E)] * 2 + [shape(T, T)] * 2,
        mix_scratch + [vm(E, T, dtype=BF)],
        flops=4 * 48 * T * T * 256,
    )
    rest_tiles = over_y(add_swapped(rest_keep, rest_send, "add_rest_cores"), "add_rest_y")

    dtok, dhalo, keep, send = call(
        last_back,
        "last_back",
        [(S, ids), (S, cont), (V, tok), (V, halo), (V, gin), (V, conv_w), (V, alog), (V, dsk)]
        + [(V, a) for a in (cs, sraw, dt, cum, ci, u, dout, dm16, dg16, zf, zr, dgf, dgr)]
        + [(V, back), (V, fore), (V, rows), (V, dgout), (V, ddsk), (ANY, rest)]
        + part_ins,
        [shape(T, D), shape(HALO, D)] + [shape(4, 96, 2048, dtype=BF)] * 2,
        [w_scratch, vm(2, D, D, dtype=BF)]
        + [vm(N, E, dtype=BF)] * 4
        + [vm(HALO + T + 16, C), vm(HALO + T, 256), vm(HALO + T, CD, dtype=BF)]
        + [vm(D, HALO + T, dtype=BF), vm(96, 128), vm(8, 128), dma((16,)), dma((8,))],
        flops=2 * T * D * (2 * CD + E),
    )
    dback = lax.ppermute(dhalo, "seq", [(i + 1, i) for i in range(SEQ - 1)])
    dtok = dtok.at[-HALO:].add(dback)
    tail_tiles = over_y(add_swapped(keep, send, "add_tail_cores"), "add_tail_y")
    rest_sum = over_seq(rest_tiles, 144, "add_rest_seq").reshape(6, 384, 128)
    tail_sum = over_seq(tail_tiles, 96, "add_tail_seq")
    dwin, dwdt, dwout, dcw, dcb, dgo, dgi, ddtb, dal, dds = call(
        finish,
        "finish",
        [(V, rest_sum), (V, tail_sum)],
        [shape(96, E + C), shape(96, 2 * H), shape(192, D), shape(4, C), shape(1, C)]
        + [shape(1, E), shape(1, D), shape(1, 2 * H), shape(1, H), shape(1, H)],
    )
    flat = lambda v: v.reshape(-1)
    return (
        out[None], dtok[None], flat(dgi), dwin, dwdt, dcw, flat(dcb), flat(ddtb), flat(dal),
        flat(dds), flat(dgo), dwout,
    )


def solution(mesh):
    split = P("dp", "seq", None)
    rows = P("dp", None)
    return jax.shard_map(
        local,
        mesh=mesh,
        in_specs=(split, P("dp", "seq"), P(), rows, rows, P(), P(), P(), P(), P(), P(), rows, split),
        out_specs=(split, split, P(), rows, rows, P(), P(), P(), P(), P(), P(), rows),
        check_vma=False,
    )
```

time: 696 us -> 315 us (0.45); the launches traced: 683 us -> 313 us
  other arithmetic: 193 us -> 5.45 us
  blocking collectives: 155 us -> 19.7 us
  matrix products: 135 us -> 0 us
  Pallas kernels: 0 us -> 121 us
  local copies, waits for them, and re-layouts: 92.4 us -> 17.8 us
  starting transfers between devices: 5.15 us -> 53.6 us
    dot_general x37 -> x0, matrix products: 132 us -> none  [the longest x6 39 us: local_mix(): return jnp.einsum('hts,shp->thp', weights, x_heads, precision=EXACT)]
    pallas_call x0 -> x16, Pallas kernels: none -> 121 us  [the longest x14 113 us: call(): pl.pallas_call(kernel, name=name, out_shape=tuple(outs), in_specs=list(sp...]
    psum x2 -> x0, blocking collectives: 98.9 us -> none  [the longest x1 74.7 us: local(): lax.psum(d_gin.astype(jnp.bfloat16), 'seq').astype(jnp.float32)]
    select_n x32 -> x0, other arithmetic: 72.9 us -> none  [lap(): return jax.tree.map(lambda a, b: jnp.where(reached, a, b), new, before)]
    all_gather x3 -> x0, blocking collectives: 55.8 us -> none  [the longest x2 42.3 us: carried_in(): lax.all_gather(part.astype(kind), axis)]
    ppermute x2 -> x17, waiting for transfers between devices: 5.91 us -> 50.7 us  [the longest x6 24.9 us: over_y(): got = [lax.ppermute(parts[k], 'dp', shift_y(k)) for k in (1, 2, 3)]]
    convert_element_type x61 -> x0, other arithmetic: 42.3 us -> none  [the longest x32 22 us: lap(): part[at].astype(own.dtype)]
    all_to_all x0 -> x7, starting transfers between devices: none -> 35.7 us  [exchange(): return lax.all_to_all(value, 'seq', 0, 0, tiled=True)]
  transfers between devices with their start and end apart: 12 -> 25, of which waited for: 6 -> 12; matrix products, arithmetic and copies ran while one was open for 55% -> 2% of each run, Pallas kernels for 0% -> 32%
where the time goes in v1:
time: 315 us; the launch traced here: 313 us
  Pallas kernels  121 us (38%)
  waiting for transfers between devices  80 us (25%)
  starting transfers between devices  53.6 us (17%)
  blocking collectives  19.7 us (6%)
  local copies, waits for them, and re-layouts  17.8 us (6%)
  between operations  15.1 us (5%)
  other arithmetic  5.45 us (2%)
    pallas_call x14, Pallas kernels, call(): pl.pallas_call(kernel, name=name, out_shape=tuple(outs), in_specs=list(sp...  113 us
    all_to_all x7, starting transfers between devices, exchange(): return lax.all_to_all(value, 'seq', 0, 0, tiled=True)  35.7 us
    all_to_all x7, waiting for transfers between devices, exchange(): return lax.all_to_all(value, 'seq', 0, 0, tiled=True)  29.2 us
    ppermute x6, waiting for transfers between devices, over_y(): got = [lax.ppermute(parts[k], 'dp', shift_y(k)) for k in (1, 2, 3)]  24.9 us
    all_to_all x1, blocking collectives, exchange(): return lax.all_to_all(value, 'seq', 0, 0, tiled=True)  19.7 us
    ppermute x3, waiting for transfers between devices, local(): column = [own] + [lax.ppermute(own, 'dp', shift_y(k)) for k in (1, 2, 3)]  16 us
    unnamed x71, local copies, waits for them, and re-layouts  10.8 us
    pallas_call x2, Pallas kernels, add_swapped(): pl.pallas_call(add_pairs, name=name, grid=(3,), out_shape=tuple((shape(ro...  8.27 us
  transfers between devices with their start and end apart: 25, of which 12 were waited for; matrix products, arithmetic and copies ran while one was open for 2% of the time, Pallas kernels for 32%

profile of v1, /device:TPU:0, one launch (start us, length us, event | category | flops | bytes accessed | tf_op | source)
XLA Modules:
  0.0 312.7 jit_solution(10634703225255475714)
XLA Ops:
  9.2 3.2 %collective-permute-start.3 = (bf16[96,1920]{1,0:T(8,128)(2,1)S(1)}, bf16[96,1920]{1,0:T(8,128)(2,1)S(1)}, u32[]{:S(2)}, u32[]{:S(2)}) collective-permute-start(bf16[96,1920]{1,0:T(8,128)(2,1)S(1)} %fusion.1.refs_0_), channel_id=1, source_target_pairs={{0,96},{16,112},{32,0},{48,16},{64,32},{80,48},{96,64},{112,80},{1... | collective-permute-start | bytes 1105928 | tf_op jit(solution)/shard_map/ppermute | solution.py:673
  15.8 12.3 %collective-permute-done.3.refs_3_ = bf16[96,1920]{1,0:T(8,128)(2,1)S(1)} collective-permute-done((bf16[96,1920]{1,0:T(8,128)(2,1)S(1)}, bf16[96,1920]{1,0:T(8,128)(2,1)S(1)}, u32[]{:S(2)}, u32[]{:S(2)}) %collective-permute-start.3) | collective-permute-done | bytes 368672 | tf_op jit(solution)/shard_map/ppermute | solution.py:673
  28.1 3.7 %collective-permute-done.1.refs_1_ = bf16[96,1920]{1,0:T(8,128)(2,1)S(1)} collective-permute-done((bf16[96,1920]{1,0:T(8,128)(2,1)S(1)}, bf16[96,1920]{1,0:T(8,128)(2,1)S(1)}, u32[]{:S(2)}, u32[]{:S(2)}) %collective-permute-start.1) | collective-permute-done | bytes 368672 | tf_op jit(solution)/shard_map/ppermute | solution.py:673
  33.7 3.8 %collective-permute-start = (bf16[16,768]{1,0:T(8,128)(2,1)S(1)}, bf16[16,768]{1,0:T(8,128)(2,1)S(1)}, u32[]{:S(2)}, u32[]{:S(2)}) collective-permute-start(bf16[16,768]{1,0:T(8,128)(2,1)S(1)} %slice_bitcast_fusion), channel_id=1, source_target_pairs={{0,1},{1,2},{2,3},{3,4},{4,5},{5,6},{6,7},{7,8},{8,9},{9,10},{10,1... | collective-permute-start | bytes 73736 | tf_op jit(solution)/shard_map/ppermute | solution.py:672
  42.2 13.2 %front.1 = (bf16[272,768]{1,0:T(8,128)(2,1)}, bf16[272,1792]{1,0:T(8,128)(2,1)}, f32[256,1792]{1,0:T(8,128)}, f32[256,128]{1,0:T(8,128)}, f32[256,128]{1,0:T(8,1...) custom-call(s32[16]{0:T(128)} %stack.64.ids, f32[1]{0:T(128)} %bitcast.15.cont, bf16[256,768]{1,0:T(8,128)(2,1)} %bitcast.32, ...), custom_call_target="tpu_custom_call" | custom-call | flops 754974720 | bytes 7617604 | tf_op jit(solution)/shard_map/front/pallas_call | solution.py:603
  55.5 19.7 %all_to_all.40.recv = bf16[16,48,384]{2,1,0:T(8,128)(2,1)} all-to-all(bf16[16,48,384]{2,1,0:T(8,128)(2,1)} %get-tuple-element.78), channel_id=1, replica_groups=mesh['dp'=8,'seq'=16] {'seq'}, dimensions={0} | all-to-all | bytes 1179648 | tf_op jit(solution)/shard_map/all_to_all | solution.py:628
  77.2 3.6 %all-to-all-start.1 = ((bf16[16,32,384]{2,1,0:T(8,128)(2,1)}), bf16[16,32,384]{2,1,0:T(8,128)(2,1)S(1)}, u32[]{:S(2)}, u32[]{:S(2)}) async-start(bf16[16,32,384]{2,1,0:T(8,128)(2,1)} %scan_states.1), calls=%async_computation.1 | async-start | bytes 786432 | tf_op jit(solution)/shard_map/all_to_all | solution.py:628
  82.1 13.2 %local_mix.1 = (f32[256,1536]{1,0:T(8,128)}, f32[256,1536]{1,0:T(8,128)}) custom-call(f32[256,1792]{1,0:T(8,128)} %get-tuple-element.73.cs, f32[256,128]{1,0:T(8,128)} %get-tuple-element.75.dt, f32[256,128]{1,0:T(8,128)} %get-tuple-element.74.cum), custom_call_target="tpu_custom_call" | custom-call | flops 1610612736 | bytes 5242880 | tf_op jit(solution)/shard_map/local_mix/pallas_call | solution.py:603
  95.3 6.3 %gate_products.1 = (f32[256,1536]{1,0:T(8,128)}, f32[256,1536]{1,0:T(8,128)}) custom-call(bf16[272,768]{1,0:T(8,128)(2,1)} %get-tuple-element.72.u, bf16[256,768]{1,0:T(8,128)(2,1)} %bitcast.35, bf16[3072,768]{1,0:T(8,128)(2,1)} %all-gather.2.cloned.1.call-done.rest), custom_call_target="tpu_custom_call" | custom-call | flops 1207959552 | bytes 8675328 | tf_op jit(solution)/shard_map/gate_products/pallas_call | solution.py:603
  102.4 17.9 %gated_norm.1 = (bf16[256,1536]{1,0:T(8,128)(2,1)}, bf16[256,1536]{1,0:T(8,128)(2,1)}, bf16[256,1536]{1,0:T(8,128)(2,1)}, f32[256,128]{1,0:T(8,128)}, f32[1,1536...) custom-call(f32[1]{0:T(128)} %bitcast.15.cont, f32[256,1792]{1,0:T(8,128)} %get-tuple-element.73.cs, ...), custom_call_target="tpu_custom_call" | custom-call | flops 301989888 | bytes 11749892 | tf_op jit(solution)/shard_map/gated_norm/pallas_call | solution.py:603
  120.4 7.2 %all-to-all-start.2 = ((bf16[16,48,384]{2,1,0:T(8,128)(2,1)}), bf16[16,48,384]{2,1,0:T(8,128)(2,1)S(1)}, u32[]{:S(2)}, u32[]{:S(2)}) async-start(bf16[16,48,384]{2,1,0:T(8,128)(2,1)} %get-tuple-element.92), calls=%async_computation.2 | async-start | bytes 1179648 | tf_op jit(solution)/shard_map/all_to_all | solution.py:628
  128.1 9.8 %all-to-all-done.2.recv = bf16[16,48,384]{2,1,0:T(8,128)(2,1)S(1)} async-done(((bf16[16,48,384]{2,1,0:T(8,128)(2,1)}), bf16[16,48,384]{2,1,0:T(8,128)(2,1)S(1)}, u32[]{:S(2)}, u32[]{:S(2)}) %all-to-all-start.2) | async-done | bytes 589856 | tf_op jit(solution)/shard_map/all_to_all | solution.py:628
  140.7 3.7 %all-to-all-start.3 = ((bf16[16,32,384]{2,1,0:T(8,128)(2,1)}), bf16[16,32,384]{2,1,0:T(8,128)(2,1)S(1)}, u32[]{:S(2)}, u32[]{:S(2)}) async-start(bf16[16,32,384]{2,1,0:T(8,128)(2,1)} %scan_adjoints.1), calls=%async_computation.3 | async-start | bytes 786432 | tf_op jit(solution)/shard_map/all_to_all | solution.py:628
  144.5 7.1 %out_and_grads.1 = (bf16[256,768]{1,0:T(8,128)(2,1)}, bf16[4,384,768]{2,1,0:T(8,128)(2,1)}, bf16[4,384,768]{2,1,0:T(8,128)(2,1)}) custom-call(s32[8]{0:T(128)} %stack.57.ids, bf16[256,768]{1,0:T(8,128)(2,1)} %bitcast.33, bf16[272,768]{1,0:T(8,128)(2,1)} %get-tuple-element.72.u, bf16[256,1536]{1,0:T(8,128)(2,1)} %get-tuple-element.82.n16, ...), custom_call_target="tpu_custom_call" | custom-call | flops 1811939328 | bytes 12607520 | tf_op jit(solution)/shard_map/out_and_grads/pallas_call | solution.py:603
  151.7 14.5 %local_back.1 = (f32[256,1536]{1,0:T(8,128)}, f32[256,1536]{1,0:T(8,128)}, f32[256,256]{1,0:T(8,128)}, f32[256,256]{1,0:T(8,128)}) custom-call(f32[256,1792]{1,0:T(8,128)} %get-tuple-element.73.cs, f32[256,128]{1,0:T(8,128)} %get-tuple-element.75.dt, f32[256,128]{1,0:T(8,128)} %get-tuple-element.74.cum, bf16[256,1536]{1,0:T(8,128)(2,1)} %get-tuple-element.87.dm16), custom_call_target="tpu_custom_call" | custom-call | flops 3221225472 | bytes 6553600 | tf_op jit(solution)/shard_map/local_back/pallas_call | solution.py:603
  166.9 25.1 %last_back.1 = (f32[256,768]{1,0:T(8,128)}, f32[16,768]{1,0:T(8,128)}, bf16[4,96,2048]{2,1,0:T(8,128)(2,1)}, bf16[4,96,2048]{2,1,0:T(8,128)(2,1)}) custom-call(s32[16]{0:T(128)} %stack.64.ids, f32[1]{0:T(128)} %bitcast.15.cont, bf16[256,768]{1,0:T(8,128)(2,1)} %bitcast.34, bf16[16,768]{1,0:T(8,128)(2,1)} %copy-done.26, f32[1,768]{1,0:T(1,128)} %reshape.95.gin, ...), custom_call_target="tpu_custom_call" | custom-call | flops 2113929216 | bytes 22286404 | tf_op jit(solution)/shard_map/last_back/pallas_call | solution.py:603
  192.7 3.2 %collective-permute-done.13.b = bf16[4,96,2048]{2,1,0:T(8,128)(2,1)S(1)} collective-permute-done((bf16[4,96,2048]{2,1,0:T(8,128)(2,1)}, bf16[4,96,2048]{2,1,0:T(8,128)(2,1)S(1)}, u32[]{:S(2)}, u32[]{:S(2)}) %collective-permute-start.13) | collective-permute-done | bytes 1572896 | tf_op jit(solution)/shard_map/ppermute | solution.py:632
  197.1 3.8 %add_tail_cores.1 = (bf16[96,2048]{1,0:T(8,128)(2,1)}, bf16[96,2048]{1,0:T(8,128)(2,1)}, bf16[96,2048]{1,0:T(8,128)(2,1)}, bf16[96,2048]{1,0:T(8,128)(2,1)}) custom-call(bf16[4,96,2048]{2,1,0:T(8,128)(2,1)} %get-tuple-element.104.a, bf16[4,96,2048]{2,1,0:T(8,128)(2,1)} %copy-done.6), custom_call_target="tpu_custom_call" | custom-call | tf_op jit(solution)/shard_map/add_tail_cores/pallas_call | solution.py:635
  200.8 2.4 collective-permute-start.15
  205.7 4.5 %add_rest_cores.1 = (bf16[384,768]{1,0:T(8,128)(2,1)}, bf16[384,768]{1,0:T(8,128)(2,1)}, bf16[384,768]{1,0:T(8,128)(2,1)}, bf16[384,768]{1,0:T(8,128)(2,1)}) custom-call(bf16[4,384,768]{2,1,0:T(8,128)(2,1)} %get-tuple-element.98.a, bf16[4,384,768]{2,1,0:T(8,128)(2,1)} %copy-done.2), custom_call_target="tpu_custom_call" | custom-call | tf_op jit(solution)/shard_map/add_rest_cores/pallas_call | solution.py:635
  213.0 9.6 %collective-permute-done.14.b = bf16[96,2048]{1,0:T(8,128)(2,1)S(1)} collective-permute-done((bf16[96,2048]{1,0:T(8,128)(2,1)}, bf16[96,2048]{1,0:T(8,128)(2,1)S(1)}, u32[]{:S(2)}, u32[]{:S(2)}) %collective-permute-start.14) | collective-permute-done | bytes 393248 | tf_op jit(solution)/shard_map/ppermute | solution.py:647
  226.7 7.0 %all-to-all-start.6 = ((bf16[16,96,128]{2,1,0:T(8,128)(2,1)}), bf16[16,96,128]{2,1,0:T(8,128)(2,1)S(1)}, u32[]{:S(2)}, u32[]{:S(2)}) async-start(bf16[16,96,128]{2,1,0:T(8,128)(2,1)} %add_tail_y.1), calls=%async_computation.6 | async-start | bytes 786432 | tf_op jit(solution)/shard_map/all_to_all | solution.py:628
  233.7 13.7 %collective-permute-done.10.b = bf16[384,768]{1,0:T(8,128)(2,1)S(1)} collective-permute-done((bf16[384,768]{1,0:T(8,128)(2,1)}, bf16[384,768]{1,0:T(8,128)(2,1)S(1)}, u32[]{:S(2)}, u32[]{:S(2)}) %collective-permute-start.10) | collective-permute-done | bytes 589856 | tf_op jit(solution)/shard_map/ppermute | solution.py:647
  248.9 2.7 add_rest_y.1
  251.6 7.0 %all-to-all-start.4 = ((bf16[16,144,128]{2,1,0:T(8,128)(2,1)}), bf16[16,144,128]{2,1,0:T(8,128)(2,1)S(1)}, u32[]{:S(2)}, u32[]{:S(2)}) async-start(bf16[16,144,128]{2,1,0:T(8,128)(2,1)} %bitcast.39), calls=%async_computation.4 | async-start | bytes 1179648 | tf_op jit(solution)/shard_map/all_to_all | solution.py:628
  260.4 9.8 %all-to-all-done.4.recv = bf16[16,144,128]{2,1,0:T(8,128)(2,1)S(1)} async-done(((bf16[16,144,128]{2,1,0:T(8,128)(2,1)}), bf16[16,144,128]{2,1,0:T(8,128)(2,1)S(1)}, u32[]{:S(2)}, u32[]{:S(2)}) %all-to-all-start.4) | async-done | bytes 589856 | tf_op jit(solution)/shard_map/all_to_all | solution.py:628
  270.2 3.6 %all-to-all-start.7 = ((bf16[16,96,128]{2,1,0:T(8,128)(2,1)}), bf16[16,96,128]{2,1,0:T(8,128)(2,1)S(1)}, u32[]{:S(2)}, u32[]{:S(2)}) async-start(bf16[16,96,128]{2,1,0:T(8,128)(2,1)} %add_tail_seq.1), calls=%async_computation.7 | async-start | bytes 786432 | tf_op jit(solution)/shard_map/all_to_all | solution.py:628
  275.8 7.1 %all-to-all-done.7.tail = bf16[16,96,128]{2,1,0:T(8,128)(2,1)S(1)} async-done(((bf16[16,96,128]{2,1,0:T(8,128)(2,1)}), bf16[16,96,128]{2,1,0:T(8,128)(2,1)S(1)}, u32[]{:S(2)}, u32[]{:S(2)}) %all-to-all-start.7) | async-done | bytes 393248 | tf_op jit(solution)/shard_map/all_to_all | solution.py:628
  282.9 3.7 %all-to-all-start.5 = ((bf16[16,144,128]{2,1,0:T(8,128)(2,1)}), bf16[16,144,128]{2,1,0:T(8,128)(2,1)S(1)}, u32[]{:S(2)}, u32[]{:S(2)}) async-start(bf16[16,144,128]{2,1,0:T(8,128)(2,1)} %add_rest_seq.1), calls=%async_computation.5 | async-start | bytes 1179648 | tf_op jit(solution)/shard_map/all_to_all | solution.py:628
  288.0 6.6 %collective-permute-done.8 = f32[16,768]{1,0:T(8,128)S(1)} collective-permute-done((f32[16,768]{1,0:T(8,128)S(1)}, f32[16,768]{1,0:T(8,128)S(1)}, u32[]{:S(2)}, u32[]{:S(2)}) %collective-permute-start.8) | collective-permute-done | bytes 49184 | tf_op jit(solution)/shard_map/ppermute | solution.py:773
  294.6 2.5 all-to-all-done.5
  297.9 2.5 finish.1
  (125 shorter events, 43.4 us)
Async XLA Ops:
  7.2 88.2 %all-gather.2.cloned.1.call-start = ((), (), s32[]{:S(2)}) async-start(), calls=%async_computation.8 | async-start | bytes 5308416 | tf_op jit(solution)/shard_map/all_gather | solution.py:682
  9.1 28.4 %copy-start.32 = (f32[24]{0:T(128)S(1)}, f32[24]{0:T(128)}, u32[]{:S(2)}) copy-start(f32[24]{0:T(128)} %param.23) | copy-start | bytes 292
  9.1 29.1 %copy-start.33 = (f32[48]{0:T(128)S(1)}, f32[48]{0:T(128)}, u32[]{:S(2)}) copy-start(f32[48]{0:T(128)} %param.22) | copy-start | bytes 580
  9.1 30.2 %copy-start.29 = (f32[768]{0:T(1024)S(1)}, f32[768]{0:T(1024)}, u32[]{:S(2)}) copy-start(f32[768]{0:T(1024)} %param.17) | copy-start | bytes 9220
  9.1 30.8 %copy-start.28 = (f32[1792]{0:T(1024)S(1)}, f32[1792]{0:T(1024)}, u32[]{:S(2)}) copy-start(f32[1792]{0:T(1024)} %param.21) | copy-start | bytes 21508
  9.2 32.0 %copy-start.1 = (bf16[96,1920]{1,0:T(8,128)(2,1)}, bf16[96,1920]{1,0:T(8,128)(2,1)S(1)}, u32[]{:S(2)}) copy-start(bf16[96,1920]{1,0:T(8,128)(2,1)S(1)} %fusion.1.refs_0_) | copy-start | bytes 1105924
  9.2 18.9 %collective-permute-start.3 = (bf16[96,1920]{1,0:T(8,128)(2,1)S(1)}, bf16[96,1920]{1,0:T(8,128)(2,1)S(1)}, u32[]{:S(2)}, u32[]{:S(2)}) collective-permute-start(bf16[96,1920]{1,0:T(8,128)(2,1)S(1)} %fusion.1.refs_0_), channel_id=1, source_target_pairs={{0,96},{16,112},{32,0},{48,16},{64,32},{80,48},{96,64},{112,80},{1... | collective-permute-start | bytes 1105928 | tf_op jit(solution)/shard_map/ppermute | solution.py:673
  12.3 15.8 %collective-permute-start.2 = (bf16[96,1920]{1,0:T(8,128)(2,1)S(1)}, bf16[96,1920]{1,0:T(8,128)(2,1)S(1)}, u32[]{:S(2)}, u32[]{:S(2)}) collective-permute-start(bf16[96,1920]{1,0:T(8,128)(2,1)S(1)} %fusion.1.refs_0_), channel_id=1, source_target_pairs={{0,64},{16,80},{32,96},{48,112},{64,0},{80,16},{96,32},{112,48},{1... | collective-permute-start | bytes 1105928 | tf_op jit(solution)/shard_map/ppermute | solution.py:673
  13.0 18.8 %collective-permute-start.1 = (bf16[96,1920]{1,0:T(8,128)(2,1)S(1)}, bf16[96,1920]{1,0:T(8,128)(2,1)S(1)}, u32[]{:S(2)}, u32[]{:S(2)}) collective-permute-start(bf16[96,1920]{1,0:T(8,128)(2,1)S(1)} %fusion.1.refs_0_), channel_id=1, source_target_pairs={{0,32},{16,48},{32,64},{48,80},{64,96},{80,112},{96,0},{112,16},{1... | collective-permute-start | bytes 1105928 | tf_op jit(solution)/shard_map/ppermute | solution.py:673
  31.8 9.3 %collective-permute-start.4 = (bf16[96,1920]{1,0:T(8,128)(2,1)S(1)}, bf16[96,1920]{1,0:T(8,128)(2,1)S(1)}, u32[]{:S(2)}, u32[]{:S(2)}) collective-permute-start(bf16[96,1920]{1,0:T(8,128)(2,1)S(1)} %fusion.1.refs_0_), channel_id=1, source_target_pairs={{0,16},{16,0},{32,48},{48,32},{64,80},{80,64},{96,112},{112,96},{1... | collective-permute-start | bytes 1105928 | tf_op jit(solution)/shard_map/ppermute | solution.py:674
  31.9 9.2 %collective-permute-start.7 = (bf16[96,1920]{1,0:T(8,128)(2,1)S(1)}, bf16[96,1920]{1,0:T(8,128)(2,1)S(1)}, u32[]{:S(2)}, u32[]{:S(2)}) collective-permute-start(bf16[96,1920]{1,0:T(8,128)(2,1)S(1)} %collective-permute-done.3.refs_3_), channel_id=1, source_target_pairs={{0,16},{16,0},{32,48},{48,32},{64,80},{80,64},{96,112},{112,96},{1... | collective-permute-start | bytes 1105928 | tf_op jit(solution)/shard_map/ppermute | solution.py:674
  32.4 8.7 %collective-permute-start.6 = (bf16[96,1920]{1,0:T(8,128)(2,1)S(1)}, bf16[96,1920]{1,0:T(8,128)(2,1)S(1)}, u32[]{:S(2)}, u32[]{:S(2)}) collective-permute-start(bf16[96,1920]{1,0:T(8,128)(2,1)S(1)} %collective-permute-done.2.refs_2_), channel_id=1, source_target_pairs={{0,16},{16,0},{32,48},{48,32},{64,80},{80,64},{96,112},{112,96},{1... | collective-permute-start | bytes 1105928 | tf_op jit(solution)/shard_map/ppermute | solution.py:674
  32.5 8.6 %collective-permute-start.5 = (bf16[96,1920]{1,0:T(8,128)(2,1)S(1)}, bf16[96,1920]{1,0:T(8,128)(2,1)S(1)}, u32[]{:S(2)}, u32[]{:S(2)}) collective-permute-start(bf16[96,1920]{1,0:T(8,128)(2,1)S(1)} %collective-permute-done.1.refs_1_), channel_id=1, source_target_pairs={{0,16},{16,0},{32,48},{48,32},{64,80},{80,64},{96,112},{112,96},{1... | collective-permute-start | bytes 1105928 | tf_op jit(solution)/shard_map/ppermute | solution.py:674
  33.7 7.4 %collective-permute-start = (bf16[16,768]{1,0:T(8,128)(2,1)S(1)}, bf16[16,768]{1,0:T(8,128)(2,1)S(1)}, u32[]{:S(2)}, u32[]{:S(2)}) collective-permute-start(bf16[16,768]{1,0:T(8,128)(2,1)S(1)} %slice_bitcast_fusion), channel_id=1, source_target_pairs={{0,1},{1,2},{2,3},{3,4},{4,5},{5,6},{6,7},{7,8},{8,9},{9,10},{10,1... | collective-permute-start | bytes 73736 | tf_op jit(solution)/shard_map/ppermute | solution.py:672
  77.2 24.5 %all-to-all-start.1 = ((bf16[16,32,384]{2,1,0:T(8,128)(2,1)}), bf16[16,32,384]{2,1,0:T(8,128)(2,1)S(1)}, u32[]{:S(2)}, u32[]{:S(2)}) async-start(bf16[16,32,384]{2,1,0:T(8,128)(2,1)} %scan_states.1), calls=%async_computation.1 | async-start | bytes 786432 | tf_op jit(solution)/shard_map/all_to_all | solution.py:628
  120.4 17.6 %all-to-all-start.2 = ((bf16[16,48,384]{2,1,0:T(8,128)(2,1)}), bf16[16,48,384]{2,1,0:T(8,128)(2,1)S(1)}, u32[]{:S(2)}, u32[]{:S(2)}) async-start(bf16[16,48,384]{2,1,0:T(8,128)(2,1)} %get-tuple-element.92), calls=%async_computation.2 | async-start | bytes 1179648 | tf_op jit(solution)/shard_map/all_to_all | solution.py:628
  140.7 25.5 %all-to-all-start.3 = ((bf16[16,32,384]{2,1,0:T(8,128)(2,1)}), bf16[16,32,384]{2,1,0:T(8,128)(2,1)S(1)}, u32[]{:S(2)}, u32[]{:S(2)}) async-start(bf16[16,32,384]{2,1,0:T(8,128)(2,1)} %scan_adjoints.1), calls=%async_computation.3 | async-start | bytes 786432 | tf_op jit(solution)/shard_map/all_to_all | solution.py:628
  151.6 52.7 %collective-permute-start.9 = (bf16[4,384,768]{2,1,0:T(8,128)(2,1)}, bf16[4,384,768]{2,1,0:T(8,128)(2,1)S(1)}, u32[]{:S(2)}, u32[]{:S(2)}) collective-permute-start(bf16[4,384,768]{2,1,0:T(8,128)(2,1)} %get-tuple-element.99), channel_id=1, source_target_pairs={{0,16},{16,0},{32,48},{48,32},{64,80},{80,64},{96,112},{112,96},{1... | collective-permute-start | bytes 7077896 | tf_op jit(solution)/shard_map/ppermute | solution.py:632
  192.1 3.8 %collective-permute-start.13 = (bf16[4,96,2048]{2,1,0:T(8,128)(2,1)}, bf16[4,96,2048]{2,1,0:T(8,128)(2,1)S(1)}, u32[]{:S(2)}, u32[]{:S(2)}) collective-permute-start(bf16[4,96,2048]{2,1,0:T(8,128)(2,1)} %get-tuple-element.105), channel_id=1, source_target_pairs={{0,16},{16,0},{32,48},{48,32},{64,80},{80,64},{96,112},{112,96},{1... | collective-permute-start | bytes 4718600 | tf_op jit(solution)/shard_map/ppermute | solution.py:632
  200.8 21.8 %collective-permute-start.14 = (bf16[96,2048]{1,0:T(8,128)(2,1)}, bf16[96,2048]{1,0:T(8,128)(2,1)S(1)}, u32[]{:S(2)}, u32[]{:S(2)}) collective-permute-start(bf16[96,2048]{1,0:T(8,128)(2,1)} %get-tuple-element.107), channel_id=1, source_target_pairs={{0,32},{16,48},{32,64},{48,80},{64,96},{80,112},{96,0},{112,16},{1... | collective-permute-start | bytes 1179656 | tf_op jit(solution)/shard_map/ppermute | solution.py:647
  200.8 21.8 %collective-permute-start.15 = (bf16[96,2048]{1,0:T(8,128)(2,1)}, bf16[96,2048]{1,0:T(8,128)(2,1)S(1)}, u32[]{:S(2)}, u32[]{:S(2)}) collective-permute-start(bf16[96,2048]{1,0:T(8,128)(2,1)} %get-tuple-element.108), channel_id=1, source_target_pairs={{0,64},{16,80},{32,96},{48,112},{64,0},{80,16},{96,32},{112,48},{1... | collective-permute-start | bytes 1179656 | tf_op jit(solution)/shard_map/ppermute | solution.py:647
  203.2 20.3 %collective-permute-start.16 = (bf16[96,2048]{1,0:T(8,128)(2,1)}, bf16[96,2048]{1,0:T(8,128)(2,1)S(1)}, u32[]{:S(2)}, u32[]{:S(2)}) collective-permute-start(bf16[96,2048]{1,0:T(8,128)(2,1)} %get-tuple-element.109), channel_id=1, source_target_pairs={{0,96},{16,112},{32,0},{48,16},{64,32},{80,48},{96,64},{112,80},{1... | collective-permute-start | bytes 1179656 | tf_op jit(solution)/shard_map/ppermute | solution.py:647
  210.2 37.1 %collective-permute-start.10 = (bf16[384,768]{1,0:T(8,128)(2,1)}, bf16[384,768]{1,0:T(8,128)(2,1)S(1)}, u32[]{:S(2)}, u32[]{:S(2)}) collective-permute-start(bf16[384,768]{1,0:T(8,128)(2,1)} %get-tuple-element.101), channel_id=1, source_target_pairs={{0,32},{16,48},{32,64},{48,80},{64,96},{80,112},{96,0},{112,16},{1... | collective-permute-start | bytes 1769480 | tf_op jit(solution)/shard_map/ppermute | solution.py:647
  211.2 36.2 %collective-permute-start.11 = (bf16[384,768]{1,0:T(8,128)(2,1)}, bf16[384,768]{1,0:T(8,128)(2,1)S(1)}, u32[]{:S(2)}, u32[]{:S(2)}) collective-permute-start(bf16[384,768]{1,0:T(8,128)(2,1)} %get-tuple-element.102), channel_id=1, source_target_pairs={{0,64},{16,80},{32,96},{48,112},{64,0},{80,16},{96,32},{112,48},{1... | collective-permute-start | bytes 1769480 | tf_op jit(solution)/shard_map/ppermute | solution.py:647
  222.6 25.4 %collective-permute-start.12 = (bf16[384,768]{1,0:T(8,128)(2,1)}, bf16[384,768]{1,0:T(8,128)(2,1)S(1)}, u32[]{:S(2)}, u32[]{:S(2)}) collective-permute-start(bf16[384,768]{1,0:T(8,128)(2,1)} %get-tuple-element.103), channel_id=1, source_target_pairs={{0,96},{16,112},{32,0},{48,16},{64,32},{80,48},{96,64},{112,80},{1... | collective-permute-start | bytes 1769480 | tf_op jit(solution)/shard_map/ppermute | solution.py:647
  226.7 24.9 %all-to-all-start.6 = ((bf16[16,96,128]{2,1,0:T(8,128)(2,1)}), bf16[16,96,128]{2,1,0:T(8,128)(2,1)S(1)}, u32[]{:S(2)}, u32[]{:S(2)}) async-start(bf16[16,96,128]{2,1,0:T(8,128)(2,1)} %add_tail_y.1), calls=%async_computation.6 | async-start | bytes 786432 | tf_op jit(solution)/shard_map/all_to_all | solution.py:628
  251.6 18.6 %all-to-all-start.4 = ((bf16[16,144,128]{2,1,0:T(8,128)(2,1)}), bf16[16,144,128]{2,1,0:T(8,128)(2,1)S(1)}, u32[]{:S(2)}, u32[]{:S(2)}) async-start(bf16[16,144,128]{2,1,0:T(8,128)(2,1)} %bitcast.39), calls=%async_computation.4 | async-start | bytes 1179648 | tf_op jit(solution)/shard_map/all_to_all | solution.py:628
  260.4 26.2 %copy-start.31 = (f32[16,768]{1,0:T(8,128)S(1)}, f32[16,768]{1,0:T(8,128)}, u32[]{:S(2)}) copy-start(f32[16,768]{1,0:T(8,128)} %get-tuple-element.97) | copy-start | bytes 147460
  260.4 27.5 %copy-start.17 = (f32[256,768]{1,0:T(8,128)S(1)}, f32[256,768]{1,0:T(8,128)}, u32[]{:S(2)}) copy-start(f32[256,768]{1,0:T(8,128)} %get-tuple-element.96) | copy-start | bytes 2359300
  270.2 12.6 %all-to-all-start.7 = ((bf16[16,96,128]{2,1,0:T(8,128)(2,1)}), bf16[16,96,128]{2,1,0:T(8,128)(2,1)S(1)}, u32[]{:S(2)}, u32[]{:S(2)}) async-start(bf16[16,96,128]{2,1,0:T(8,128)(2,1)} %add_tail_seq.1), calls=%async_computation.7 | async-start | bytes 786432 | tf_op jit(solution)/shard_map/all_to_all | solution.py:628
  282.9 14.2 %all-to-all-start.5 = ((bf16[16,144,128]{2,1,0:T(8,128)(2,1)}), bf16[16,144,128]{2,1,0:T(8,128)(2,1)S(1)}, u32[]{:S(2)}, u32[]{:S(2)}) async-start(bf16[16,144,128]{2,1,0:T(8,128)(2,1)} %add_rest_seq.1), calls=%async_computation.5 | async-start | bytes 1179648 | tf_op jit(solution)/shard_map/all_to_all | solution.py:628
  286.6 8.0 %collective-permute-start.8 = (f32[16,768]{1,0:T(8,128)S(1)}, f32[16,768]{1,0:T(8,128)S(1)}, u32[]{:S(2)}, u32[]{:S(2)}) collective-permute-start(f32[16,768]{1,0:T(8,128)S(1)} %copy-done.31), channel_id=1, source_target_pairs={{1,0},{2,1},{3,2},{4,3},{5,4},{6,5},{7,6},{8,7},{9,8},{10,9},{11,1... | collective-permute-start | bytes 147464 | tf_op jit(solution)/shard_map/ppermute | solution.py:773
  (27 other events, 145.8 us)
Sparse Core Ops, SparseCore 0:
  31.9 34.1 all-gather.1

commit v2 on v1

v2 whole, which is shorter than its diff:
```python
from functools import partial

import jax
import jax.numpy as jnp
from jax import lax
from jax.experimental import pallas as pl
from jax.experimental.pallas import tpu as pltpu
from jax.sharding import PartitionSpec as P

F32, BF = jnp.float32, jnp.bfloat16
EPS = 1e-05
LOG2E = 1.4426950408889634
D, H, E, N, T = 768, 24, 1536, 64, 256
C = E + 4 * N
CD = C + 128
HALO = 16
WIDE = E // 256
DP, SEQ = 8, 16
VMEM = 56 * 1024 * 1024
SMALL = 12 * 1024 * 1024


def iota(shape, dim):
    return lax.broadcasted_iota(jnp.int32, shape, dim)


def mm(a, b):
    return jnp.dot(a, b, preferred_element_type=F32)


def mm_nt(a, b):
    return lax.dot_general(a, b, (((1,), (1,)), ((), ())), preferred_element_type=F32)


def flip(v):
    return v.astype(F32).T.astype(v.dtype)


def sigmoid(v):
    return 1.0 / (1.0 + jnp.exp(-v))


def silu(v):
    return v * sigmoid(v)


def split2(v):
    hi = v.astype(BF)
    return hi, (v - hi.astype(F32)).astype(BF)


def pair(v):
    return jnp.concatenate(split2(v), axis=1)


def onehot(cond):
    return jnp.where(cond, 1.0, 0.0).astype(BF)


def marks():
    columns = onehot((iota((256, E), 0) & 127) == (iota((256, E), 1) >> 6))
    return columns, onehot((iota((E, 128), 0) >> 6) == iota((E, 128), 1))


def to_front(v):
    return pltpu.roll(v, 128 - H, 1)


def to_back(v):
    return pltpu.roll(v, H, 1)


def pairs_of(v):
    return pair(v), pair(to_front(v))


def tri_sum(mask, v):
    hi = v.astype(BF)
    rest = v - hi.astype(F32)
    mid = rest.astype(BF)
    low = (rest - mid.astype(F32)).astype(BF)
    return mm(mask, hi) + mm(mask, mid) + mm(mask, low)


def tri(cond):
    return onehot(cond(iota((T, T), 0), iota((T, T), 1)))


def lanes(rows=T):
    return iota((rows, 128), 1)


def wide(i):
    return pl.ds(pl.multiple_of(i * 256, 256), 256)


def fetch(sources, sems, tiles=WIDE):
    def copies(i):
        return [
            pltpu.make_async_copy(src.at[:, wide(i)], dst.at[:, wide(i)], sems.at[k, i])
            for k, (src, dst) in enumerate(sources)
        ]

    for i in range(tiles):
        for copy in copies(i):
            copy.start()

    def wait(i):
        for copy in copies(i):
            copy.wait()

    return wait


def parts_of_bc(act):
    return [act[:, N * k : N * k + N].astype(BF) for k in range(4)]


def ends(cum):
    return jnp.where(lanes(1) < H, cum[T - 1 : T], cum[0:1])


def put_slices(pay, i, first, second, dec_first, dec_second):
    row = iota((16, 128), 0)
    for e in range(2):
        at = slice(128 * e, 128 * e + 128)
        tile = 2 * i + e
        group = lax.div(tile, 3)
        into = pl.ds(pl.multiple_of(lax.rem(tile, 3) * 128, 128), 128)
        a, b = dec_first[:, at], dec_second[:, at]
        ah, bh = a.astype(BF).astype(F32), b.astype(BF).astype(F32)
        dec = jnp.where(
            row == 0, ah, jnp.where(row == 1, a - ah, jnp.where(row == 2, bh, b - bh))
        )
        dec = jnp.where(row < 4, dec, 0.0).astype(BF)
        for q in range(4):
            j = 4 * group + q
            pay[j, 0:16, into] = first[16 * q : 16 * q + 16, at].astype(BF)
            pay[j, 16:32, into] = second[16 * q : 16 * q + 16, at].astype(BF)
            pay[j, 32:48, into] = dec


def take_slices(recv, first, second, first_scale):
    for j in range(SEQ):
        rows, at = pl.ds(16 * (j % 4), 16), pl.ds(384 * (j // 4), 384)
        first[rows, at] = (recv[j, 0:16].astype(F32) * first_scale).astype(BF)
        second[rows, at] = recv[j, 16:32]


def load_weights(ids, parts, w, sem):
    copies = [
        pltpu.make_async_copy(
            parts[k], w.at[pl.ds(pl.multiple_of(ids[k] * 96, 32), 96)], sem.at[k]
        )
        for k in range(8)
    ]
    for copy in copies:
        copy.start()
    return copies


def load_rest(rest, wg, wo, sem):
    gates, outs = [], []
    for p in range(DP):
        at = 384 * p
        if wg is not None:
            gates.append((rest.at[pl.ds(at, 96)], wg.at[0, pl.ds(96 * p, 96)]))
            gates.append((rest.at[pl.ds(at + 96, 96)], wg.at[1, pl.ds(96 * p, 96)]))
        if wo is not None:
            outs.append((rest.at[pl.ds(at + 192, 192)], wo.at[pl.ds(192 * p, 192)]))
    copies = [pltpu.make_async_copy(a, b, sem.at[k]) for k, (a, b) in enumerate(gates + outs)]
    for copy in copies:
        copy.start()
    return copies[: len(gates)], copies[len(gates) :]


def finish_all(copies):
    for copy in copies:
        copy.wait()


def front(ids, cont, tok, halo, gin, cw, cb, dtb, alog, hc, *refs):
    parts, outs, (w, cif, csv, civ, sem, osem) = refs[:8], refs[8:15], refs[15:]
    u_out, ci_out, cs_out, sraw_out, dt_out, cum_out, pay = outs
    copies = load_weights(ids, parts, w, sem)
    x = jnp.concatenate([halo[...], tok[...]], axis=0).astype(F32)
    u = x * lax.rsqrt(jnp.mean(x * x, axis=1, keepdims=True) + EPS) * gin[...]
    u_out[...] = u.astype(BF)
    keep = cont[0]
    mask = jnp.where(iota((HALO + T, 1), 0) < HALO, keep, 1.0)
    finish_all(copies)
    sraw = mm(u_out[HALO:, :], w[:, C:]) + dtb[...]
    sraw_out[...] = sraw
    dt = jnp.maximum(sraw, 0.0) + jnp.log1p(jnp.exp(-jnp.abs(sraw)))
    dt = jnp.where(lanes() < 2 * H, dt, 0.0)
    dt_out[...] = dt
    rate = jnp.where(lanes(1) < 2 * H, jnp.exp(alog[...]), 0.0)
    la = -dt * rate
    cum = jnp.where(
        lanes() < H,
        tri_sum(tri(lambda r, c: r >= c), la),
        tri_sum(tri(lambda r, c: r <= c), la),
    )
    cum_out[...] = cum
    last = ends(cum)
    tail_f, tail_r = pairs_of(jnp.exp(last - cum) * dt)
    dec_f, dec_r = pairs_of(jnp.broadcast_to(jnp.exp(last) * keep, (16, 128)))

    def outward(i):
        at = wide(i)
        return [
            pltpu.make_async_copy(csv.at[:, at], cs_out.at[:, at], osem.at[0, i]),
            pltpu.make_async_copy(civ.at[:, at], ci_out.at[:, at], osem.at[1, i]),
        ]

    def convolve(i):
        at = wide(i)
        ci = (mm(u_out[...], w[:, at]) * mask).astype(BF)
        civ[:, at] = ci
        for e in range(2):
            here = pl.ds(pl.multiple_of(i * 256 + 128 * e, 128), 128)
            cif[e] = ci[:, 128 * e : 128 * e + 128].astype(F32)
            total = cb[:, here]
            for k in range(4):
                total = total + cw[k : k + 1, here] * cif[e, HALO - 3 + k : HALO - 3 + k + T]
            csv[:, here] = total
        for copy in outward(i):
            copy.start()
        return silu(csv[:, at])

    bf, _, br, _ = parts_of_bc(convolve(WIDE))
    bf_t, br_t = flip(bf), flip(br)

    def tile(i, _):
        at = wide(i)
        x_act = convolve(i)
        sf = mm(bf_t, (mm(tail_f, hc[:, at]) * x_act).astype(BF))
        sr = mm(br_t, (mm(tail_r, hc[:, at]) * x_act).astype(BF)) * keep
        put_slices(pay, i, sf, sr, mm(dec_f, hc[:, at]), mm(dec_r, hc[:, at]))
        return 0

    lax.fori_loop(0, WIDE, tile, 0)
    for i in range(WIDE + 1):
        finish_all(outward(i))


def scan_blocks(recv, out):
    carry = jnp.zeros((16, 384), F32)
    back = jnp.zeros((16, 384), F32)
    for i in range(SEQ):
        k = SEQ - 1 - i
        out[i, 0:16] = carry.astype(BF)
        out[k, 16:32] = back.astype(BF)
        dec = recv[i, 32:48].astype(F32)
        carry = (dec[0:1] + dec[1:2]) * carry + recv[i, 0:16].astype(F32)
        dec = recv[k, 32:48].astype(F32)
        back = (dec[2:3] + dec[3:4]) * back + recv[k, 16:32].astype(F32)


def columns_of(cum2, col, base=0):
    for h in range(col.shape[0]):
        col[h] = jnp.broadcast_to(cum2[:, base + h : base + h + 1], (T, 128))


def by_head(v):
    head = iota((T, 256), 1) >> 6
    return [jnp.where(head == e, v, 0.0).astype(BF) for e in range(4)]


def low_full(left, right):
    right = jnp.concatenate([jnp.zeros((128, 128), right.dtype), right], axis=0)
    return jnp.concatenate([left, right], axis=1)


def up_full(left, right):
    left = jnp.concatenate([left, jnp.zeros((128, 128), left.dtype)], axis=0)
    return jnp.concatenate([left, right], axis=1)


def local_mix(forward, cs, dt, cum, hc, *refs):
    if forward:
        y, csv, ysv, hcv, col, row, g, sem, osem = refs
    else:
        ylf, dsk, y, base_out, csv, ysv, yfv, bsv, hcv, col, row, g, sem, osem = refs
    hc_copy = pltpu.make_async_copy(hc, hcv, sem.at[2, 1])
    hc_copy.start()
    first = 0 if forward else H
    bc = pltpu.make_async_copy(cs.at[:, E:], csv.at[:, E:], sem.at[2, 0])
    bc.start()
    wait = fetch([(cs, csv)] if forward else [(cs, csv), (ylf, yfv)], sem)
    cum2 = cum[...] * LOG2E
    row[...] = cum2.T
    columns_of(cum2, col, first)
    dt2 = pairs_of(dt[...])[0 if forward else 1]
    bc.wait()
    parts = parts_of_bc(silu(csv[:, E:]))
    b, cc = parts[:2] if forward else parts[2:]
    r, c = iota((T, T), 0), iota((T, T), 1)
    g[...] = jnp.where(r > c if forward else r < c, mm_nt(cc, b), 0.0)
    hc_copy.wait()

    def weights(h):
        at, along = col[h], row[pl.ds(first + h, 1), :]
        if forward:
            left = jnp.exp2(jnp.minimum(at - along[:, :128], 0.0)) * g[:, :128]
            right = jnp.exp2(jnp.minimum(at[128:] - along[:, 128:], 0.0)) * g[128:, 128:]
            return low_full(left.astype(BF), right.astype(BF))
        left = jnp.exp2(jnp.minimum(at[:128] - along[:, :128], 0.0)) * g[:128, :128]
        right = jnp.exp2(jnp.minimum(at - along[:, 128:], 0.0)) * g[:, 128:]
        return up_full(left.astype(BF), right.astype(BF))

    def outward(i):
        pairs = [(ysv, y)] if forward else [(ysv, y), (bsv, base_out)]
        return [
            pltpu.make_async_copy(a.at[:, wide(i)], b.at[:, wide(i)], osem.at[k, i])
            for k, (a, b) in enumerate(pairs)
        ]

    def tile(i, _):
        at = wide(i)
        wait(i)
        x = silu(csv[:, at])
        xs = by_head(x * mm(dt2, hcv[:, at]))
        left = jnp.concatenate([weights(4 * i + e) for e in range(4)], axis=1)
        own = mm(left, jnp.concatenate(xs, axis=0))
        ysv[:, at] = own.astype(BF)
        if not forward:
            bsv[:, at] = own + yfv[:, at].astype(F32) + dsk[:, at] * x
        for copy in outward(i):
            copy.start()
        return 0

    lax.fori_loop(0, WIDE, tile, 0)
    for i in range(WIDE):
        finish_all(outward(i))


def gate_products(u, dout, rest, gate, dn, wg, wo, sem):
    gates, outs = load_rest(rest, wg, wo, sem)
    finish_all(gates)
    gate[:, :D] = mm(u[HALO:, :], wg[0])
    gate[:, D:] = mm(u[HALO:, :], wg[1])
    finish_all(outs)
    dn[...] = mm_nt(dout[...], wo[...])


def gated_norm(cont, cum, recv, gout, hc, cs, base, gate, dn, *refs):
    (n16, dg16, dm16, dgout, pay), scratch = refs[:5], refs[5:]
    bcv, yv, gv, dv, gds, eff, efr, nv, dgv, dmv, sf, sr, bsem, sem, osem = scratch
    bc = pltpu.make_async_copy(cs.at[:, E:], bcv, bsem)
    bc.start()
    wait = fetch([(base, yv), (gate, gv), (dn, dv)], sem)
    keep = cont[0]
    take_slices(recv, sf, sr, keep)
    cumv = cum[...]
    ef_f, ef_r = pairs_of(jnp.exp(cumv))
    dec_f, dec_r = pairs_of(jnp.broadcast_to(jnp.exp(ends(cumv)) * keep, (16, 128)))
    bc.wait()
    _, cf, _, cr = parts_of_bc(silu(bcv[...]))
    zero = jnp.zeros((T, 128), F32)

    def first(i, sums):
        at = wide(i)
        wait(i)
        ef, er = mm(ef_f, hc[:, at]), mm(ef_r, hc[:, at])
        eff[:, at] = ef
        efr[:, at] = er
        m = yv[:, at] + ef * mm(cf, sf[:, at]) + er * mm(cr, sr[:, at])
        g = gv[:, at]
        sg = sigmoid(g)
        sl = g * sg
        gd = m * sl
        gds[:, at] = gd
        gv[:, at] = sl
        yv[:, at] = m * sg * (1.0 + g * (1.0 - sg))
        squares, crossed = gd * gd, dv[:, at] * gout[:, at] * gd
        return (
            sums[0] + squares[:, :128] + squares[:, 128:],
            sums[1] + crossed[:, :128] + crossed[:, 128:],
        )

    squares, crossed = lax.fori_loop(0, WIDE, first, (zero, zero))
    rs = lax.rsqrt(jnp.sum(squares, axis=1, keepdims=True) / E + EPS)
    pull = jnp.sum(crossed, axis=1, keepdims=True) / E * (rs * rs * rs)
    cf_t, cr_t = flip(cf), flip(cr)

    def outward(i):
        return [
            pltpu.make_async_copy(a.at[:, wide(i)], b.at[:, wide(i)], osem.at[k, i])
            for k, (a, b) in enumerate([(nv, n16), (dgv, dg16), (dmv, dm16)])
        ]

    def second(i, _):
        at = wide(i)
        gd = gds[:, at]
        gdr = gd * rs
        go = gout[:, at]
        nv[:, at] = (gdr * go).astype(BF)
        d = dv[:, at]
        dgout[:, at] = jnp.sum(d * gdr, axis=0, keepdims=True)
        dgd = rs * (d * go) - gd * pull
        dgv[:, at] = (dgd * yv[:, at]).astype(BF)
        dm = dgd * gv[:, at]
        dmv[:, at] = dm.astype(BF)
        for copy in outward(i):
            copy.start()
        lf = mm(cf_t, (eff[:, at] * dm).astype(BF)) * keep
        lr = mm(cr_t, (efr[:, at] * dm).astype(BF))
        put_slices(pay, i, lr, lf, mm(dec_r, hc[:, at]), mm(dec_f, hc[:, at]))
        return 0

    lax.fori_loop(0, WIDE, second, 0)
    for i in range(WIDE):
        finish_all(outward(i))


def pieces_out(ids, sources, keep, send, sem):
    copies = []
    for ref, base in ((send, 12), (keep, 8)):
        for k in range(4):
            for src, rows, put in sources:
                start = pl.multiple_of(ids[base + k] * rows, 32)
                copies.append((src.at[pl.ds(start, rows)], put(ref, k)))
    return [pltpu.make_async_copy(a, b, sem.at[k]) for k, (a, b) in enumerate(copies)]


def out_and_rows(
    ids, cont, tok, u, dout, n16, dg16, dm16, cum, recv, hc, hr, rest, cs, ylf, ylr, *refs
):
    (out, rows, dc, keep, send), scratch = refs[:5], refs[5:]
    wo, n_t, u_t, dwo, dwg, bcv, yfv, yrv, sf, sr, bsem, sem, wsem, osem = scratch
    bc = pltpu.make_async_copy(cs.at[:, E:], bcv, bsem)
    bc.start()
    wait = fetch([(ylf, yfv), (ylr, yrv)], sem)
    _, copies = load_rest(rest, None, wo, wsem)
    n_t[...] = flip(n16[...])
    u_t[...] = flip(u[HALO:, :])

    def rows_out(i, _):
        at = pl.ds(pl.multiple_of(i * 256, 256), 256)
        dwo[at, :] = mm(n_t[at, :], dout[...]).astype(BF)
        return 0

    def rows_gate(i, _):
        at = pl.ds(pl.multiple_of(i * 256, 256), 256)
        dwg[at, :] = mm(u_t[at, :], dg16[...]).astype(BF)
        return 0

    lax.fori_loop(0, E // 256, rows_out, 0)
    lax.fori_loop(0, D // 256, rows_gate, 0)
    outward = pieces_out(
        ids,
        [
            (dwg.at[:, :D], 96, lambda ref, k: ref.at[k, 0:96]),
            (dwg.at[:, D:], 96, lambda ref, k: ref.at[k, 96:192]),
            (dwo, 192, lambda ref, k: ref.at[k, 192:384]),
        ],
        keep,
        send,
        osem,
    )
    for copy in outward:
        copy.start()
    take_slices(recv, sf, sr, cont[0])
    ef_f, ef_r = pairs_of(jnp.exp(cum[...]))
    bc.wait()
    _, cf, _, cr = parts_of_bc(silu(bcv[...]))

    def tile(i, sums):
        at = wide(i)
        wait(i)
        dm = dm16[:, at].astype(F32)
        new = []
        for ef2, c, s, yl in ((ef_f, cf, sf, yfv), (ef_r, cr, sr, yrv)):
            ef = mm(ef2, hc[:, at])
            y = yl[:, at].astype(F32) + ef * mm(c, s[:, at])
            new.append(mm((dm * y).astype(BF), hr[at, :]))
            new.append(mm_nt((ef * dm).astype(BF), s[:, at]))
        return tuple(a + b for a, b in zip(sums, new))

    zero, zn = jnp.zeros((T, 128), F32), jnp.zeros((T, N), F32)
    rf, dcf, rr, dcr = lax.fori_loop(0, WIDE, tile, (zero, zn, zero, zn))
    rows[...] = rf + to_back(rr)
    dc[...] = jnp.concatenate([dcf, dcr], axis=1)
    finish_all(copies)
    out[...] = (tok[...].astype(F32) + mm(n16[...], wo[...])).astype(BF)
    finish_all(outward)


def local_back(dt, cum, dm16, hc, cs, zf, zr, dgf, dgr, *scratch):
    csv, zfv, zrv, col, row, gf, gr, dm_t, sem, osem = scratch
    bc = pltpu.make_async_copy(cs.at[:, E:], csv.at[:, E:], sem.at[0, WIDE])
    bc.start()
    wait = fetch([(cs, csv)], sem)
    cum2 = cum[...] * LOG2E
    row[...] = cum2.T
    columns_of(cum2, col)
    dm_t[...] = flip(dm16[...])
    dt_f, dt_r = pairs_of(dt[...])
    bc.wait()
    bf, cf, br, cr = parts_of_bc(silu(csv[:, E:]))
    s, t = iota((T, T), 0), iota((T, T), 1)
    gf[...] = jnp.where(t > s, mm_nt(bf, cf), 0.0)
    gr[...] = jnp.where(t < s, mm_nt(br, cr), 0.0)
    dgf[...] = jnp.zeros((T, T), F32)
    dgr[...] = jnp.zeros((T, T), F32)

    def outward(i):
        return [
            pltpu.make_async_copy(a.at[:, wide(i)], b.at[:, wide(i)], osem.at[k, i])
            for k, (a, b) in enumerate([(zfv, zf), (zrv, zr)])
        ]

    def tile(i, _):
        at = wide(i)
        wait(i)
        x = silu(csv[:, at])
        ds = jnp.concatenate(by_head(dm16[:, at].astype(F32)), axis=0)
        dms = dm_t[at, :]
        for forward in (True, False):
            first = 0 if forward else H
            xs = by_head(x * mm(dt_f if forward else dt_r, hc[:, at]))
            ws = []
            small = jnp.zeros((128, 128), F32)
            large = jnp.zeros((T, 128), F32)
            for e in range(4):
                h = first + 4 * i + e
                at_s, along = col[h], row[pl.ds(h, 1), :]
                dw = mm(xs[e], dms)
                if forward:
                    ea = jnp.exp2(jnp.minimum(along[:, :128] - at_s[:128], 0.0))
                    eb = jnp.exp2(jnp.minimum(along[:, 128:] - at_s, 0.0))
                    ws.append(
                        up_full((ea * gf[:128, :128]).astype(BF), (eb * gf[:, 128:]).astype(BF))
                    )
                    small = small + ea * dw[:128, :128]
                    large = large + eb * dw[:, 128:]
                else:
                    ea = jnp.exp2(jnp.minimum(along[:, :128] - at_s, 0.0))
                    eb = jnp.exp2(jnp.minimum(along[:, 128:] - at_s[128:], 0.0))
                    ws.append(
                        low_full((ea * gr[:, :128]).astype(BF), (eb * gr[128:, 128:]).astype(BF))
                    )
                    large = large + ea * dw[:, :128]
                    small = small + eb * dw[128:, 128:]
            total = mm(jnp.concatenate(ws, axis=1), ds)
            if forward:
                zfv[:, at] = total.astype(BF)
                dgf[:128, :128] += small
                dgf[:, 128:] += large
            else:
                zrv[:, at] = total.astype(BF)
                dgr[:, :128] += large
                dgr[128:, 128:] += small
        for copy in outward(i):
            copy.start()
        return 0

    lax.fori_loop(0, WIDE, tile, 0)
    dgf[...] = jnp.where(t > s, dgf[...], 0.0)
    dgr[...] = jnp.where(t < s, dgr[...], 0.0)
    for i in range(WIDE):
        finish_all(outward(i))


def inner_back(
    ids, cont, tok, halo, gin, cw, alog, dsk, sraw, dt, cum, u, dout, dgf, dgr, back, fore, rows,
    dc, dgout, hc, hr, cs, zf, zr, dm16, ci, dg16, rest, *refs
):
    parts, (dtok, dhalo, dall, small_out), scratch = refs[:8], refs[8:12], refs[12:]
    csv, zfv, zrv, dmv, civ, dgv, w, wg, sf, sr, kf, kr, dcs, cif, du, small = scratch[:16]
    line, sem, csem, wsem, gsem, dsem = scratch[16:]
    bcc = pltpu.make_async_copy(cs.at[:, E:], csv.at[:, E:], csem.at[1])
    bcc.start()
    wait = fetch([(cs, csv), (zf, zfv), (zr, zrv), (dm16, dmv)], sem)
    cic = pltpu.make_async_copy(ci, civ, csem.at[0])
    cic.start()
    loads = load_weights(ids, parts, w, wsem) + load_rest(rest, wg, None, gsem)[0]
    loads.append(pltpu.make_async_copy(dg16, dgv, dsem))
    loads[-1].start()
    keep = cont[0]
    take_slices(back, kr, kf, keep)
    take_slices(fore, sf, sr, keep)
    cumv, dtv = cum[...], dt[...]
    last = ends(cumv)
    te_f, te_r = pairs_of(jnp.exp(last - cumv))
    dt_f, dt_r = pairs_of(dtv)
    line[...] = jnp.zeros((8, E), F32)
    dcs[:, 0:HALO] = jnp.zeros((C // 128, HALO, 128), F32)
    dcs[:, HALO + T :] = jnp.zeros((C // 128, 16, 128), F32)
    bcc.wait()
    bc = csv[:, E:]
    bf, cf, br, cr = parts_of_bc(silu(bc))

    def slope(v, sg):
        return sg * (1.0 + v * (1.0 - sg))

    def tile(i, sums):
        at = wide(i)
        wait(i)
        v = csv[:, at]
        sg = sigmoid(v)
        x = v * sg
        dm = dmv[:, at].astype(F32)
        line[2:3, at] = jnp.sum(dm * x, axis=0, keepdims=True)
        dx = dsk[:, at] * dm
        new = []
        for d, dt2, te2, z, k, s, b in (
            (0, dt_f, te_f, zfv, kf, sf, bf),
            (1, dt_r, te_r, zrv, kr, sr, br),
        ):
            dts, te = mm(dt2, hc[:, at]), mm(te2, hc[:, at])
            xd = (x * dts).astype(BF).astype(F32)
            zi, zt = z[:, at].astype(F32), te * mm(b, k[:, at])
            dx = dx + dts * (zi + zt)
            new.append(mm((xd * zi).astype(BF), hr[at, :]))
            new.append(mm((xd * zt).astype(BF), hr[at, :]))
            new.append(mm_nt((te * xd).astype(BF), k[:, at]))
            both = s[:, at].astype(F32) * k[:, at].astype(F32)
            line[d : d + 1, at] = jnp.sum(both, axis=0, keepdims=True)
        dx = dx * slope(v, sg)
        for e in range(2):
            dcs[2 * i + e, HALO : HALO + T] = dx[:, 128 * e : 128 * e + 128]
        return tuple(a + b for a, b in zip(sums, new))

    zero, zn = jnp.zeros((T, 128), F32), jnp.zeros((T, N), F32)
    sums = lax.fori_loop(0, WIDE, tile, (zero, zero, zn, zero, zero, zn))
    inner, tails = sums[0] + to_back(sums[3]), sums[1] + to_back(sums[4])
    gf16, gr16 = dgf[...].astype(BF), dgr[...].astype(BF)
    dbf = sums[2] + mm(gf16, cf)
    dbr = sums[5] + mm(gr16, cr)
    dcf = dc[:, :N] + mm(flip(gf16), bf)
    dcr = dc[:, N:] + mm(flip(gr16), br)
    dbc = jnp.concatenate([dbf, dcf, dbr, dcr], axis=1) * slope(bc, sigmoid(bc))
    for e in range(2):
        dcs[2 * WIDE + e, HALO : HALO + T] = dbc[:, 128 * e : 128 * e + 128]
    hi, lo = split2(line[...])
    heads = mm(hi, hr[...]) + mm(lo, hr[...])
    dots = heads[0:1] + to_back(heads)[1:2]
    rate = jnp.where(lanes(1) < 2 * H, jnp.exp(alog[...]), 0.0)
    v = rows[...] - inner
    dla = jnp.where(
        lanes() < H,
        tri_sum(tri(lambda r, c: r <= c), v) + tri_sum(tri(lambda r, c: r > c), tails),
        tri_sum(tri(lambda r, c: r >= c), v) + tri_sum(tri(lambda r, c: r < c), tails),
    ) + jnp.exp(last) * dots
    sg = sigmoid(sraw[...])
    ratio = jnp.where(dtv > 1e-20, sg / jnp.maximum(dtv, 1e-20), 1.0)
    dstep = (inner + tails) * ratio - dla * rate * sg
    dstep = jnp.where(lanes() < 2 * H, dstep, 0.0)
    dall[0:HALO, C:] = jnp.zeros((HALO, 128), BF)
    dall[HALO:, C:] = dstep.astype(BF)
    dal = jnp.broadcast_to(jnp.sum(dla * (-dtv * rate), axis=0, keepdims=True), (8, 128))
    small[...] = jnp.zeros((96, 128), F32)
    small[88:89] = jnp.sum(dstep, axis=0, keepdims=True)
    small[89:90] = jnp.where(lanes(1) < H, dal[0:1] + to_front(dal)[0:1], 0.0)
    small[90:91] = jnp.where(lanes(1) < H, heads[2:3], 0.0)
    mask = jnp.where(iota((HALO + T, 1), 0) < HALO, keep, 1.0)

    cic.wait()

    def convolution(i, _):
        at = pl.ds(pl.multiple_of(i * 128, 128), 128)
        g = dcs[i, HALO : HALO + T]
        cif[...] = civ[:, at].astype(F32)
        small[pl.ds(56 + i, 1)] = jnp.sum(g, axis=0, keepdims=True)
        total = jnp.zeros((HALO + T, 128), F32)
        for k in range(4):
            shifted = cif[HALO - 3 + k : HALO - 3 + k + T]
            small[pl.ds(14 * k + i, 1)] = jnp.sum(g * shifted, axis=0, keepdims=True)
            total = total + cw[k : k + 1, at] * dcs[i, 3 - k : 3 - k + HALO + T]
        dall[:, at] = (total * mask).astype(BF)
        return 0

    lax.fori_loop(0, C // 128, convolution, 0)
    for j in range(E // 128):
        small[70 + j : 71 + j] = dgout[:, 128 * j : 128 * j + 128]
    finish_all(loads)

    def input_grad(i, _):
        at = wide(i)
        du[:, at] = mm_nt(dall[...], w[at, :])
        du[HALO:, at] += mm_nt(dgv[:, :D], wg[0, at, :]) + mm_nt(dgv[:, D:], wg[1, at, :])
        return 0

    lax.fori_loop(0, D // 256, input_grad, 0)
    x = jnp.concatenate([halo[...], tok[...]], axis=0).astype(F32)
    r = lax.rsqrt(jnp.mean(x * x, axis=1, keepdims=True) + EPS)
    duxr = jnp.sum(du[...] * x * r, axis=0, keepdims=True)
    for j in range(6):
        small[82 + j : 83 + j] = duxr[:, 128 * j : 128 * j + 128]
    small_out[...] = small[...].astype(BF)
    dxh = du[...] * gin[...]
    dx = r * dxh - x * (r * r * r * jnp.mean(dxh * x, axis=1, keepdims=True))
    dhalo[...] = dx[:HALO]
    dtok[...] = dout[...].astype(F32) + dx[HALO:]


def weight_back(ids, u, dall, small, keep, send, u_t, dw, osem, ssem):
    u_t[...] = flip(u[...])
    extra = []
    for ref, base in ((send, 0), (keep, 4)):
        for k in range(4):
            extra.append(
                pltpu.make_async_copy(small, ref.at[k, :, pl.ds(CD, 128)], ssem.at[base + k])
            )
            extra[-1].start()

    def rows(i, _):
        at = pl.ds(pl.multiple_of(i * 256, 256), 256)
        dw[at, :] = mm(u_t[at, :], dall[...]).astype(BF)
        return 0

    lax.fori_loop(0, D // 256, rows, 0)
    copies = pieces_out(
        ids, [(dw, 96, lambda ref, k: ref.at[k, :, pl.ds(0, CD)])], keep, send, osem
    )
    for copy in copies:
        copy.start()
    finish_all(extra)
    finish_all(copies)


def add_pairs(a, b, *outs):
    for k in range(4):

        def rows(i, _, k=k):
            at = pl.ds(pl.multiple_of(i * 48, 16), 48)
            outs[k][at] = (a[k, at].astype(F32) + b[k, at].astype(F32)).astype(BF)
            return 0

        lax.fori_loop(0, a.shape[1] // 48, rows, 0)


def add_middle(one, up, three, down, out_one, out_three):
    half = one.shape[0] // 2
    for ref, part, out, at in ((one, up, out_one, 0), (three, down, out_three, half)):
        for r in range(0, 2 * half, 48):
            rows = slice(r, r + 48)
            total = ref[rows].astype(F32)
            if at <= r < at + half:
                total = total + part[r - at : r - at + 48].astype(F32)
            out[rows] = total.astype(BF)


def add_y(*refs):
    rest, tail, out = refs[:3], refs[3:7], refs[7]

    def total(parts, rows, at):
        return sum(part[rows, at].astype(F32) for part in parts).astype(BF)

    for j in range(6):
        for r in range(0, 384, 48):
            row = 384 * j + r
            out[row // 144, row % 144 : row % 144 + 48] = total(
                rest, slice(r, r + 48), slice(128 * j, 128 * j + 128)
            )
    for j in range(SEQ):
        out[j, 144:] = total(tail, slice(0, 96), slice(128 * j, 128 * j + 128))


def add_blocks(recv, out):
    total = recv[0].astype(F32)
    for i in range(1, SEQ):
        total = total + recv[i].astype(F32)
    low = total.astype(BF)
    for i in range(SEQ):
        out[i] = low


def finish(sums, dwin, dwdt, dwout, dcw, dcb, dgout, dgin, ddtb, dal, ddsk):
    def put(ref, at, start, rows):
        for r in range(0, rows, 48):
            j, k = (start + r) // 144, (start + r) % 144
            ref[r : r + 48, at] = sums[j, k : k + 48].astype(F32)

    for j in range(6):
        at = slice(128 * j, 128 * j + 128)
        put(dwin, at, 384 * j, 96)
        put(dwin, slice(D + 128 * j, D + 128 * j + 128), 384 * j + 96, 96)
        put(dwout, at, 384 * j + 192, 192)
    for j in range(14):
        dwin[:, E + 128 * j : E + 128 * j + 128] = sums[j, 144:].astype(F32)
    dwdt[...] = sums[14, 144:, 0 : 2 * H].astype(F32)
    small = sums[15, 144:].astype(F32)
    for j in range(14):
        at = slice(128 * j, 128 * j + 128)
        for k in range(4):
            dcw[k : k + 1, at] = small[14 * k + j : 14 * k + j + 1]
        dcb[at] = small[56 + j]
    for j in range(E // 128):
        dgout[128 * j : 128 * j + 128] = small[70 + j]
    for j in range(6):
        dgin[128 * j : 128 * j + 128] = small[82 + j]
    ddtb[...] = small[88, 0 : 2 * H]
    dal[...] = small[89, 0:H]
    ddsk[...] = small[90, 0:H]


V = pl.BlockSpec(memory_space=pltpu.VMEM)
S = pl.BlockSpec(memory_space=pltpu.SMEM)
ANY = pl.BlockSpec(memory_space=pl.ANY)


def shape(*dims, dtype=F32):
    return jax.ShapeDtypeStruct(dims, dtype)


def call(kernel, name, ins, outs, scratch=(), flops=0, apart=(), limit=VMEM, light=False):
    specs, args = zip(*ins)
    moved = sum(a.size * a.dtype.itemsize for a in args)
    moved += sum(o.size * o.dtype.itemsize for o in outs)
    return pl.pallas_call(
        kernel,
        name=name,
        out_shape=tuple(outs),
        in_specs=list(specs),
        out_specs=tuple(ANY if i in apart else V for i in range(len(outs))),
        scratch_shapes=list(scratch),
        cost_estimate=pl.CostEstimate(
            flops=flops, bytes_accessed=0 if light else moved, transcendentals=0
        ),
        compiler_params=pltpu.CompilerParams(vmem_limit_bytes=limit),
    )(*args)


def vm(*dims, dtype=F32):
    return pltpu.VMEM(dims, dtype)


def shift_y(k):
    return [(2 * y + c, 2 * ((y + k) % 4) + c) for y in range(4) for c in range(2)]


SWAP = [(i, i ^ 1) for i in range(DP)]


def exchange(value):
    return lax.all_to_all(value, "seq", 0, 0, tiled=True)


def add_swapped(keep, send, name, after=None):
    recv = lax.ppermute(send, "dp", SWAP)
    if after is not None:
        recv = together(recv, after)[0]
    rows, cols = keep.shape[1:]
    outs = [shape(rows, cols, dtype=BF)] * 4
    return call(add_pairs, name, [(V, keep), (V, recv)], outs, limit=SMALL)


def over_y(parts):
    return [parts[0]] + [lax.ppermute(parts[k], "dp", shift_y(k)) for k in (1, 2, 3)]


def together(*values):
    return lax.optimization_barrier(values)


def local(
    tokens, starts, g_in, w_in, w_dt, conv_w, conv_b, dt_bias, a_log, dskip, g_out, w_out, d_out
):
    dp = lax.axis_index("dp")
    y, core = dp // 2, dp % 2
    tok, dout = tokens[0], d_out[0]
    cont = (1 - starts[0]).astype(F32)

    row = lambda v: v.reshape(1, -1)
    pad = lambda v: jnp.pad(v, (0, 128 - v.shape[0])).reshape(1, 128)
    alog = pad(jnp.concatenate([a_log, a_log]))
    dsk = row(jnp.repeat(dskip, N))
    gin, gout, cb, dtb = row(g_in), row(g_out), row(conv_b), pad(dt_bias)
    to_y = [(y + k) % 4 for k in range(4)]
    from_y = [(y - k) % 4 for k in range(4)]
    ids = [2 * t + core for t in from_y] + [2 * t + 1 - core for t in from_y]
    ids = jnp.stack(ids + [2 * t + core for t in to_y] + [2 * t + 1 - core for t in to_y])

    own = jnp.concatenate([w_in[:, E:], jnp.pad(w_dt, ((0, 0), (0, 128 - 2 * H)))], axis=1)
    column = [lax.ppermute(own, "dp", shift_y(k)) for k in (1, 2, 3)]
    halo = lax.ppermute(tok[-HALO:], "seq", [(i, i + 1) for i in range(SEQ - 1)])
    beside = lax.ppermute(own, "dp", SWAP)
    rest_own = jnp.concatenate([w_in[:, :D], w_in[:, D:E], w_out], axis=0)
    hc, hr = marks()
    *column, halo, beside, rest_own, alog, dsk, gin, gout, cb, dtb, ids, hc, hr = together(
        *column, halo, beside, rest_own, alog, dsk, gin, gout, cb, dtb, ids, hc, hr
    )
    parts = [own, *column, beside] + [lax.ppermute(part, "dp", SWAP) for part in column]
    rest = lax.all_gather(rest_own, "dp", axis=0, tiled=True)

    part_ins = [(ANY, part) for part in parts]
    w_scratch = vm(D, CD, dtype=BF)
    dma = pltpu.SemaphoreType.DMA
    full, half, state = vm(T, E), vm(T, E, dtype=BF), vm(N, E, dtype=BF)

    u, ci, cs, sraw, dt, cum, pay = call(
        front,
        "front",
        [(S, ids), (S, cont), (V, tok), (V, halo), (V, gin), (V, conv_w), (V, cb)]
        + [(V, dtb), (V, alog), (V, hc)]
        + part_ins,
        [shape(HALO + T, D, dtype=BF), shape(HALO + T, C, dtype=BF), shape(T, C)]
        + [shape(T, 128)] * 3
        + [shape(SEQ, 48, 384, dtype=BF)],
        [w_scratch, vm(2, HALO + T, 128), vm(T, C), vm(HALO + T, C, dtype=BF)]
        + [dma((8,)), dma((2, WIDE + 1))],
        flops=2 * T * D * CD,
        apart=(1, 2),
    )

    def scan(got, name):
        out = shape(SEQ, 32, 384, dtype=BF)
        return call(scan_blocks, name, [(V, got)], [out], limit=SMALL)[0]

    mix_scratch = [vm(256, E, dtype=BF), vm(H, T, 128), vm(128, T), vm(T, T)]
    mix_scratch += [dma((3, WIDE)), dma((2, WIDE))]
    mix_cost = 2 * 24 * T * T * 256
    got = exchange(pay)
    ylf = call(
        partial(local_mix, True),
        "mix_forward",
        [(ANY, cs), (V, dt), (V, cum), (ANY, hc)],
        [shape(T, E, dtype=BF)],
        [vm(T, C), half] + mix_scratch,
        flops=mix_cost,
        apart=(0,),
    )[0]
    ylr, base = call(
        partial(local_mix, False),
        "mix_reverse",
        [(ANY, cs), (V, dt), (V, cum), (ANY, hc), (ANY, ylf), (V, dsk)],
        [shape(T, E, dtype=BF), shape(T, E)],
        [vm(T, C), half, half, full] + mix_scratch,
        flops=mix_cost,
        apart=(0, 1),
    )
    got, ylr, base = together(got, ylr, base)
    fore = exchange(scan(got, "scan_states"))
    gate, dn = call(
        gate_products,
        "gate_products",
        [(V, u), (V, dout), (ANY, rest)],
        [shape(T, E)] * 2,
        [vm(2, D, D, dtype=BF), vm(E, D, dtype=BF), dma((24,))],
        flops=4 * T * D * E,
    )
    n16, dg16, dm16, dgout, pay_back = call(
        gated_norm,
        "gated_norm",
        [(S, cont), (V, cum), (V, fore), (V, gout), (V, hc)]
        + [(ANY, a) for a in (cs, base, gate, dn)],
        [shape(T, E, dtype=BF)] * 3 + [shape(1, E), shape(SEQ, 48, 384, dtype=BF)],
        [vm(T, 256)] + [full] * 6 + [half] * 3 + [state] * 2
        + [dma(()), dma((3, WIDE)), dma((3, WIDE))],
        flops=12 * T * N * E,
        apart=(0, 1, 2),
    )
    got = exchange(pay_back)
    out, rows, dc, rest_keep, rest_send = call(
        out_and_rows,
        "out_and_rows",
        [(S, ids), (S, cont)]
        + [(V, a) for a in (tok, u, dout, n16, dg16, dm16, cum, fore, hc, hr)]
        + [(ANY, a) for a in (rest, cs, ylf, ylr)],
        [shape(T, D, dtype=BF), shape(T, 128), shape(T, 128)] + [shape(4, 384, D, dtype=BF)] * 2,
        [vm(E, D, dtype=BF), vm(E, T, dtype=BF), vm(D, T, dtype=BF), vm(E, D, dtype=BF)]
        + [vm(D, E, dtype=BF), vm(T, 256), half, half, state, state]
        + [dma(()), dma((2, WIDE)), dma((8,)), dma((24,))],
        flops=8 * T * D * E,
        apart=(3, 4),
    )
    got, out, rows, rest_keep, rest_send = together(got, out, rows, rest_keep, rest_send)
    scanned = scan(got, "scan_adjoints")
    back = exchange(scanned)
    rest_parts = add_swapped(rest_keep, rest_send, "add_rest_cores", scanned)
    dm16, *rest_parts = together(dm16, *rest_parts)
    half_up = lax.ppermute(rest_parts[2][:192], "dp", shift_y(1))
    half_down = lax.ppermute(rest_parts[2][192:], "dp", shift_y(3))
    zf, zr, dgf, dgr = call(
        local_back,
        "local_back",
        [(V, dt), (V, cum), (V, dm16), (V, hc), (ANY, cs)],
        [shape(T, E, dtype=BF)] * 2 + [shape(T, T)] * 2,
        [vm(T, C), half, half, vm(2 * H, T, 128), vm(128, T), vm(T, T), vm(T, T)]
        + [vm(E, T, dtype=BF), dma((1, WIDE + 1)), dma((2, WIDE))],
        flops=4 * 48 * T * T * 256,
        apart=(0, 1),
    )
    back, zf, half_up, half_down = together(back, zf, half_up, half_down)
    up, down = call(
        add_middle,
        "add_rest_middle",
        [(V, rest_parts[1]), (V, half_up), (V, rest_parts[3]), (V, half_down)],
        [shape(384, D, dtype=BF)] * 2,
        limit=SMALL,
    )
    zf, up, down = together(zf, up, down)
    rest_parts = [
        rest_parts[0], lax.ppermute(up, "dp", shift_y(1)), lax.ppermute(down, "dp", shift_y(3))
    ]
    dtok, dhalo, dall, small = call(
        inner_back,
        "inner_back",
        [(S, ids), (S, cont)]
        + [(V, a) for a in (tok, halo, gin, conv_w, alog, dsk, sraw, dt, cum, u, dout, dgf, dgr)]
        + [(V, a) for a in (back, fore, rows, dc, dgout, hc, hr)]
        + [(ANY, a) for a in (cs, zf, zr, dm16, ci, dg16, rest)]
        + part_ins,
        [shape(T, D), shape(HALO, D), shape(HALO + T, CD, dtype=BF), shape(96, 128, dtype=BF)],
        [vm(T, C), half, half, half, vm(HALO + T, C, dtype=BF), half, w_scratch]
        + [vm(2, D, D, dtype=BF)]
        + [state] * 4
        + [vm(C // 128, HALO + T + 16, 128), vm(HALO + T, 128), vm(HALO + T, D), vm(96, 128)]
        + [vm(8, E), dma((4, WIDE)), dma((2,)), dma((8,)), dma((16,)), dma(())],
        flops=2 * T * D * (CD + E),
    )
    dall, *rest_parts = together(dall, *rest_parts)
    keep, send = call(
        weight_back,
        "weight_back",
        [(S, ids), (V, u), (V, dall), (V, small)],
        [shape(4, 96, 2048, dtype=BF)] * 2,
        [vm(D, HALO + T, dtype=BF), w_scratch, dma((8,)), dma((8,))],
        flops=2 * T * D * CD,
        apart=(0, 1),
    )
    tail_parts = over_y(add_swapped(keep, send, "add_tail_cores"))
    dback = lax.ppermute(dhalo, "seq", [(i + 1, i) for i in range(SEQ - 1)])
    dtok = dtok.at[-HALO:].add(dback)
    *tail_parts, dtok = together(*tail_parts, dtok)
    slices = shape(SEQ, 240, 128, dtype=BF)
    sums = [(V, part) for part in (*rest_parts, *tail_parts)]
    sums = call(add_y, "add_y", sums, [slices], limit=SMALL)[0]
    sums = call(add_blocks, "add_seq", [(V, exchange(sums))], [slices], limit=SMALL)[0]
    dwin, dwdt, dwout, dcw, dcb, dgo, dgi, ddtb, dal, dds = call(
        finish,
        "finish",
        [(V, exchange(sums))],
        [shape(96, E + C), shape(96, 2 * H), shape(192, D), shape(4, C), shape(C)]
        + [shape(E), shape(D), shape(2 * H), shape(H), shape(H)],
        limit=SMALL,
    )
    return (
        out[None], dtok[None], dgi, dwin, dwdt, dcw, dcb, ddtb, dal, dds, dgo, dwout,
    )


def solution(mesh):
    split = P("dp", "seq", None)
    rows = P("dp", None)
    return jax.shard_map(
        local,
        mesh=mesh,
        in_specs=(split, P("dp", "seq"), P(), rows, rows, P(), P(), P(), P(), P(), P(), rows, split),
        out_specs=(split, split, P(), rows, rows, P(), P(), P(), P(), P(), P(), rows),
        check_vma=False,
    )
```

time: 315 us -> 241 us (0.77)
  waiting for transfers between devices: 80 us -> 26.3 us
  Pallas kernels: 121 us -> 90.7 us
  blocking collectives: 19.7 us -> 40.2 us
  starting transfers between devices: 53.6 us -> 47.6 us
  local copies, waits for them, and re-layouts: 17.8 us -> 12.8 us
    ppermute x13 -> x14, waiting for transfers between devices: 40.9 us -> 14.2 us  [the longest x3 10.2 us: over_y(): lax.ppermute(parts[k], 'dp', shift_y(k))]
    all_to_all x7 -> x4, waiting for transfers between devices: 29.2 us -> 3.73 us  [exchange(): return lax.all_to_all(value, 'seq', 0, 0, tiled=True)]
    pallas_call x14 -> x17, Pallas kernels: 113 us -> 90.7 us  [call(): pl.pallas_call(kernel, name=name, out_shape=tuple(outs), in_specs=list(sp...]
    all_to_all x1 -> x2, blocking collectives: 19.7 us -> 40.2 us  [exchange(): return lax.all_to_all(value, 'seq', 0, 0, tiled=True)]
    all_to_all x7 -> x4, starting transfers between devices: 35.7 us -> 26.1 us  [exchange(): return lax.all_to_all(value, 'seq', 0, 0, tiled=True)]
    pallas_call x2 -> x0, Pallas kernels: 8.27 us -> none  [add_swapped(): pl.pallas_call(add_pairs, name=name, grid=(3,), out_shape=tuple((shape(ro...]
    ppermute x13 -> x14, starting transfers between devices: 12.1 us -> 16.2 us  [the longest x3 5.98 us: local(): column = [lax.ppermute(own, 'dp', shift_y(k)) for k in (1, 2, 3)]]
    unnamed x71 -> x46, local copies, waits for them, and re-layouts: 10.8 us -> 6.86 us
  transfers between devices with their start and end apart: 25 -> 23, of which waited for: 12 -> 10; matrix products, arithmetic and copies ran while one was open for 2% -> 4% of each run, Pallas kernels for 32% -> 31%
where the time goes in v2:
time: 241 us; the launch traced here: 238 us
  Pallas kernels  90.7 us (38%)
  starting transfers between devices  47.6 us (20%)
  blocking collectives  40.2 us (17%)
  waiting for transfers between devices  26.3 us (11%)
  between operations  15.2 us (6%)
  local copies, waits for them, and re-layouts  12.8 us (5%)
  other arithmetic  5.04 us (2%)
    pallas_call x17, Pallas kernels, call(): pl.pallas_call(kernel, name=name, out_shape=tuple(outs), in_specs=list(sp...  90.7 us
    all_to_all x2, blocking collectives, exchange(): return lax.all_to_all(value, 'seq', 0, 0, tiled=True)  40.2 us
    all_to_all x4, starting transfers between devices, exchange(): return lax.all_to_all(value, 'seq', 0, 0, tiled=True)  26.1 us
    ppermute x3, waiting for transfers between devices, over_y(): lax.ppermute(parts[k], 'dp', shift_y(k))  10.2 us
    unnamed x46, local copies, waits for them, and re-layouts  6.86 us
    ppermute x3, starting transfers between devices, local(): column = [lax.ppermute(own, 'dp', shift_y(k)) for k in (1, 2, 3)]  5.98 us
  transfers between devices with their start and end apart: 23, of which 10 were waited for; matrix products, arithmetic and copies ran while one was open for 4% of the time, Pallas kernels for 31%

profile of v2, /device:TPU:0, one launch (start us, length us, event | category | flops | bytes accessed | tf_op | source)
XLA Modules:
  0.0 237.8 jit_solution(7431521005368362978)
XLA Ops:
  9.2 1.7 collective-permute-start
  10.9 2.9 %collective-permute-start.1 = (bf16[96,1920]{1,0:T(8,128)(2,1)S(1)}, bf16[96,1920]{1,0:T(8,128)(2,1)S(1)}, u32[]{:S(2)}, u32[]{:S(2)}) collective-permute-start(bf16[96,1920]{1,0:T(8,128)(2,1)S(1)} %fusion.1.refs_0_), channel_id=1, source_target_pairs={{0,64},{16,80},{32,96},{48,112},{64,0},{80,16},{96,32},{112,48},{1... | collective-permute-start | bytes 1105928 | tf_op jit(solution)/shard_map/ppermute | solution.py:878
  13.8 1.3 collective-permute-start.2
  15.9 3.8 %collective-permute-start.3 = (bf16[16,768]{1,0:T(8,128)(2,1)S(1)}, bf16[16,768]{1,0:T(8,128)(2,1)S(1)}, u32[]{:S(2)}, u32[]{:S(2)}) collective-permute-start(bf16[16,768]{1,0:T(8,128)(2,1)S(1)} %slice_bitcast_fusion), channel_id=1, source_target_pairs={{0,1},{1,2},{2,3},{3,4},{4,5},{5,6},{6,7},{7,8},{8,9},{9,10},{10,1... | collective-permute-start | bytes 73736 | tf_op jit(solution)/shard_map/ppermute | solution.py:879
  27.5 2.5 %collective-permute-done.1.refs_2_ = bf16[96,1920]{1,0:T(8,128)(2,1)S(1)} collective-permute-done((bf16[96,1920]{1,0:T(8,128)(2,1)S(1)}, bf16[96,1920]{1,0:T(8,128)(2,1)S(1)}, u32[]{:S(2)}, u32[]{:S(2)}) %collective-permute-start.1) | collective-permute-done | bytes 368672 | tf_op jit(solution)/shard_map/ppermute | solution.py:878
  33.6 11.3 %front.1 = (bf16[272,768]{1,0:T(8,128)(2,1)}, bf16[272,1792]{1,0:T(8,128)(2,1)}, f32[256,1792]{1,0:T(8,128)}, f32[256,128]{1,0:T(8,128)}, f32[256,128]{1,0:T(8,1...) custom-call(s32[16]{0:T(128)} %stack.61.ids, f32[1]{0:T(128)} %bitcast.cont, bf16[256,768]{1,0:T(8,128)(2,1)} %bitcast.25, ...), custom_call_target="tpu_custom_call" | custom-call | flops 754974720 | bytes 8404036 | tf_op jit(solution)/shard_map/front/pallas_call | solution.py:813
  44.9 7.9 %all-to-all-start = ((bf16[16,48,384]{2,1,0:T(8,128)(2,1)}), bf16[16,48,384]{2,1,0:T(8,128)(2,1)S(1)}, u32[]{:S(2)}, u32[]{:S(2)}) async-start(bf16[16,48,384]{2,1,0:T(8,128)(2,1)} %get-tuple-element.132), calls=%async_computation | async-start | bytes 1179648 | tf_op jit(solution)/shard_map/all_to_all | solution.py:839
  52.8 6.6 %mix_forward.1.refs_0_.ylf = bf16[256,1536]{1,0:T(8,128)(2,1)} custom-call(f32[256,1792]{1,0:T(8,128)} %get-tuple-element.133.cs, f32[256,128]{1,0:T(8,128)} %get-tuple-element.134.dt, f32[256,128]{1,0:T(8,128)} %get-tuple-element.131.cum, bf16[256,1536]{1,0:T(8,128)(2,1)} %select_convert_fusion.hc), custom_call_target="tpu_custom_call" | custom-call | flops 805306368 | bytes 3670016 | tf_op jit(solution)/shard_map/mix_forward/pallas_call | solution.py:813
  59.4 6.8 %mix_reverse.1 = (bf16[256,1536]{1,0:T(8,128)(2,1)}, f32[256,1536]{1,0:T(8,128)}) custom-call(f32[256,1792]{1,0:T(8,128)} %get-tuple-element.133.cs, f32[256,128]{1,0:T(8,128)} %get-tuple-element.134.dt, f32[256,128]{1,0:T(8,128)} %get-tuple-element.131.cum, bf16[256,1536]{1,0:T(8,128)(2,1)} %select_convert_fusion.hc, ...), custom_call_target="tpu_custom_call" | custom-call | flops 805306368 | bytes 6035456 | tf_op jit(solution)/shard_map/mix_reverse/pallas_call | solution.py:813
  67.1 7.2 %all-to-all-start.1 = ((bf16[16,32,384]{2,1,0:T(8,128)(2,1)}), bf16[16,32,384]{2,1,0:T(8,128)(2,1)S(1)}, u32[]{:S(2)}, u32[]{:S(2)}) async-start(bf16[16,32,384]{2,1,0:T(8,128)(2,1)} %scan_states.1), calls=%async_computation.1 | async-start | bytes 786432 | tf_op jit(solution)/shard_map/all_to_all | solution.py:839
  74.4 5.8 %gate_products.1 = (f32[256,1536]{1,0:T(8,128)}, f32[256,1536]{1,0:T(8,128)}) custom-call(bf16[272,768]{1,0:T(8,128)(2,1)} %get-tuple-element.141.u, bf16[256,768]{1,0:T(8,128)(2,1)} %bitcast.28, bf16[3072,768]{1,0:T(8,128)(2,1)} %all-gather.2.cloned.1.call-done.rest), custom_call_target="tpu_custom_call" | custom-call | flops 1207959552 | bytes 8675328 | tf_op jit(solution)/shard_map/gate_products/pallas_call | solution.py:813
  80.2 3.7 %all-to-all-done.1.recv.fore = bf16[16,32,384]{2,1,0:T(8,128)(2,1)S(1)} async-done(((bf16[16,32,384]{2,1,0:T(8,128)(2,1)}), bf16[16,32,384]{2,1,0:T(8,128)(2,1)S(1)}, u32[]{:S(2)}, u32[]{:S(2)}) %all-to-all-start.1) | async-done | bytes 393248 | tf_op jit(solution)/shard_map/all_to_all | solution.py:839
  84.7 10.3 %gated_norm.1 = (bf16[256,1536]{1,0:T(8,128)(2,1)}, bf16[256,1536]{1,0:T(8,128)(2,1)}, bf16[256,1536]{1,0:T(8,128)(2,1)}, f32[1,1536]{1,0:T(1,128)}, bf16[16,48,384]{2,1,0:T(8,128)(2,1)}) custom-call(f32[1]{0:T(128)} %bitcast.cont, f32[256,128]{1,0:T(8,128)} %get-tuple-element.131.cum, bf16[16,32,384]{2,1,0:T(8,128)(2,1)} %copy-done.4, ...), custom_call_target="tpu_custom_call" | custom-call | flops 301989888 | bytes 10825732 | tf_op jit(solution)/shard_map/gated_norm/pallas_call | solution.py:813
  95.0 3.8 %all-to-all-start.2 = ((bf16[16,48,384]{2,1,0:T(8,128)(2,1)}), bf16[16,48,384]{2,1,0:T(8,128)(2,1)S(1)}, u32[]{:S(2)}, u32[]{:S(2)}) async-start(bf16[16,48,384]{2,1,0:T(8,128)(2,1)} %get-tuple-element.145), calls=%async_computation.2 | async-start | bytes 1179648 | tf_op jit(solution)/shard_map/all_to_all | solution.py:839
  98.8 12.0 %out_and_rows.1 = (bf16[256,768]{1,0:T(8,128)(2,1)}, f32[256,128]{1,0:T(8,128)}, f32[256,128]{1,0:T(8,128)}, bf16[4,384,768]{2,1,0:T(8,128)(2,1)}, bf16[4,384,768]{2,1,0:T(8,128)(2,1)}) custom-call(s32[16]{0:T(128)} %stack.61.ids, f32[1]{0:T(128)} %bitcast.cont, bf16[256,768]{1,0:T(8,128)(2,1)} %bitcast.26, bf16[272,768]{1,0:T(8,128)(2,1)} %get-tuple-element.141.u, ...), custom_call_target="tpu_custom_call" | custom-call | flops 2415919104 | bytes 18767940 | tf_op jit(solution)/shard_map/out_and_rows/pallas_call | solution.py:813
  111.7 7.2 %all-to-all-start.3 = ((bf16[16,32,384]{2,1,0:T(8,128)(2,1)}), bf16[16,32,384]{2,1,0:T(8,128)(2,1)}, u32[]{:S(2)}, u32[]{:S(2)}) async-start(bf16[16,32,384]{2,1,0:T(8,128)(2,1)} %scan_adjoints.1), calls=%async_computation.3 | async-start | bytes 786432 | tf_op jit(solution)/shard_map/all_to_all | solution.py:839
  118.9 1.7 copy-done
  122.2 2.1 collective-permute-start.10
  124.3 11.7 %local_back.1 = (bf16[256,1536]{1,0:T(8,128)(2,1)}, bf16[256,1536]{1,0:T(8,128)(2,1)}, f32[256,256]{1,0:T(8,128)}, f32[256,256]{1,0:T(8,128)}) custom-call(f32[256,128]{1,0:T(8,128)} %get-tuple-element.134.dt, f32[256,128]{1,0:T(8,128)} %get-tuple-element.131.cum, bf16[256,1536]{1,0:T(8,128)(2,1)} %get-tuple-element.165.dm16, ...), custom_call_target="tpu_custom_call" | custom-call | flops 3221225472 | bytes 5767168 | tf_op jit(solution)/shard_map/local_back/pallas_call | solution.py:813
  137.3 2.5 %collective-permute-start.12 = (bf16[384,768]{1,0:T(8,128)(2,1)S(1)}, bf16[384,768]{1,0:T(8,128)(2,1)S(1)}, u32[]{:S(2)}, u32[]{:S(2)}) collective-permute-start(bf16[384,768]{1,0:T(8,128)(2,1)S(1)} %get-tuple-element.187), channel_id=1, source_target_pairs={{0,96},{16,112},{32,0},{48,16},{64,32},{80,48},{96,64},{112,80},{1... | collective-permute-start | bytes 1769480 | tf_op jit(solution)/shard_map/ppermute | solution.py:997
  139.8 15.9 %inner_back.1 = (f32[256,768]{1,0:T(8,128)}, f32[16,768]{1,0:T(8,128)}, bf16[272,1920]{1,0:T(8,128)(2,1)}, bf16[96,128]{1,0:T(8,128)(2,1)}) custom-call(s32[16]{0:T(128)} %stack.61.ids, f32[1]{0:T(128)} %bitcast.cont, bf16[256,768]{1,0:T(8,128)(2,1)} %bitcast.27, bf16[16,768]{1,0:T(8,128)(2,1)} %copy-done.14, f32[1,768]{1,0:T(1,128)} %reshape.70.gin, ...), custom_call_target="tpu_custom_call" | custom-call | flops 1358954496 | bytes 19947076 | tf_op jit(solution)/shard_map/inner_back/pallas_call | solution.py:813
  155.7 5.4 %weight_back.1 = (bf16[4,96,2048]{2,1,0:T(8,128)(2,1)}, bf16[4,96,2048]{2,1,0:T(8,128)(2,1)}) custom-call(s32[16]{0:T(128)} %stack.61.ids, bf16[272,768]{1,0:T(8,128)(2,1)} %get-tuple-element.141.u, bf16[272,1920]{1,0:T(8,128)(2,1)} %get-tuple-element.188.dall, bf16[96,128]{1,0:T(8,128)(2,1)} %get-tuple-element.189.small), custom_call_target="tpu_custom_call" | custom-call | flops 754974720 | bytes 4632640 | tf_op jit(solution)/shard_map/weight_back/pallas_call | solution.py:813
  161.2 3.6 %collective-permute-done.13.b = bf16[4,96,2048]{2,1,0:T(8,128)(2,1)S(1)} collective-permute-done((bf16[4,96,2048]{2,1,0:T(8,128)(2,1)}, bf16[4,96,2048]{2,1,0:T(8,128)(2,1)S(1)}, u32[]{:S(2)}, u32[]{:S(2)}) %collective-permute-start.13) | collective-permute-done | bytes 1572896 | tf_op jit(solution)/shard_map/ppermute | solution.py:843
  164.8 1.4 copy-done.1
  166.7 3.2 %collective-permute-start.15 = (bf16[96,2048]{1,0:T(8,128)(2,1)S(1)}, bf16[96,2048]{1,0:T(8,128)(2,1)S(1)}, u32[]{:S(2)}, u32[]{:S(2)}) collective-permute-start(bf16[96,2048]{1,0:T(8,128)(2,1)S(1)} %get-tuple-element.194), channel_id=1, source_target_pairs={{0,64},{16,80},{32,96},{48,112},{64,0},{80,16},{96,32},{112,48},{1... | collective-permute-start | bytes 1179656 | tf_op jit(solution)/shard_map/ppermute | solution.py:852
  171.8 4.7 %collective-permute-done.17 = f32[16,768]{1,0:T(8,128)S(1)} collective-permute-done((f32[16,768]{1,0:T(8,128)S(1)}, f32[16,768]{1,0:T(8,128)S(1)}, u32[]{:S(2)}, u32[]{:S(2)}) %collective-permute-start.17) | collective-permute-done | bytes 49184 | tf_op jit(solution)/shard_map/ppermute | solution.py:1026
  176.5 1.4 add_dynamic-update-slice_fusion
  177.9 2.0 collective-permute-done.14.refs_4_
  179.9 7.6 %collective-permute-done.15.refs_5_ = bf16[96,2048]{1,0:T(8,128)(2,1)S(1)} collective-permute-done((bf16[96,2048]{1,0:T(8,128)(2,1)S(1)}, bf16[96,2048]{1,0:T(8,128)(2,1)S(1)}, u32[]{:S(2)}, u32[]{:S(2)}) %collective-permute-start.15) | collective-permute-done | bytes 393248 | tf_op jit(solution)/shard_map/ppermute | solution.py:852
  188.6 22.6 %all_to_all.30.recv = bf16[16,240,128]{2,1,0:T(8,128)(2,1)S(1)} all-to-all(bf16[16,240,128]{2,1,0:T(8,128)(2,1)S(1)} %add_y.1), channel_id=1, replica_groups=mesh['dp'=8,'seq'=16] {'seq'}, dimensions={0} | all-to-all | bytes 1966080 | tf_op jit(solution)/shard_map/all_to_all | solution.py:839
  211.3 17.7 %all_to_all.31.sums = bf16[16,240,128]{2,1,0:T(8,128)(2,1)S(1)} all-to-all(bf16[16,240,128]{2,1,0:T(8,128)(2,1)S(1)} %add_seq.1), channel_id=1, replica_groups=mesh['dp'=8,'seq'=16] {'seq'}, dimensions={0} | all-to-all | bytes 1966080 | tf_op jit(solution)/shard_map/all_to_all | solution.py:839
  229.0 1.3 finish.1
  (98 shorter events, 23.1 us)
Async XLA Ops:
  7.2 15.7 %copy-start.13 = (bf16[192,768]{1,0:T(8,128)(2,1)S(1)}, bf16[192,768]{1,0:T(8,128)(2,1)}, u32[]{:S(2)}) copy-start(bf16[192,768]{1,0:T(8,128)(2,1)} %param.26) | copy-start | bytes 884740
  7.2 67.2 %all-gather.2.cloned.1.call-start = ((), (), s32[]{:S(2)}) async-start(), calls=%async_computation.6 | async-start | bytes 5308416 | tf_op jit(solution)/shard_map/all_gather | solution.py:887
  9.1 15.2 %copy-start.5 = (bf16[96,1920]{1,0:T(8,128)(2,1)}, bf16[96,1920]{1,0:T(8,128)(2,1)S(1)}, u32[]{:S(2)}) copy-start(bf16[96,1920]{1,0:T(8,128)(2,1)S(1)} %fusion.1.refs_0_) | copy-start | bytes 1105924
  9.1 14.6 %copy-start.19 = (f32[24]{0:T(128)S(1)}, f32[24]{0:T(128)}, u32[]{:S(2)}) copy-start(f32[24]{0:T(128)} %param.23) | copy-start | bytes 292
  9.1 14.6 %copy-start.20 = (f32[48]{0:T(128)S(1)}, f32[48]{0:T(128)}, u32[]{:S(2)}) copy-start(f32[48]{0:T(128)} %param.22) | copy-start | bytes 580
  9.2 18.3 %collective-permute-start = (bf16[96,1920]{1,0:T(8,128)(2,1)S(1)}, bf16[96,1920]{1,0:T(8,128)(2,1)S(1)}, u32[]{:S(2)}, u32[]{:S(2)}) collective-permute-start(bf16[96,1920]{1,0:T(8,128)(2,1)S(1)} %fusion.1.refs_0_), channel_id=1, source_target_pairs={{0,32},{16,48},{32,64},{48,80},{64,96},{80,112},{96,0},{112,16},{1... | collective-permute-start | bytes 1105928 | tf_op jit(solution)/shard_map/ppermute | solution.py:878
  10.9 19.1 %collective-permute-start.1 = (bf16[96,1920]{1,0:T(8,128)(2,1)S(1)}, bf16[96,1920]{1,0:T(8,128)(2,1)S(1)}, u32[]{:S(2)}, u32[]{:S(2)}) collective-permute-start(bf16[96,1920]{1,0:T(8,128)(2,1)S(1)} %fusion.1.refs_0_), channel_id=1, source_target_pairs={{0,64},{16,80},{32,96},{48,112},{64,0},{80,16},{96,32},{112,48},{1... | collective-permute-start | bytes 1105928 | tf_op jit(solution)/shard_map/ppermute | solution.py:878
  13.8 16.2 %collective-permute-start.2 = (bf16[96,1920]{1,0:T(8,128)(2,1)S(1)}, bf16[96,1920]{1,0:T(8,128)(2,1)S(1)}, u32[]{:S(2)}, u32[]{:S(2)}) collective-permute-start(bf16[96,1920]{1,0:T(8,128)(2,1)S(1)} %fusion.1.refs_0_), channel_id=1, source_target_pairs={{0,96},{16,112},{32,0},{48,16},{64,32},{80,48},{96,64},{112,80},{1... | collective-permute-start | bytes 1105928 | tf_op jit(solution)/shard_map/ppermute | solution.py:878
  15.1 14.9 %collective-permute-start.4 = (bf16[96,1920]{1,0:T(8,128)(2,1)S(1)}, bf16[96,1920]{1,0:T(8,128)(2,1)S(1)}, u32[]{:S(2)}, u32[]{:S(2)}) collective-permute-start(bf16[96,1920]{1,0:T(8,128)(2,1)S(1)} %fusion.1.refs_0_), channel_id=1, source_target_pairs={{0,16},{16,0},{32,48},{48,32},{64,80},{80,64},{96,112},{112,96},{1... | collective-permute-start | bytes 1105928 | tf_op jit(solution)/shard_map/ppermute | solution.py:880
  15.9 11.6 %collective-permute-start.3 = (bf16[16,768]{1,0:T(8,128)(2,1)S(1)}, bf16[16,768]{1,0:T(8,128)(2,1)S(1)}, u32[]{:S(2)}, u32[]{:S(2)}) collective-permute-start(bf16[16,768]{1,0:T(8,128)(2,1)S(1)} %slice_bitcast_fusion), channel_id=1, source_target_pairs={{0,1},{1,2},{2,3},{3,4},{4,5},{5,6},{6,7},{7,8},{8,9},{9,10},{10,1... | collective-permute-start | bytes 73736 | tf_op jit(solution)/shard_map/ppermute | solution.py:879
  19.7 5.4 %copy-start.16 = (f32[1792]{0:T(1024)S(1)}, f32[1792]{0:T(1024)}, u32[]{:S(2)}) copy-start(f32[1792]{0:T(1024)} %param.21) | copy-start | bytes 21508
  19.7 6.0 %copy-start.15 = (f32[1536]{0:T(1024)S(1)}, f32[1536]{0:T(1024)}, u32[]{:S(2)}) copy-start(f32[1536]{0:T(1024)} %param.25) | copy-start | bytes 18436
  19.8 6.6 %copy-start.17 = (f32[768]{0:T(1024)S(1)}, f32[768]{0:T(1024)}, u32[]{:S(2)}) copy-start(f32[768]{0:T(1024)} %param.17) | copy-start | bytes 9220
  27.5 5.4 %copy-start.14 = (bf16[16,768]{1,0:T(8,128)(2,1)}, bf16[16,768]{1,0:T(8,128)(2,1)S(1)}, u32[]{:S(2)}) copy-start(bf16[16,768]{1,0:T(8,128)(2,1)S(1)} %collective-permute-done.3.halo) | copy-start | bytes 73732
  30.0 1.8 collective-permute-start.5
  30.1 2.2 collective-permute-start.6
  30.6 2.2 collective-permute-start.7
  44.9 21.3 %all-to-all-start = ((bf16[16,48,384]{2,1,0:T(8,128)(2,1)}), bf16[16,48,384]{2,1,0:T(8,128)(2,1)S(1)}, u32[]{:S(2)}, u32[]{:S(2)}) async-start(bf16[16,48,384]{2,1,0:T(8,128)(2,1)} %get-tuple-element.132), calls=%async_computation | async-start | bytes 1179648 | tf_op jit(solution)/shard_map/all_to_all | solution.py:839
  67.1 16.8 %all-to-all-start.1 = ((bf16[16,32,384]{2,1,0:T(8,128)(2,1)}), bf16[16,32,384]{2,1,0:T(8,128)(2,1)S(1)}, u32[]{:S(2)}, u32[]{:S(2)}) async-start(bf16[16,32,384]{2,1,0:T(8,128)(2,1)} %scan_states.1), calls=%async_computation.1 | async-start | bytes 786432 | tf_op jit(solution)/shard_map/all_to_all | solution.py:839
  95.0 15.8 %all-to-all-start.2 = ((bf16[16,48,384]{2,1,0:T(8,128)(2,1)}), bf16[16,48,384]{2,1,0:T(8,128)(2,1)S(1)}, u32[]{:S(2)}, u32[]{:S(2)}) async-start(bf16[16,48,384]{2,1,0:T(8,128)(2,1)} %get-tuple-element.145), calls=%async_computation.2 | async-start | bytes 1179648 | tf_op jit(solution)/shard_map/all_to_all | solution.py:839
  110.8 8.2 %collective-permute-start.8 = (bf16[4,384,768]{2,1,0:T(8,128)(2,1)}, bf16[4,384,768]{2,1,0:T(8,128)(2,1)S(1)}, u32[]{:S(2)}, u32[]{:S(2)}) collective-permute-start(bf16[4,384,768]{2,1,0:T(8,128)(2,1)} %get-tuple-element.158), channel_id=1, source_target_pairs={{0,16},{16,0},{32,48},{48,32},{64,80},{80,64},{96,112},{112,96},{1... | collective-permute-start | bytes 7077896 | tf_op jit(solution)/shard_map/ppermute | solution.py:843
  111.7 24.3 %all-to-all-start.3 = ((bf16[16,32,384]{2,1,0:T(8,128)(2,1)}), bf16[16,32,384]{2,1,0:T(8,128)(2,1)}, u32[]{:S(2)}, u32[]{:S(2)}) async-start(bf16[16,32,384]{2,1,0:T(8,128)(2,1)} %scan_adjoints.1), calls=%async_computation.3 | async-start | bytes 786432 | tf_op jit(solution)/shard_map/all_to_all | solution.py:839
  122.2 13.9 %collective-permute-start.10 = (bf16[192,768]{1,0:T(8,128)(2,1)S(1)}, bf16[192,768]{1,0:T(8,128)(2,1)S(1)}, u32[]{:S(2)}, u32[]{:S(2)}) collective-permute-start(bf16[192,768]{1,0:T(8,128)(2,1)S(1)} %get-tuple-element.230), channel_id=1, source_target_pairs={{0,96},{16,112},{32,0},{48,16},{64,32},{80,48},{96,64},{112,80},{1... | collective-permute-start | bytes 884744 | tf_op jit(solution)/shard_map/ppermute | solution.py:976
  124.3 11.8 %collective-permute-start.9 = (bf16[192,768]{1,0:T(8,128)(2,1)S(1)}, bf16[192,768]{1,0:T(8,128)(2,1)S(1)}, u32[]{:S(2)}, u32[]{:S(2)}) collective-permute-start(bf16[192,768]{1,0:T(8,128)(2,1)S(1)} %get-tuple-element.231), channel_id=1, source_target_pairs={{0,32},{16,48},{32,64},{48,80},{64,96},{80,112},{96,0},{112,16},{1... | collective-permute-start | bytes 884744 | tf_op jit(solution)/shard_map/ppermute | solution.py:975
  136.2 19.5 %collective-permute-start.11 = (bf16[384,768]{1,0:T(8,128)(2,1)S(1)}, bf16[384,768]{1,0:T(8,128)(2,1)S(1)}, u32[]{:S(2)}, u32[]{:S(2)}) collective-permute-start(bf16[384,768]{1,0:T(8,128)(2,1)S(1)} %get-tuple-element.186), channel_id=1, source_target_pairs={{0,32},{16,48},{32,64},{48,80},{64,96},{80,112},{96,0},{112,16},{1... | collective-permute-start | bytes 1769480 | tf_op jit(solution)/shard_map/ppermute | solution.py:997
  137.3 18.4 %collective-permute-start.12 = (bf16[384,768]{1,0:T(8,128)(2,1)S(1)}, bf16[384,768]{1,0:T(8,128)(2,1)S(1)}, u32[]{:S(2)}, u32[]{:S(2)}) collective-permute-start(bf16[384,768]{1,0:T(8,128)(2,1)S(1)} %get-tuple-element.187), channel_id=1, source_target_pairs={{0,96},{16,112},{32,0},{48,16},{64,32},{80,48},{96,64},{112,80},{1... | collective-permute-start | bytes 1769480 | tf_op jit(solution)/shard_map/ppermute | solution.py:997
  161.1 3.7 %collective-permute-start.13 = (bf16[4,96,2048]{2,1,0:T(8,128)(2,1)}, bf16[4,96,2048]{2,1,0:T(8,128)(2,1)S(1)}, u32[]{:S(2)}, u32[]{:S(2)}) collective-permute-start(bf16[4,96,2048]{2,1,0:T(8,128)(2,1)} %get-tuple-element.191), channel_id=1, source_target_pairs={{0,16},{16,0},{32,48},{48,32},{64,80},{80,64},{96,112},{112,96},{1... | collective-permute-start | bytes 4718600 | tf_op jit(solution)/shard_map/ppermute | solution.py:843
  166.2 21.9 %copy-start.3 = (bf16[384,768]{1,0:T(8,128)(2,1)S(1)}, bf16[384,768]{1,0:T(8,128)(2,1)}, u32[]{:S(2)}) copy-start(bf16[384,768]{1,0:T(8,128)(2,1)} %copy-done.2) | copy-start | bytes 1769476
  166.7 13.2 %collective-permute-start.14 = (bf16[96,2048]{1,0:T(8,128)(2,1)S(1)}, bf16[96,2048]{1,0:T(8,128)(2,1)S(1)}, u32[]{:S(2)}, u32[]{:S(2)}) collective-permute-start(bf16[96,2048]{1,0:T(8,128)(2,1)S(1)} %get-tuple-element.193), channel_id=1, source_target_pairs={{0,32},{16,48},{32,64},{48,80},{64,96},{80,112},{96,0},{112,16},{1... | collective-permute-start | bytes 1179656 | tf_op jit(solution)/shard_map/ppermute | solution.py:852
  166.7 20.8 %collective-permute-start.15 = (bf16[96,2048]{1,0:T(8,128)(2,1)S(1)}, bf16[96,2048]{1,0:T(8,128)(2,1)S(1)}, u32[]{:S(2)}, u32[]{:S(2)}) collective-permute-start(bf16[96,2048]{1,0:T(8,128)(2,1)S(1)} %get-tuple-element.194), channel_id=1, source_target_pairs={{0,64},{16,80},{32,96},{48,112},{64,0},{80,16},{96,32},{112,48},{1... | collective-permute-start | bytes 1179656 | tf_op jit(solution)/shard_map/ppermute | solution.py:852
  169.9 18.2 %collective-permute-start.16 = (bf16[96,2048]{1,0:T(8,128)(2,1)S(1)}, bf16[96,2048]{1,0:T(8,128)(2,1)S(1)}, u32[]{:S(2)}, u32[]{:S(2)}) collective-permute-start(bf16[96,2048]{1,0:T(8,128)(2,1)S(1)} %get-tuple-element.195), channel_id=1, source_target_pairs={{0,96},{16,112},{32,0},{48,16},{64,32},{80,48},{96,64},{112,80},{1... | collective-permute-start | bytes 1179656 | tf_op jit(solution)/shard_map/ppermute | solution.py:852
  170.5 6.0 %collective-permute-start.17 = (f32[16,768]{1,0:T(8,128)S(1)}, f32[16,768]{1,0:T(8,128)S(1)}, u32[]{:S(2)}, u32[]{:S(2)}) collective-permute-start(f32[16,768]{1,0:T(8,128)S(1)} %copy-done.21), channel_id=1, source_target_pairs={{1,0},{2,1},{3,2},{4,3},{5,4},{6,5},{7,6},{8,7},{9,8},{10,9},{11,1... | collective-permute-start | bytes 147464 | tf_op jit(solution)/shard_map/ppermute | solution.py:1026
  (13 other events, 30.2 us)
Sparse Core Ops, SparseCore 0:
  30.2 36.0 all-gather.1

commit v3 on v2

--- a/solution.py
+++ b/solution.py
@@ -16,6 +16,7 @@
 HALO = 16
 WIDE = E // 256
 DP, SEQ = 8, 16
+HALF = 21
 VMEM = 56 * 1024 * 1024
 SMALL = 12 * 1024 * 1024
 
@@ -49,16 +50,13 @@
     return hi, (v - hi.astype(F32)).astype(BF)
 
 
-def pair(v):
-    return jnp.concatenate(split2(v), axis=1)
-
-
 def onehot(cond):
     return jnp.where(cond, 1.0, 0.0).astype(BF)
 
 
 def marks():
-    columns = onehot((iota((256, E), 0) & 127) == (iota((256, E), 1) >> 6))
+    row, head = iota((64, E), 0), iota((64, E), 1) >> 6
+    columns = onehot((row == head) | (row == head + H))
     return columns, onehot((iota((E, 128), 0) >> 6) == iota((E, 128), 1))
 
 
@@ -71,7 +69,18 @@
 
 
 def pairs_of(v):
-    return pair(v), pair(to_front(v))
+    def terms(v):
+        hi = v.astype(BF).astype(F32)
+        lane = lanes(v.shape[0])
+        both = jnp.where(lane < H, hi, jnp.where(lane < 2 * H, to_back(v - hi), 0.0))
+        return both[:, :64].astype(BF)
+
+    return terms(v), terms(to_front(v))
+
+
+def head_sum(v, marks):
+    hi, lo = split2(v)
+    return mm(hi, marks) + mm(lo, marks)
 
 
 def tri_sum(mask, v):
@@ -147,19 +156,20 @@
         second[rows, at] = recv[j, 16:32]
 
 
-def load_weights(ids, parts, w, sem):
+def load_weights(ids, parts, w, sem, start=True):
     copies = [
         pltpu.make_async_copy(
             parts[k], w.at[pl.ds(pl.multiple_of(ids[k] * 96, 32), 96)], sem.at[k]
         )
         for k in range(8)
     ]
-    for copy in copies:
-        copy.start()
+    if start:
+        for copy in copies:
+            copy.start()
     return copies
 
 
-def load_rest(rest, wg, wo, sem):
+def load_rest(rest, wg, wo, sem, start=True):
     gates, outs = [], []
     for p in range(DP):
         at = 384 * p
@@ -169,8 +179,9 @@
         if wo is not None:
             outs.append((rest.at[pl.ds(at + 192, 192)], wo.at[pl.ds(192 * p, 192)]))
     copies = [pltpu.make_async_copy(a, b, sem.at[k]) for k, (a, b) in enumerate(gates + outs)]
-    for copy in copies:
-        copy.start()
+    if start:
+        for copy in copies:
+            copy.start()
     return copies[: len(gates)], copies[len(gates) :]
 
 
@@ -180,16 +191,18 @@
 
 
 def front(ids, cont, tok, halo, gin, cw, cb, dtb, alog, hc, *refs):
-    parts, outs, (w, cif, csv, civ, sem, osem) = refs[:8], refs[8:15], refs[15:]
+    parts, outs, (w, cif, csv, civ, uv, sem, osem, usem) = refs[:8], refs[8:15], refs[15:]
     u_out, ci_out, cs_out, sraw_out, dt_out, cum_out, pay = outs
     copies = load_weights(ids, parts, w, sem)
     x = jnp.concatenate([halo[...], tok[...]], axis=0).astype(F32)
     u = x * lax.rsqrt(jnp.mean(x * x, axis=1, keepdims=True) + EPS) * gin[...]
-    u_out[...] = u.astype(BF)
+    uv[...] = u.astype(BF)
+    u_copy = pltpu.make_async_copy(uv, u_out, usem)
+    u_copy.start()
     keep = cont[0]
     mask = jnp.where(iota((HALO + T, 1), 0) < HALO, keep, 1.0)
     finish_all(copies)
-    sraw = mm(u_out[HALO:, :], w[:, C:]) + dtb[...]
+    sraw = mm(uv[HALO:, :], w[:, C:]) + dtb[...]
     sraw_out[...] = sraw
     dt = jnp.maximum(sraw, 0.0) + jnp.log1p(jnp.exp(-jnp.abs(sraw)))
     dt = jnp.where(lanes() < 2 * H, dt, 0.0)
@@ -215,7 +228,7 @@
 
     def convolve(i):
         at = wide(i)
-        ci = (mm(u_out[...], w[:, at]) * mask).astype(BF)
+        ci = (mm(uv[...], w[:, at]) * mask).astype(BF)
         civ[:, at] = ci
         for e in range(2):
             here = pl.ds(pl.multiple_of(i * 256 + 128 * e, 128), 128)
@@ -240,6 +253,7 @@
         return 0
 
     lax.fori_loop(0, WIDE, tile, 0)
+    u_copy.wait()
     for i in range(WIDE + 1):
         finish_all(outward(i))
 
@@ -277,55 +291,49 @@
     return jnp.concatenate([left, right], axis=1)
 
 
-def local_mix(forward, cs, dt, cum, hc, *refs):
-    if forward:
-        y, csv, ysv, hcv, col, row, g, sem, osem = refs
-    else:
-        ylf, dsk, y, base_out, csv, ysv, yfv, bsv, hcv, col, row, g, sem, osem = refs
-    hc_copy = pltpu.make_async_copy(hc, hcv, sem.at[2, 1])
-    hc_copy.start()
-    first = 0 if forward else H
-    bc = pltpu.make_async_copy(cs.at[:, E:], csv.at[:, E:], sem.at[2, 0])
+def local_mix(dt, cum, dsk, hc, cs, ylf, ylr, base, *scratch):
+    csv, yfv, yrv, bsv, col, row, gf, gr, bsem, sem, osem = scratch
+    bc = pltpu.make_async_copy(cs.at[:, E:], csv.at[:, E:], bsem)
     bc.start()
-    wait = fetch([(cs, csv)] if forward else [(cs, csv), (ylf, yfv)], sem)
+    wait = fetch([(cs, csv)], sem)
     cum2 = cum[...] * LOG2E
     row[...] = cum2.T
-    columns_of(cum2, col, first)
-    dt2 = pairs_of(dt[...])[0 if forward else 1]
+    columns_of(cum2, col)
+    dt_f, dt_r = pairs_of(dt[...])
     bc.wait()
-    parts = parts_of_bc(silu(csv[:, E:]))
-    b, cc = parts[:2] if forward else parts[2:]
+    bf, cf, br, cr = parts_of_bc(silu(csv[:, E:]))
     r, c = iota((T, T), 0), iota((T, T), 1)
-    g[...] = jnp.where(r > c if forward else r < c, mm_nt(cc, b), 0.0)
-    hc_copy.wait()
-
-    def weights(h):
-        at, along = col[h], row[pl.ds(first + h, 1), :]
+    gf[...] = jnp.where(r > c, mm_nt(cf, bf), 0.0)
+    gr[...] = jnp.where(r < c, mm_nt(cr, br), 0.0)
+
+    def weights(h, forward):
+        at, along = col[h], row[pl.ds(h, 1), :]
         if forward:
-            left = jnp.exp2(jnp.minimum(at - along[:, :128], 0.0)) * g[:, :128]
-            right = jnp.exp2(jnp.minimum(at[128:] - along[:, 128:], 0.0)) * g[128:, 128:]
+            left = jnp.exp2(jnp.minimum(at - along[:, :128], 0.0)) * gf[:, :128]
+            right = jnp.exp2(jnp.minimum(at[128:] - along[:, 128:], 0.0)) * gf[128:, 128:]
             return low_full(left.astype(BF), right.astype(BF))
-        left = jnp.exp2(jnp.minimum(at[:128] - along[:, :128], 0.0)) * g[:128, :128]
-        right = jnp.exp2(jnp.minimum(at - along[:, 128:], 0.0)) * g[:, 128:]
+        left = jnp.exp2(jnp.minimum(at[:128] - along[:, :128], 0.0)) * gr[:128, :128]
+        right = jnp.exp2(jnp.minimum(at - along[:, 128:], 0.0)) * gr[:, 128:]
         return up_full(left.astype(BF), right.astype(BF))
 
     def outward(i):
-        pairs = [(ysv, y)] if forward else [(ysv, y), (bsv, base_out)]
         return [
             pltpu.make_async_copy(a.at[:, wide(i)], b.at[:, wide(i)], osem.at[k, i])
-            for k, (a, b) in enumerate(pairs)
+            for k, (a, b) in enumerate([(yfv, ylf), (yrv, ylr), (bsv, base)])
         ]
 
     def tile(i, _):
         at = wide(i)
         wait(i)
         x = silu(csv[:, at])
-        xs = by_head(x * mm(dt2, hcv[:, at]))
-        left = jnp.concatenate([weights(4 * i + e) for e in range(4)], axis=1)
-        own = mm(left, jnp.concatenate(xs, axis=0))
-        ysv[:, at] = own.astype(BF)
-        if not forward:
-            bsv[:, at] = own + yfv[:, at].astype(F32) + dsk[:, at] * x
+        total = dsk[:, at] * x
+        for forward, first, dt2, y in ((True, 0, dt_f, yfv), (False, H, dt_r, yrv)):
+            xs = by_head(x * mm(dt2, hc[:, at]))
+            left = jnp.concatenate([weights(first + 4 * i + e, forward) for e in range(4)], axis=1)
+            own = mm(left, jnp.concatenate(xs, axis=0))
+            y[:, at] = own
+            total = total + own
+        bsv[:, at] = total
         for copy in outward(i):
             copy.start()
         return 0
@@ -335,18 +343,27 @@
         finish_all(outward(i))
 
 
-def gate_products(u, dout, rest, gate, dn, wg, wo, sem):
+def gate_products(u, dout, rest, gate, dn, wg, wo, gv, dv, sem, osem):
     gates, outs = load_rest(rest, wg, wo, sem)
+    copies = []
+
+    def put(k, value, src, dst, at):
+        src[:, at] = value.astype(BF)
+        copies.append(pltpu.make_async_copy(src.at[:, at], dst.at[:, at], osem.at[k]))
+        copies[-1].start()
+
     finish_all(gates)
-    gate[:, :D] = mm(u[HALO:, :], wg[0])
-    gate[:, D:] = mm(u[HALO:, :], wg[1])
+    put(0, mm(u[HALO:, :], wg[0]), gv, gate, slice(0, D))
+    put(1, mm(u[HALO:, :], wg[1]), gv, gate, slice(D, E))
     finish_all(outs)
-    dn[...] = mm_nt(dout[...], wo[...])
+    put(2, mm_nt(dout[...], wo[:D]), dv, dn, slice(0, D))
+    put(3, mm_nt(dout[...], wo[D:]), dv, dn, slice(D, E))
+    finish_all(copies)
 
 
 def gated_norm(cont, cum, recv, gout, hc, cs, base, gate, dn, *refs):
     (n16, dg16, dm16, dgout, pay), scratch = refs[:5], refs[5:]
-    bcv, yv, gv, dv, gds, eff, efr, nv, dgv, dmv, sf, sr, bsem, sem, osem = scratch
+    bcv, yv, gv, dv, gds, sls, eff, efr, nv, dgv, dmv, sf, sr, bsem, sem, osem = scratch
     bc = pltpu.make_async_copy(cs.at[:, E:], bcv, bsem)
     bc.start()
     wait = fetch([(base, yv), (gate, gv), (dn, dv)], sem)
@@ -366,14 +383,14 @@
         eff[:, at] = ef
         efr[:, at] = er
         m = yv[:, at] + ef * mm(cf, sf[:, at]) + er * mm(cr, sr[:, at])
-        g = gv[:, at]
+        g = gv[:, at].astype(F32)
         sg = sigmoid(g)
         sl = g * sg
         gd = m * sl
         gds[:, at] = gd
-        gv[:, at] = sl
+        sls[:, at] = sl
         yv[:, at] = m * sg * (1.0 + g * (1.0 - sg))
-        squares, crossed = gd * gd, dv[:, at] * gout[:, at] * gd
+        squares, crossed = gd * gd, dv[:, at].astype(F32) * gout[:, at] * gd
         return (
             sums[0] + squares[:, :128] + squares[:, 128:],
             sums[1] + crossed[:, :128] + crossed[:, 128:],
@@ -396,11 +413,11 @@
         gdr = gd * rs
         go = gout[:, at]
         nv[:, at] = (gdr * go).astype(BF)
-        d = dv[:, at]
+        d = dv[:, at].astype(F32)
         dgout[:, at] = jnp.sum(d * gdr, axis=0, keepdims=True)
         dgd = rs * (d * go) - gd * pull
         dgv[:, at] = (dgd * yv[:, at]).astype(BF)
-        dm = dgd * gv[:, at]
+        dm = dgd * sls[:, at]
         dmv[:, at] = dm.astype(BF)
         for copy in outward(i):
             copy.start()
@@ -414,67 +431,57 @@
         finish_all(outward(i))
 
 
-def pieces_out(ids, sources, keep, send, sem):
-    copies = []
-    for ref, base in ((send, 12), (keep, 8)):
-        for k in range(4):
-            for src, rows, put in sources:
-                start = pl.multiple_of(ids[base + k] * rows, 32)
-                copies.append((src.at[pl.ds(start, rows)], put(ref, k)))
-    return [pltpu.make_async_copy(a, b, sem.at[k]) for k, (a, b) in enumerate(copies)]
-
-
-def out_and_rows(
-    ids, cont, tok, u, dout, n16, dg16, dm16, cum, recv, hc, hr, rest, cs, ylf, ylr, *refs
+def grads_and_rows(
+    cont, cum, recv, hc, hr, dout, n16, u, dg16, dm16, cs, ylf, ylr, rows, dc, grads, *scratch
 ):
-    (out, rows, dc, keep, send), scratch = refs[:5], refs[5:]
-    wo, n_t, u_t, dwo, dwg, bcv, yfv, yrv, sf, sr, bsem, sem, wsem, osem = scratch
-    bc = pltpu.make_async_copy(cs.at[:, E:], bcv, bsem)
-    bc.start()
-    wait = fetch([(ylf, yfv), (ylr, yrv)], sem)
-    _, copies = load_rest(rest, None, wo, wsem)
-    n_t[...] = flip(n16[...])
-    u_t[...] = flip(u[HALO:, :])
+    n_t, u_t, dwo, dwg, bcv, yfv, yrv, sf, sr, doutv, nv, uv, dgv, dmv = scratch[:14]
+    lsem, sem, osem = scratch[14:]
+    loads = [(dout, doutv), (n16, nv), (u, uv), (dg16, dgv), (cs.at[:, E:], bcv)]
+    loads = [pltpu.make_async_copy(a, b, lsem.at[k]) for k, (a, b) in enumerate(loads)]
+    for copy in loads:
+        copy.start()
+    finish_all(loads[:2])
+    wait = fetch([(ylf, yfv), (ylr, yrv), (dm16, dmv)], sem)
+    n_t[...] = flip(nv[...])
 
     def rows_out(i, _):
         at = pl.ds(pl.multiple_of(i * 256, 256), 256)
-        dwo[at, :] = mm(n_t[at, :], dout[...]).astype(BF)
+        dwo[at, :] = mm(n_t[at, :], doutv[...]).astype(BF)
         return 0
 
     def rows_gate(i, _):
         at = pl.ds(pl.multiple_of(i * 256, 256), 256)
-        dwg[at, :] = mm(u_t[at, :], dg16[...]).astype(BF)
+        dwg[at, :] = mm(u_t[at, :], dgv[...]).astype(BF)
         return 0
 
     lax.fori_loop(0, E // 256, rows_out, 0)
+    finish_all(loads[2:4])
+    u_t[...] = flip(uv[HALO:, :])
     lax.fori_loop(0, D // 256, rows_gate, 0)
-    outward = pieces_out(
-        ids,
-        [
-            (dwg.at[:, :D], 96, lambda ref, k: ref.at[k, 0:96]),
-            (dwg.at[:, D:], 96, lambda ref, k: ref.at[k, 96:192]),
-            (dwo, 192, lambda ref, k: ref.at[k, 192:384]),
-        ],
-        keep,
-        send,
-        osem,
-    )
-    for copy in outward:
-        copy.start()
+    outward = []
+    for d in range(DP):
+        for src, rows_at, into in (
+            (dwg.at[:, :D], 96, slice(384 * d, 384 * d + 96)),
+            (dwg.at[:, D:], 96, slice(384 * d + 96, 384 * d + 192)),
+            (dwo, 192, slice(384 * d + 192, 384 * d + 384)),
+        ):
+            src = src.at[pl.ds(rows_at * d, rows_at)]
+            outward.append(pltpu.make_async_copy(src, grads.at[into], osem.at[len(outward)]))
+            outward[-1].start()
     take_slices(recv, sf, sr, cont[0])
     ef_f, ef_r = pairs_of(jnp.exp(cum[...]))
-    bc.wait()
+    finish_all(loads[4:])
     _, cf, _, cr = parts_of_bc(silu(bcv[...]))
 
     def tile(i, sums):
         at = wide(i)
         wait(i)
-        dm = dm16[:, at].astype(F32)
+        dm = dmv[:, at].astype(F32)
         new = []
         for ef2, c, s, yl in ((ef_f, cf, sf, yfv), (ef_r, cr, sr, yrv)):
             ef = mm(ef2, hc[:, at])
-            y = yl[:, at].astype(F32) + ef * mm(c, s[:, at])
-            new.append(mm((dm * y).astype(BF), hr[at, :]))
+            y = yl[:, at] + ef * mm(c, s[:, at])
+            new.append(head_sum(dm * y, hr[at, :]))
             new.append(mm_nt((ef * dm).astype(BF), s[:, at]))
         return tuple(a + b for a, b in zip(sums, new))
 
@@ -482,12 +489,15 @@
     rf, dcf, rr, dcr = lax.fori_loop(0, WIDE, tile, (zero, zn, zero, zn))
     rows[...] = rf + to_back(rr)
     dc[...] = jnp.concatenate([dcf, dcr], axis=1)
-    finish_all(copies)
+    finish_all(outward)
+
+
+def project_out(tok, n16, rest, out, wo, sem):
+    finish_all(load_rest(rest, None, wo, sem)[1])
     out[...] = (tok[...].astype(F32) + mm(n16[...], wo[...])).astype(BF)
-    finish_all(outward)
-
-
-def local_back(dt, cum, dm16, hc, cs, zf, zr, dgf, dgr, *scratch):
+
+
+def local_back(dt, cum, dm16, hc, hr, cs, zf, zr, dgf, dgr, inner, *scratch):
     csv, zfv, zrv, col, row, gf, gr, dm_t, sem, osem = scratch
     bc = pltpu.make_async_copy(cs.at[:, E:], csv.at[:, E:], sem.at[0, WIDE])
     bc.start()
@@ -511,15 +521,17 @@
             for k, (a, b) in enumerate([(zfv, zf), (zrv, zr)])
         ]
 
-    def tile(i, _):
+    def tile(i, sums):
         at = wide(i)
         wait(i)
         x = silu(csv[:, at])
+        new = []
         ds = jnp.concatenate(by_head(dm16[:, at].astype(F32)), axis=0)
         dms = dm_t[at, :]
         for forward in (True, False):
             first = 0 if forward else H
-            xs = by_head(x * mm(dt_f if forward else dt_r, hc[:, at]))
+            xd = x * mm(dt_f if forward else dt_r, hc[:, at])
+            xs = by_head(xd)
             ws = []
             small = jnp.zeros((128, 128), F32)
             large = jnp.zeros((T, 128), F32)
@@ -544,6 +556,7 @@
                     large = large + ea * dw[:, :128]
                     small = small + eb * dw[128:, 128:]
             total = mm(jnp.concatenate(ws, axis=1), ds)
+            new.append(head_sum(xd.astype(BF).astype(F32) * total, hr[at, :]))
             if forward:
                 zfv[:, at] = total.astype(BF)
                 dgf[:128, :128] += small
@@ -554,9 +567,11 @@
                 dgr[128:, 128:] += small
         for copy in outward(i):
             copy.start()
-        return 0
-
-    lax.fori_loop(0, WIDE, tile, 0)
+        return sums[0] + new[0], sums[1] + new[1]
+
+    zero = jnp.zeros((T, 128), F32)
+    sums = lax.fori_loop(0, WIDE, tile, (zero, zero))
+    inner[...] = sums[0] + to_back(sums[1])
     dgf[...] = jnp.where(t > s, dgf[...], 0.0)
     dgr[...] = jnp.where(t < s, dgr[...], 0.0)
     for i in range(WIDE):
@@ -564,20 +579,18 @@
 
 
 def inner_back(
-    ids, cont, tok, halo, gin, cw, alog, dsk, sraw, dt, cum, u, dout, dgf, dgr, back, fore, rows,
-    dc, dgout, hc, hr, cs, zf, zr, dm16, ci, dg16, rest, *refs
+    ids, cont, halo, gin, cw, alog, dsk, sraw, dt, cum, back, fore, rows, inner, dc, dgout, hc, hr,
+    dgf, dgr, tok, dout, cs, zf, zr, dm16, ci, dg16, rest, *refs
 ):
-    parts, (dtok, dhalo, dall, small_out), scratch = refs[:8], refs[8:12], refs[12:]
+    parts, (dtok, dhalo, dall_out, small_out), scratch = refs[:8], refs[8:12], refs[12:]
     csv, zfv, zrv, dmv, civ, dgv, w, wg, sf, sr, kf, kr, dcs, cif, du, small = scratch[:16]
-    line, sem, csem, wsem, gsem, dsem = scratch[16:]
-    bcc = pltpu.make_async_copy(cs.at[:, E:], csv.at[:, E:], csem.at[1])
+    line, dall, gfv, grv, tokv, doutv, sem, csem, wsem, gsem, osem = scratch[16:]
+    first = [(cs.at[:, E:], csv.at[:, E:])]
+    bcc = pltpu.make_async_copy(*first[0], csem.at[0])
     bcc.start()
     wait = fetch([(cs, csv), (zf, zfv), (zr, zrv), (dm16, dmv)], sem)
-    cic = pltpu.make_async_copy(ci, civ, csem.at[0])
-    cic.start()
-    loads = load_weights(ids, parts, w, wsem) + load_rest(rest, wg, None, gsem)[0]
-    loads.append(pltpu.make_async_copy(dg16, dgv, dsem))
-    loads[-1].start()
+    later = [(dgf, gfv), (dgr, grv), (ci, civ), (dg16, dgv), (tok, tokv), (dout, doutv)]
+    later = [pltpu.make_async_copy(a, b, csem.at[1 + k]) for k, (a, b) in enumerate(later)]
     keep = cont[0]
     take_slices(back, kr, kf, keep)
     take_slices(fore, sf, sr, keep)
@@ -592,11 +605,26 @@
     bc = csv[:, E:]
     bf, cf, br, cr = parts_of_bc(silu(bc))
 
+    def weights():
+        gates = load_rest(rest, wg, None, gsem, False)[0]
+        return load_weights(ids, parts, w, wsem, False) + gates
+
     def slope(v, sg):
         return sg * (1.0 + v * (1.0 - sg))
 
     def tile(i, sums):
         at = wide(i)
+
+        @pl.when(i == 1)
+        def _():
+            for copy in later:
+                copy.start()
+
+        @pl.when(i == 3)
+        def _():
+            for copy in weights():
+                copy.start()
+
         wait(i)
         v = csv[:, at]
         sg = sigmoid(v)
@@ -611,9 +639,8 @@
         ):
             dts, te = mm(dt2, hc[:, at]), mm(te2, hc[:, at])
             xd = (x * dts).astype(BF).astype(F32)
-            zi, zt = z[:, at].astype(F32), te * mm(b, k[:, at])
-            dx = dx + dts * (zi + zt)
-            new.append(mm((xd * zi).astype(BF), hr[at, :]))
+            zt = te * mm(b, k[:, at])
+            dx = dx + dts * (z[:, at].astype(F32) + zt)
             new.append(mm((xd * zt).astype(BF), hr[at, :]))
             new.append(mm_nt((te * xd).astype(BF), k[:, at]))
             both = s[:, at].astype(F32) * k[:, at].astype(F32)
@@ -624,11 +651,12 @@
         return tuple(a + b for a, b in zip(sums, new))
 
     zero, zn = jnp.zeros((T, 128), F32), jnp.zeros((T, N), F32)
-    sums = lax.fori_loop(0, WIDE, tile, (zero, zero, zn, zero, zero, zn))
-    inner, tails = sums[0] + to_back(sums[3]), sums[1] + to_back(sums[4])
-    gf16, gr16 = dgf[...].astype(BF), dgr[...].astype(BF)
-    dbf = sums[2] + mm(gf16, cf)
-    dbr = sums[5] + mm(gr16, cr)
+    sums = lax.fori_loop(0, WIDE, tile, (zero, zn, zero, zn))
+    tails = sums[0] + to_back(sums[2])
+    finish_all(later)
+    gf16, gr16 = gfv[...].astype(BF), grv[...].astype(BF)
+    dbf = sums[1] + mm(gf16, cf)
+    dbr = sums[3] + mm(gr16, cr)
     dcf = dc[:, :N] + mm(flip(gf16), bf)
     dcr = dc[:, N:] + mm(flip(gr16), br)
     dbc = jnp.concatenate([dbf, dcf, dbr, dcr], axis=1) * slope(bc, sigmoid(bc))
@@ -638,7 +666,7 @@
     heads = mm(hi, hr[...]) + mm(lo, hr[...])
     dots = heads[0:1] + to_back(heads)[1:2]
     rate = jnp.where(lanes(1) < 2 * H, jnp.exp(alog[...]), 0.0)
-    v = rows[...] - inner
+    v = rows[...] - inner[...]
     dla = jnp.where(
         lanes() < H,
         tri_sum(tri(lambda r, c: r <= c), v) + tri_sum(tri(lambda r, c: r > c), tails),
@@ -646,7 +674,7 @@
     ) + jnp.exp(last) * dots
     sg = sigmoid(sraw[...])
     ratio = jnp.where(dtv > 1e-20, sg / jnp.maximum(dtv, 1e-20), 1.0)
-    dstep = (inner + tails) * ratio - dla * rate * sg
+    dstep = (inner[...] + tails) * ratio - dla * rate * sg
     dstep = jnp.where(lanes() < 2 * H, dstep, 0.0)
     dall[0:HALO, C:] = jnp.zeros((HALO, 128), BF)
     dall[HALO:, C:] = dstep.astype(BF)
@@ -657,7 +685,11 @@
     small[90:91] = jnp.where(lanes(1) < H, heads[2:3], 0.0)
     mask = jnp.where(iota((HALO + T, 1), 0) < HALO, keep, 1.0)
 
-    cic.wait()
+    def outward(i):
+        at = pl.ds(pl.multiple_of(i * 128, 128), 128)
+        return pltpu.make_async_copy(dall.at[:, at], dall_out.at[:, at], osem.at[i])
+
+    outward(C // 128).start()
 
     def convolution(i, _):
         at = pl.ds(pl.multiple_of(i * 128, 128), 128)
@@ -670,12 +702,13 @@
             small[pl.ds(14 * k + i, 1)] = jnp.sum(g * shifted, axis=0, keepdims=True)
             total = total + cw[k : k + 1, at] * dcs[i, 3 - k : 3 - k + HALO + T]
         dall[:, at] = (total * mask).astype(BF)
+        outward(i).start()
         return 0
 
     lax.fori_loop(0, C // 128, convolution, 0)
     for j in range(E // 128):
         small[70 + j : 71 + j] = dgout[:, 128 * j : 128 * j + 128]
-    finish_all(loads)
+    finish_all(weights())
 
     def input_grad(i, _):
         at = wide(i)
@@ -684,7 +717,7 @@
         return 0
 
     lax.fori_loop(0, D // 256, input_grad, 0)
-    x = jnp.concatenate([halo[...], tok[...]], axis=0).astype(F32)
+    x = jnp.concatenate([halo[...], tokv[...]], axis=0).astype(F32)
     r = lax.rsqrt(jnp.mean(x * x, axis=1, keepdims=True) + EPS)
     duxr = jnp.sum(du[...] * x * r, axis=0, keepdims=True)
     for j in range(6):
@@ -693,11 +726,12 @@
     dxh = du[...] * gin[...]
     dx = r * dxh - x * (r * r * r * jnp.mean(dxh * x, axis=1, keepdims=True))
     dhalo[...] = dx[:HALO]
-    dtok[...] = dout[...].astype(F32) + dx[HALO:]
+    dtok[...] = doutv[...].astype(F32) + dx[HALO:]
+    for i in range(CD // 128):
+        outward(i).wait()
 
 
 def weight_back(ids, u, dall, small, keep, send, u_t, dw, osem, ssem):
-    u_t[...] = flip(u[...])
     extra = []
     for ref, base in ((send, 0), (keep, 4)):
         for k in range(4):
@@ -705,58 +739,66 @@
                 pltpu.make_async_copy(small, ref.at[k, :, pl.ds(CD, 128)], ssem.at[base + k])
             )
             extra[-1].start()
-
-    def rows(i, _):
-        at = pl.ds(pl.multiple_of(i * 256, 256), 256)
+    u_t[...] = flip(u[...])
+
+    def piece(d, ref):
+        where = ids[16 + d // 2]
+        src = dw.at[pl.ds(96 * d, 96)]
+        return pltpu.make_async_copy(src, ref.at[where, :, pl.ds(0, CD)], osem.at[d])
+
+    def each(d, act):
+        mine = ids[20] == d % 2
+
+        @pl.when(mine)
+        def _():
+            act(piece(d, keep))
+
+        @pl.when(jnp.logical_not(mine))
+        def _():
+            act(piece(d, send))
+
+    done = 0
+    for c in range(D // 256):
+        at = slice(256 * c, 256 * c + 256)
         dw[at, :] = mm(u_t[at, :], dall[...]).astype(BF)
-        return 0
-
-    lax.fori_loop(0, D // 256, rows, 0)
-    copies = pieces_out(
-        ids, [(dw, 96, lambda ref, k: ref.at[k, :, pl.ds(0, CD)])], keep, send, osem
-    )
-    for copy in copies:
-        copy.start()
+        while 96 * (done + 1) <= 256 * (c + 1):
+            each(done, lambda copy: copy.start())
+            done += 1
     finish_all(extra)
-    finish_all(copies)
-
-
-def add_pairs(a, b, *outs):
-    for k in range(4):
-
-        def rows(i, _, k=k):
+    for d in range(DP):
+        each(d, lambda copy: copy.wait())
+
+
+def add_pairs(ids, a, b, whole, one, three, mine, other):
+    for k, out in ((0, whole), (1, one), (3, three)):
+
+        def rows(i, _, k=k, out=out):
             at = pl.ds(pl.multiple_of(i * 48, 16), 48)
-            outs[k][at] = (a[k, at].astype(F32) + b[k, at].astype(F32)).astype(BF)
+            out[at] = (a[k, at].astype(F32) + b[k, at].astype(F32)).astype(BF)
             return 0
 
-        lax.fori_loop(0, a.shape[1] // 48, rows, 0)
-
-
-def add_middle(one, up, three, down, out_one, out_three):
-    half = one.shape[0] // 2
-    for ref, part, out, at in ((one, up, out_one, 0), (three, down, out_three, half)):
-        for r in range(0, 2 * half, 48):
-            rows = slice(r, r + 48)
-            total = ref[rows].astype(F32)
-            if at <= r < at + half:
-                total = total + part[r - at : r - at + 48].astype(F32)
-            out[rows] = total.astype(BF)
-
-
-def add_y(*refs):
-    rest, tail, out = refs[:3], refs[3:7], refs[7]
-
-    def total(parts, rows, at):
-        return sum(part[rows, at].astype(F32) for part in parts).astype(BF)
-
+        lax.fori_loop(0, 2, rows, 0)
+    for out, half in ((mine, ids[HALF]), (other, 1 - ids[HALF])):
+        at = pl.ds(pl.multiple_of(half * 1024, 1024), 1024)
+        out[...] = (a[2, :, at].astype(F32) + b[2, :, at].astype(F32)).astype(BF)
+
+
+def add_two(a, b, out):
+    out[...] = (a[...].astype(F32) + b[...].astype(F32)).astype(BF)
+
+
+def add_y(ids, rest, whole, one, three, half, out):
     for j in range(6):
         for r in range(0, 384, 48):
             row = 384 * j + r
-            out[row // 144, row % 144 : row % 144 + 48] = total(
-                rest, slice(r, r + 48), slice(128 * j, 128 * j + 128)
-            )
+            out[row // 144, row % 144 : row % 144 + 48] = rest[
+                r : r + 48, 128 * j : 128 * j + 128
+            ]
     for j in range(SEQ):
-        out[j, 144:] = total(tail, slice(0, 96), slice(128 * j, 128 * j + 128))
+        at, in_half = slice(128 * j, 128 * j + 128), slice(128 * (j % 8), 128 * (j % 8) + 128)
+        mine = jnp.where(ids[HALF] == j // 8, 1.0, 0.0)
+        total = sum(part[:, at].astype(F32) for part in (whole, one, three))
+        out[j, 144:] = (total + half[:, in_half].astype(F32) * mine).astype(BF)
 
 
 def add_blocks(recv, out):
@@ -781,7 +823,7 @@
         put(dwout, at, 384 * j + 192, 192)
     for j in range(14):
         dwin[:, E + 128 * j : E + 128 * j + 128] = sums[j, 144:].astype(F32)
-    dwdt[...] = sums[14, 144:, 0 : 2 * H].astype(F32)
+    dwdt[...] = sums[14, 144:].astype(F32).T[: 2 * H]
     small = sums[15, 144:].astype(F32)
     for j in range(14):
         at = slice(128 * j, 128 * j + 128)
@@ -833,23 +875,11 @@
 
 
 SWAP = [(i, i ^ 1) for i in range(DP)]
+NEXT_Z = [(i, i ^ 1) for i in range(SEQ)]
 
 
 def exchange(value):
     return lax.all_to_all(value, "seq", 0, 0, tiled=True)
-
-
-def add_swapped(keep, send, name, after=None):
-    recv = lax.ppermute(send, "dp", SWAP)
-    if after is not None:
-        recv = together(recv, after)[0]
-    rows, cols = keep.shape[1:]
-    outs = [shape(rows, cols, dtype=BF)] * 4
-    return call(add_pairs, name, [(V, keep), (V, recv)], outs, limit=SMALL)
-
-
-def over_y(parts):
-    return [parts[0]] + [lax.ppermute(parts[k], "dp", shift_y(k)) for k in (1, 2, 3)]
 
 
 def together(*values):
@@ -872,7 +902,9 @@
     to_y = [(y + k) % 4 for k in range(4)]
     from_y = [(y - k) % 4 for k in range(4)]
     ids = [2 * t + core for t in from_y] + [2 * t + 1 - core for t in from_y]
-    ids = jnp.stack(ids + [2 * t + core for t in to_y] + [2 * t + 1 - core for t in to_y])
+    ids += [2 * t + core for t in to_y] + [2 * t + 1 - core for t in to_y]
+    parity = lax.axis_index("seq") % 2
+    ids = jnp.stack(ids + [(t - y) % 4 for t in range(4)] + [core, parity])
 
     own = jnp.concatenate([w_in[:, E:], jnp.pad(w_dt, ((0, 0), (0, 128 - 2 * H)))], axis=1)
     column = [lax.ppermute(own, "dp", shift_y(k)) for k in (1, 2, 3)]
@@ -901,36 +933,25 @@
         + [shape(T, 128)] * 3
         + [shape(SEQ, 48, 384, dtype=BF)],
         [w_scratch, vm(2, HALO + T, 128), vm(T, C), vm(HALO + T, C, dtype=BF)]
-        + [dma((8,)), dma((2, WIDE + 1))],
+        + [vm(HALO + T, D, dtype=BF), dma((8,)), dma((2, WIDE + 1)), dma(())],
         flops=2 * T * D * CD,
-        apart=(1, 2),
+        apart=(0, 1, 2),
     )
 
     def scan(got, name):
         out = shape(SEQ, 32, 384, dtype=BF)
         return call(scan_blocks, name, [(V, got)], [out], limit=SMALL)[0]
 
-    mix_scratch = [vm(256, E, dtype=BF), vm(H, T, 128), vm(128, T), vm(T, T)]
-    mix_scratch += [dma((3, WIDE)), dma((2, WIDE))]
-    mix_cost = 2 * 24 * T * T * 256
     got = exchange(pay)
-    ylf = call(
-        partial(local_mix, True),
-        "mix_forward",
-        [(ANY, cs), (V, dt), (V, cum), (ANY, hc)],
-        [shape(T, E, dtype=BF)],
-        [vm(T, C), half] + mix_scratch,
-        flops=mix_cost,
-        apart=(0,),
-    )[0]
-    ylr, base = call(
-        partial(local_mix, False),
-        "mix_reverse",
-        [(ANY, cs), (V, dt), (V, cum), (ANY, hc), (ANY, ylf), (V, dsk)],
-        [shape(T, E, dtype=BF), shape(T, E)],
-        [vm(T, C), half, half, full] + mix_scratch,
-        flops=mix_cost,
-        apart=(0, 1),
+    ylf, ylr, base = call(
+        local_mix,
+        "local_mix",
+        [(V, dt), (V, cum), (V, dsk), (V, hc), (ANY, cs)],
+        [shape(T, E)] * 3,
+        [vm(T, C), full, full, full, vm(2 * H, T, 128), vm(128, T), vm(T, T), vm(T, T)]
+        + [dma(()), dma((1, WIDE)), dma((3, WIDE))],
+        flops=4 * 24 * T * T * 256,
+        apart=(0, 1, 2),
     )
     got, ylr, base = together(got, ylr, base)
     fore = exchange(scan(got, "scan_states"))
@@ -938,9 +959,10 @@
         gate_products,
         "gate_products",
         [(V, u), (V, dout), (ANY, rest)],
-        [shape(T, E)] * 2,
-        [vm(2, D, D, dtype=BF), vm(E, D, dtype=BF), dma((24,))],
+        [shape(T, E, dtype=BF)] * 2,
+        [vm(2, D, D, dtype=BF), vm(E, D, dtype=BF), half, half, dma((24,)), dma((4,))],
         flops=4 * T * D * E,
+        apart=(0, 1),
     )
     n16, dg16, dm16, dgout, pay_back = call(
         gated_norm,
@@ -948,98 +970,107 @@
         [(S, cont), (V, cum), (V, fore), (V, gout), (V, hc)]
         + [(ANY, a) for a in (cs, base, gate, dn)],
         [shape(T, E, dtype=BF)] * 3 + [shape(1, E), shape(SEQ, 48, 384, dtype=BF)],
-        [vm(T, 256)] + [full] * 6 + [half] * 3 + [state] * 2
+        [vm(T, 256), full, half, half] + [full] * 4 + [half] * 3 + [state] * 2
         + [dma(()), dma((3, WIDE)), dma((3, WIDE))],
         flops=12 * T * N * E,
         apart=(0, 1, 2),
     )
     got = exchange(pay_back)
-    out, rows, dc, rest_keep, rest_send = call(
-        out_and_rows,
-        "out_and_rows",
-        [(S, ids), (S, cont)]
-        + [(V, a) for a in (tok, u, dout, n16, dg16, dm16, cum, fore, hc, hr)]
-        + [(ANY, a) for a in (rest, cs, ylf, ylr)],
-        [shape(T, D, dtype=BF), shape(T, 128), shape(T, 128)] + [shape(4, 384, D, dtype=BF)] * 2,
-        [vm(E, D, dtype=BF), vm(E, T, dtype=BF), vm(D, T, dtype=BF), vm(E, D, dtype=BF)]
-        + [vm(D, E, dtype=BF), vm(T, 256), half, half, state, state]
-        + [dma(()), dma((2, WIDE)), dma((8,)), dma((24,))],
+    rows, dc, rest_grads = call(
+        grads_and_rows,
+        "grads_and_rows",
+        [(S, cont)]
+        + [(V, a) for a in (cum, fore, hc, hr)]
+        + [(ANY, a) for a in (dout, n16, u, dg16, dm16, cs, ylf, ylr)],
+        [shape(T, 128), shape(T, 128), shape(DP * 384, D, dtype=BF)],
+        [vm(E, T, dtype=BF), vm(D, T, dtype=BF), vm(E, D, dtype=BF), vm(D, E, dtype=BF)]
+        + [vm(T, 256), full, full, state, state, vm(T, D, dtype=BF), half]
+        + [vm(HALO + T, D, dtype=BF), half, half]
+        + [dma((5,)), dma((3, WIDE)), dma((24,))],
         flops=8 * T * D * E,
-        apart=(3, 4),
-    )
-    got, out, rows, rest_keep, rest_send = together(got, out, rows, rest_keep, rest_send)
-    scanned = scan(got, "scan_adjoints")
-    back = exchange(scanned)
-    rest_parts = add_swapped(rest_keep, rest_send, "add_rest_cores", scanned)
-    dm16, *rest_parts = together(dm16, *rest_parts)
-    half_up = lax.ppermute(rest_parts[2][:192], "dp", shift_y(1))
-    half_down = lax.ppermute(rest_parts[2][192:], "dp", shift_y(3))
-    zf, zr, dgf, dgr = call(
+        apart=(2,),
+    )
+    got, rows, rest_grads = together(got, rows, rest_grads)
+    rest_sum = lax.psum_scatter(rest_grads, "dp", scatter_dimension=0, tiled=True)
+    back = exchange(scan(got, "scan_adjoints"))
+    zf, zr, dgf, dgr, inner = call(
         local_back,
         "local_back",
-        [(V, dt), (V, cum), (V, dm16), (V, hc), (ANY, cs)],
-        [shape(T, E, dtype=BF)] * 2 + [shape(T, T)] * 2,
+        [(V, dt), (V, cum), (V, dm16), (V, hc), (V, hr), (ANY, cs)],
+        [shape(T, E, dtype=BF)] * 2 + [shape(T, T)] * 2 + [shape(T, 128)],
         [vm(T, C), half, half, vm(2 * H, T, 128), vm(128, T), vm(T, T), vm(T, T)]
         + [vm(E, T, dtype=BF), dma((1, WIDE + 1)), dma((2, WIDE))],
         flops=4 * 48 * T * T * 256,
         apart=(0, 1),
     )
-    back, zf, half_up, half_down = together(back, zf, half_up, half_down)
-    up, down = call(
-        add_middle,
-        "add_rest_middle",
-        [(V, rest_parts[1]), (V, half_up), (V, rest_parts[3]), (V, half_down)],
-        [shape(384, D, dtype=BF)] * 2,
-        limit=SMALL,
-    )
-    zf, up, down = together(zf, up, down)
-    rest_parts = [
-        rest_parts[0], lax.ppermute(up, "dp", shift_y(1)), lax.ppermute(down, "dp", shift_y(3))
-    ]
     dtok, dhalo, dall, small = call(
         inner_back,
         "inner_back",
         [(S, ids), (S, cont)]
-        + [(V, a) for a in (tok, halo, gin, conv_w, alog, dsk, sraw, dt, cum, u, dout, dgf, dgr)]
-        + [(V, a) for a in (back, fore, rows, dc, dgout, hc, hr)]
-        + [(ANY, a) for a in (cs, zf, zr, dm16, ci, dg16, rest)]
+        + [(V, a) for a in (halo, gin, conv_w, alog, dsk, sraw, dt, cum, back, fore, rows)]
+        + [(V, a) for a in (inner, dc, dgout, hc, hr)]
+        + [(ANY, a) for a in (dgf, dgr, tok, dout, cs, zf, zr, dm16, ci, dg16, rest)]
         + part_ins,
         [shape(T, D), shape(HALO, D), shape(HALO + T, CD, dtype=BF), shape(96, 128, dtype=BF)],
         [vm(T, C), half, half, half, vm(HALO + T, C, dtype=BF), half, w_scratch]
         + [vm(2, D, D, dtype=BF)]
         + [state] * 4
         + [vm(C // 128, HALO + T + 16, 128), vm(HALO + T, 128), vm(HALO + T, D), vm(96, 128)]
-        + [vm(8, E), dma((4, WIDE)), dma((2,)), dma((8,)), dma((16,)), dma(())],
+        + [vm(8, E), vm(HALO + T, CD, dtype=BF), vm(T, T), vm(T, T)]
+        + [vm(T, D, dtype=BF), vm(T, D, dtype=BF)]
+        + [dma((4, WIDE)), dma((7,)), dma((8,)), dma((16,)), dma((CD // 128,))],
         flops=2 * T * D * (CD + E),
-    )
-    dall, *rest_parts = together(dall, *rest_parts)
+        apart=(2,),
+    )
     keep, send = call(
         weight_back,
         "weight_back",
         [(S, ids), (V, u), (V, dall), (V, small)],
         [shape(4, 96, 2048, dtype=BF)] * 2,
-        [vm(D, HALO + T, dtype=BF), w_scratch, dma((8,)), dma((8,))],
+        [vm(D, HALO + T, dtype=BF), vm(D, CD, dtype=BF), dma((8,)), dma((8,))],
         flops=2 * T * D * CD,
         apart=(0, 1),
-    )
-    tail_parts = over_y(add_swapped(keep, send, "add_tail_cores"))
+        limit=16 * 1024 * 1024,
+    )
+    recv = lax.ppermute(send, "dp", SWAP)
+    whole, one, three, mine, other = call(
+        add_pairs,
+        "add_tail_cores",
+        [(S, ids), (V, keep), (V, recv)],
+        [shape(96, 2048, dtype=BF)] * 3 + [shape(96, 1024, dtype=BF)] * 2,
+        limit=SMALL,
+    )
+    other = lax.ppermute(other, "seq", NEXT_Z)
+    one, three = lax.ppermute(one, "dp", shift_y(1)), lax.ppermute(three, "dp", shift_y(3))
+    sides = [(V, mine), (V, other)]
+    half = call(add_two, "add_tail_z", sides, [shape(96, 1024, dtype=BF)], limit=SMALL)[0]
+    half, n16, dhalo = together(half, n16, dhalo)
+    half = lax.ppermute(half, "dp", shift_y(2))
     dback = lax.ppermute(dhalo, "seq", [(i + 1, i) for i in range(SEQ - 1)])
+    out = call(
+        project_out,
+        "project_out",
+        [(V, tok), (V, n16), (ANY, rest)],
+        [shape(T, D, dtype=BF)],
+        [vm(E, D, dtype=BF), dma((8,))],
+        flops=2 * T * D * E,
+    )[0]
     dtok = dtok.at[-HALO:].add(dback)
-    *tail_parts, dtok = together(*tail_parts, dtok)
+    one, three, half, out, dtok = together(one, three, half, out, dtok)
     slices = shape(SEQ, 240, 128, dtype=BF)
-    sums = [(V, part) for part in (*rest_parts, *tail_parts)]
+    sums = [(S, ids)] + [(V, part) for part in (rest_sum, whole, one, three, half)]
     sums = call(add_y, "add_y", sums, [slices], limit=SMALL)[0]
     sums = call(add_blocks, "add_seq", [(V, exchange(sums))], [slices], limit=SMALL)[0]
     dwin, dwdt, dwout, dcw, dcb, dgo, dgi, ddtb, dal, dds = call(
         finish,
         "finish",
         [(V, exchange(sums))],
-        [shape(96, E + C), shape(96, 2 * H), shape(192, D), shape(4, C), shape(C)]
+        [shape(96, E + C), shape(2 * H, 96), shape(192, D), shape(4, C), shape(C)]
         + [shape(E), shape(D), shape(2 * H), shape(H), shape(H)],
         limit=SMALL,
     )
     return (
-        out[None], dtok[None], dgi, dwin, dwdt, dcw, dcb, ddtb, dal, dds, dgo, dwout,
+        out[None], dtok[None], dgi, dwin, dwdt.T, dcw, dcb, ddtb, dal, dds, dgo, dwout,
     )
 
 

time: 241 us -> 225 us (0.934)
  starting transfers between devices: 47.6 us -> 39.5 us
  blocking collectives: 40.2 us -> 36.8 us
    ppermute x9 -> x5, waiting for transfers between devices: 13.9 us -> 8.47 us  [the longest x1 3.4 us: local(): recv = lax.ppermute(send, 'dp', SWAP)]
    ppermute x1, waiting for transfers between devices: 4.68 us -> 0.01 us  [local(): dback = lax.ppermute(dhalo, 'seq', [(i + 1, i) for i in range(SEQ - 1)])]
    all_to_all x4, waiting for transfers between devices: 3.73 us -> 7.78 us  [exchange(): return lax.all_to_all(value, 'seq', 0, 0, tiled=True)]
    ppermute x3, waiting for transfers between devices: 2.49 us -> 6.3 us  [local(): column = [lax.ppermute(own, 'dp', shift_y(k)) for k in (1, 2, 3)]]
    all_to_all x4, starting transfers between devices: 26.1 us -> 22.4 us  [exchange(): return lax.all_to_all(value, 'seq', 0, 0, tiled=True)]
    ppermute x9 -> x5, starting transfers between devices: 9.76 us -> 6.24 us  [the longest x1 3.23 us: local(): lax.ppermute(three, 'dp', shift_y(3))]
    all_to_all x2, blocking collectives: 40.2 us -> 36.8 us  [exchange(): return lax.all_to_all(value, 'seq', 0, 0, tiled=True)]
    pallas_call x17 -> x16, Pallas kernels: 90.7 us -> 89.6 us  [call(): pl.pallas_call(kernel, name=name, out_shape=tuple(outs), in_specs=list(sp...]
  transfers between devices with their start and end apart: 23 -> 20, of which waited for: 10 -> 11; matrix products, arithmetic and copies ran while one was open for 4% -> 4% of each run, Pallas kernels for 31% -> 35%
where the time goes in v3:
time: 225 us; the launch traced here: 222 us
  Pallas kernels  89.6 us (40%)
  starting transfers between devices  39.5 us (18%)
  blocking collectives  36.8 us (16%)
  waiting for transfers between devices  24.1 us (11%)
  between operations  15.1 us (7%)
  local copies, waits for them, and re-layouts  12.1 us (5%)
  other arithmetic  4.77 us (2%)
    pallas_call x16, Pallas kernels, call(): pl.pallas_call(kernel, name=name, out_shape=tuple(outs), in_specs=list(sp...  89.6 us
    all_to_all x2, blocking collectives, exchange(): return lax.all_to_all(value, 'seq', 0, 0, tiled=True)  36.8 us
    all_to_all x4, starting transfers between devices, exchange(): return lax.all_to_all(value, 'seq', 0, 0, tiled=True)  22.4 us
    all_to_all x4, waiting for transfers between devices, exchange(): return lax.all_to_all(value, 'seq', 0, 0, tiled=True)  7.78 us
    ppermute x3, waiting for transfers between devices, local(): column = [lax.ppermute(own, 'dp', shift_y(k)) for k in (1, 2, 3)]  6.3 us
    unnamed x49, local copies, waits for them, and re-layouts  6.15 us
    ppermute x3, starting transfers between devices, local(): column = [lax.ppermute(own, 'dp', shift_y(k)) for k in (1, 2, 3)]  4.77 us
  transfers between devices with their start and end apart: 20, of which 11 were waited for; matrix products, arithmetic and copies ran while one was open for 4% of the time, Pallas kernels for 35%

profile of v3, /device:TPU:0, one launch (start us, length us, event | category | flops | bytes accessed | tf_op | source)
XLA Modules:
  0.0 222.0 jit_solution(1281920637500551405)
XLA Ops:
  9.3 3.2 %collective-permute-start.2 = (bf16[96,1920]{1,0:T(8,128)(2,1)S(1)}, bf16[96,1920]{1,0:T(8,128)(2,1)S(1)}, u32[]{:S(2)}, u32[]{:S(2)}) collective-permute-start(bf16[96,1920]{1,0:T(8,128)(2,1)S(1)} %fusion.2.refs_0_), channel_id=1, source_target_pairs={{0,96},{16,112},{32,0},{48,16},{64,32},{80,48},{96,64},{112,80},{1... | collective-permute-start | bytes 1105928 | tf_op jit(solution)/shard_map/ppermute | solution.py:910
  14.8 3.8 %collective-permute-start.3 = (bf16[16,768]{1,0:T(8,128)(2,1)S(1)}, bf16[16,768]{1,0:T(8,128)(2,1)S(1)}, u32[]{:S(2)}, u32[]{:S(2)}) collective-permute-start(bf16[16,768]{1,0:T(8,128)(2,1)S(1)} %slice_bitcast_fusion), channel_id=1, source_target_pairs={{0,1},{1,2},{2,3},{3,4},{4,5},{5,6},{6,7},{7,8},{8,9},{9,10},{10,1... | collective-permute-start | bytes 73736 | tf_op jit(solution)/shard_map/ppermute | solution.py:911
  26.2 2.6 %collective-permute-done.2.refs_3_ = bf16[96,1920]{1,0:T(8,128)(2,1)S(1)} collective-permute-done((bf16[96,1920]{1,0:T(8,128)(2,1)S(1)}, bf16[96,1920]{1,0:T(8,128)(2,1)S(1)}, u32[]{:S(2)}, u32[]{:S(2)}) %collective-permute-start.2) | collective-permute-done | bytes 368672 | tf_op jit(solution)/shard_map/ppermute | solution.py:910
  28.8 3.7 %collective-permute-done.refs_1_ = bf16[96,1920]{1,0:T(8,128)(2,1)S(1)} collective-permute-done((bf16[96,1920]{1,0:T(8,128)(2,1)S(1)}, bf16[96,1920]{1,0:T(8,128)(2,1)S(1)}, u32[]{:S(2)}, u32[]{:S(2)}) %collective-permute-start) | collective-permute-done | bytes 368672 | tf_op jit(solution)/shard_map/ppermute | solution.py:910
  36.2 10.9 %front.1 = (bf16[272,768]{1,0:T(8,128)(2,1)}, bf16[272,1792]{1,0:T(8,128)(2,1)}, f32[256,1792]{1,0:T(8,128)}, f32[256,128]{1,0:T(8,128)}, f32[256,128]{1,0:T(8,1...) custom-call(s32[22]{0:T(128)} %stack.85.ids, f32[1]{0:T(128)} %bitcast.23.cont, bf16[256,768]{1,0:T(8,128)(2,1)} %bitcast.32, ...), custom_call_target="tpu_custom_call" | custom-call | flops 754974720 | bytes 7814236 | tf_op jit(solution)/shard_map/front/pallas_call | solution.py:855
  47.1 7.9 %all-to-all-start = ((bf16[16,48,384]{2,1,0:T(8,128)(2,1)}), bf16[16,48,384]{2,1,0:T(8,128)(2,1)S(1)}, u32[]{:S(2)}, u32[]{:S(2)}) async-start(bf16[16,48,384]{2,1,0:T(8,128)(2,1)} %get-tuple-element.115), calls=%async_computation | async-start | bytes 1179648 | tf_op jit(solution)/shard_map/all_to_all | solution.py:882
  55.0 8.5 %local_mix.1 = (f32[256,1536]{1,0:T(8,128)}, f32[256,1536]{1,0:T(8,128)}, f32[256,1536]{1,0:T(8,128)}) custom-call(f32[256,128]{1,0:T(8,128)} %get-tuple-element.113.dt, f32[256,128]{1,0:T(8,128)} %get-tuple-element.114.cum, f32[1,1536]{1,0:T(1,128)} %reshape_reshape.3.dsk, bf16[64,1536]{1,0:T(8,128)(2,1)} %select_convert_fusion.1.hc, ...), custom_call_target="tpu_custom_call" | custom-call | flops 1610612736 | bytes 7018496 | tf_op jit(solution)/shard_map/local_mix/pallas_call | solution.py:855
  63.5 3.9 %all-to-all-done.recv = bf16[16,48,384]{2,1,0:T(8,128)(2,1)S(1)} async-done(((bf16[16,48,384]{2,1,0:T(8,128)(2,1)}), bf16[16,48,384]{2,1,0:T(8,128)(2,1)S(1)}, u32[]{:S(2)}, u32[]{:S(2)}) %all-to-all-start) | async-done | bytes 589856 | tf_op jit(solution)/shard_map/all_to_all | solution.py:882
  68.3 3.6 %all-to-all-start.1 = ((bf16[16,32,384]{2,1,0:T(8,128)(2,1)}), bf16[16,32,384]{2,1,0:T(8,128)(2,1)S(1)}, u32[]{:S(2)}, u32[]{:S(2)}) async-start(bf16[16,32,384]{2,1,0:T(8,128)(2,1)} %scan_states.1), calls=%async_computation.1 | async-start | bytes 786432 | tf_op jit(solution)/shard_map/all_to_all | solution.py:882
  71.9 5.4 %gate_products.1 = (bf16[256,1536]{1,0:T(8,128)(2,1)}, bf16[256,1536]{1,0:T(8,128)(2,1)}) custom-call(bf16[272,768]{1,0:T(8,128)(2,1)} %get-tuple-element.110.u, bf16[256,768]{1,0:T(8,128)(2,1)} %bitcast.35, bf16[3072,768]{1,0:T(8,128)(2,1)} %all-gather.2.cloned.1.call-done.rest), custom_call_target="tpu_custom_call" | custom-call | flops 1207959552 | bytes 7102464 | tf_op jit(solution)/shard_map/gate_products/pallas_call | solution.py:855
  77.3 3.8 %all-to-all-done.1.recv.fore = bf16[16,32,384]{2,1,0:T(8,128)(2,1)S(1)} async-done(((bf16[16,32,384]{2,1,0:T(8,128)(2,1)}), bf16[16,32,384]{2,1,0:T(8,128)(2,1)S(1)}, u32[]{:S(2)}, u32[]{:S(2)}) %all-to-all-start.1) | async-done | bytes 393248 | tf_op jit(solution)/shard_map/all_to_all | solution.py:882
  81.9 9.6 %gated_norm.1 = (bf16[256,1536]{1,0:T(8,128)(2,1)}, bf16[256,1536]{1,0:T(8,128)(2,1)}, bf16[256,1536]{1,0:T(8,128)(2,1)}, f32[1,1536]{1,0:T(1,128)}, bf16[16,48,384]{2,1,0:T(8,128)(2,1)}) custom-call(f32[1]{0:T(128)} %bitcast.23.cont, f32[256,128]{1,0:T(8,128)} %get-tuple-element.114.cum, bf16[16,32,384]{2,1,0:T(8,128)(2,1)} %copy-done.5, ...), custom_call_target="tpu_custom_call" | custom-call | flops 301989888 | bytes 8663044 | tf_op jit(solution)/shard_map/gated_norm/pallas_call | solution.py:855
  91.5 3.7 %all-to-all-start.2 = ((bf16[16,48,384]{2,1,0:T(8,128)(2,1)}), bf16[16,48,384]{2,1,0:T(8,128)(2,1)S(1)}, u32[]{:S(2)}, u32[]{:S(2)}) async-start(bf16[16,48,384]{2,1,0:T(8,128)(2,1)} %get-tuple-element.125), calls=%async_computation.2 | async-start | bytes 1179648 | tf_op jit(solution)/shard_map/all_to_all | solution.py:882
  95.5 12.1 %grads_and_rows.1 = (f32[256,128]{1,0:T(8,128)}, f32[256,128]{1,0:T(8,128)}, bf16[3072,768]{1,0:T(8,128)(2,1)}) custom-call(f32[1]{0:T(128)} %bitcast.23.cont, f32[256,128]{1,0:T(8,128)} %get-tuple-element.114.cum, bf16[16,32,384]{2,1,0:T(8,128)(2,1)} %copy-done.5, bf16[64,1536]{1,0:T(8,128)(2,1)} %select_convert_fusion.1.hc, ...), custom_call_target="tpu_custom_call" | custom-call | flops 2415919104 | bytes 14245892 | tf_op jit(solution)/shard_map/grads_and_rows/pallas_call | solution.py:855
  108.5 7.2 %all-to-all-start.3 = ((bf16[16,32,384]{2,1,0:T(8,128)(2,1)}), bf16[16,32,384]{2,1,0:T(8,128)(2,1)S(1)}, u32[]{:S(2)}, u32[]{:S(2)}) async-start(bf16[16,32,384]{2,1,0:T(8,128)(2,1)} %scan_adjoints.1), calls=%async_computation.3 | async-start | bytes 786432 | tf_op jit(solution)/shard_map/all_to_all | solution.py:882
  115.7 15.7 %local_back.1 = (bf16[256,1536]{1,0:T(8,128)(2,1)}, bf16[256,1536]{1,0:T(8,128)(2,1)}, f32[256,256]{1,0:T(8,128)}, f32[256,256]{1,0:T(8,128)}, f32[256,128]{1,0:T(8,128)}) custom-call(f32[256,128]{1,0:T(8,128)} %get-tuple-element.113.dt, f32[256,128]{1,0:T(8,128)} %get-tuple-element.114.cum, bf16[256,1536]{1,0:T(8,128)(2,1)} %get-tuple-element.129.dm16, ...), custom_call_target="tpu_custom_call" | custom-call | flops 3221225472 | bytes 5701632 | tf_op jit(solution)/shard_map/local_back/pallas_call | solution.py:855
  132.2 14.4 %inner_back.1 = (f32[256,768]{1,0:T(8,128)}, f32[16,768]{1,0:T(8,128)}, bf16[272,1920]{1,0:T(8,128)(2,1)}, bf16[96,128]{1,0:T(8,128)(2,1)}) custom-call(s32[22]{0:T(128)} %stack.85.ids, f32[1]{0:T(128)} %bitcast.23.cont, bf16[16,768]{1,0:T(8,128)(2,1)} %copy-done.16, f32[1,768]{1,0:T(1,128)} %reshape.70.gin, f32[4,1792]{1,0:T(4,128)} %cw.3, ...), custom_call_target="tpu_custom_call" | custom-call | flops 1358954496 | bytes 19070556 | tf_op jit(solution)/shard_map/inner_back/pallas_call | solution.py:855
  146.6 1.2 copy-done.3
  148.6 3.4 %weight_back.1 = (bf16[4,96,2048]{2,1,0:T(8,128)(2,1)S(1)}, bf16[4,96,2048]{2,1,0:T(8,128)(2,1)S(1)}) custom-call(s32[22]{0:T(128)S(1)} %copy-done.2, bf16[272,768]{1,0:T(8,128)(2,1)S(1)} %copy-done, bf16[272,1920]{1,0:T(8,128)(2,1)S(1)} %copy-done.3, bf16[96,128]{1,0:T(8,128)(2,1)S(1)} %copy-done.4), custom_call_target="tpu_custom_call" | custom-call | flops 754974720 | bytes 4632664 | tf_op jit(solution)/shard_map/weight_back/pallas_call | solution.py:855
  152.1 3.4 %collective-permute-done.8.b = bf16[4,96,2048]{2,1,0:T(8,128)(2,1)S(1)} collective-permute-done((bf16[4,96,2048]{2,1,0:T(8,128)(2,1)S(1)}, bf16[4,96,2048]{2,1,0:T(8,128)(2,1)S(1)}, u32[]{:S(2)}, u32[]{:S(2)}) %collective-permute-start.8) | collective-permute-done | bytes 1572896 | tf_op jit(solution)/shard_map/ppermute | solution.py:1035
  156.4 2.2 collective-permute-start.11
  158.6 3.2 %collective-permute-start.10 = (bf16[96,2048]{1,0:T(8,128)(2,1)S(1)}, bf16[96,2048]{1,0:T(8,128)(2,1)S(1)}, u32[]{:S(2)}, u32[]{:S(2)}) collective-permute-start(bf16[96,2048]{1,0:T(8,128)(2,1)S(1)} %get-tuple-element.149), channel_id=1, source_target_pairs={{0,96},{16,112},{32,0},{48,16},{64,32},{80,48},{96,64},{112,80},{1... | collective-permute-start | bytes 1179656 | tf_op jit(solution)/shard_map/ppermute | solution.py:1044
  161.8 2.0 collective-permute-done.11.b
  163.9 1.3 collective-permute-start.13
  165.9 4.4 %project_out.1 = bf16[256,768]{1,0:T(8,128)(2,1)} custom-call(bf16[256,768]{1,0:T(8,128)(2,1)} %bitcast.34, bf16[256,1536]{1,0:T(8,128)(2,1)} %get-tuple-element.154.n16, bf16[3072,768]{1,0:T(8,128)(2,1)} %all-gather.2.cloned.1.call-done.rest), custom_call_target="tpu_custom_call" | custom-call | flops 603979776 | bytes 6291456 | tf_op jit(solution)/shard_map/project_out/pallas_call | solution.py:855
  170.4 1.4 add_dynamic-update-slice_fusion
  171.8 2.1 collective-permute-done.12.half
  173.8 1.0 collective-permute-done.9.one
  174.9 1.1 copy-done.1
  176.9 20.5 %all_to_all.30.recv = bf16[16,240,128]{2,1,0:T(8,128)(2,1)S(1)} all-to-all(bf16[16,240,128]{2,1,0:T(8,128)(2,1)S(1)} %add_y.1), channel_id=1, replica_groups=mesh['dp'=8,'seq'=16] {'seq'}, dimensions={0} | all-to-all | bytes 1966080 | tf_op jit(solution)/shard_map/all_to_all | solution.py:882
  197.5 16.3 %all_to_all.31.sums = bf16[16,240,128]{2,1,0:T(8,128)(2,1)S(1)} all-to-all(bf16[16,240,128]{2,1,0:T(8,128)(2,1)S(1)} %add_seq.1), channel_id=1, replica_groups=mesh['dp'=8,'seq'=16] {'seq'}, dimensions={0} | all-to-all | bytes 1966080 | tf_op jit(solution)/shard_map/all_to_all | solution.py:882
  213.8 1.4 finish.1
  (93 shorter events, 22.0 us)
Async XLA Ops:
  7.2 14.3 %copy-start.15 = (bf16[192,768]{1,0:T(8,128)(2,1)S(1)}, bf16[192,768]{1,0:T(8,128)(2,1)}, u32[]{:S(2)}) copy-start(bf16[192,768]{1,0:T(8,128)(2,1)} %param.26) | copy-start | bytes 884740
  7.2 64.7 %all-gather.2.cloned.1.call-start = ((), (), s32[]{:S(2)}) async-start(), calls=%async_computation.7 | async-start | bytes 5308416 | tf_op jit(solution)/shard_map/all_gather | solution.py:919
  9.1 13.2 %copy-start.21 = (f32[24]{0:T(128)S(1)}, f32[24]{0:T(128)}, u32[]{:S(2)}) copy-start(f32[24]{0:T(128)} %param.23) | copy-start | bytes 292
  9.1 13.2 %copy-start.22 = (f32[48]{0:T(128)S(1)}, f32[48]{0:T(128)}, u32[]{:S(2)}) copy-start(f32[48]{0:T(128)} %param.22) | copy-start | bytes 580
  9.1 23.4 %copy-start.6 = (bf16[96,1920]{1,0:T(8,128)(2,1)}, bf16[96,1920]{1,0:T(8,128)(2,1)S(1)}, u32[]{:S(2)}) copy-start(bf16[96,1920]{1,0:T(8,128)(2,1)S(1)} %fusion.2.refs_0_) | copy-start | bytes 1105924
  9.2 13.8 %copy-start.19 = (f32[768]{0:T(1024)S(1)}, f32[768]{0:T(1024)}, u32[]{:S(2)}) copy-start(f32[768]{0:T(1024)} %param.17) | copy-start | bytes 9220
  9.2 14.4 %copy-start.17 = (f32[1536]{0:T(1024)S(1)}, f32[1536]{0:T(1024)}, u32[]{:S(2)}) copy-start(f32[1536]{0:T(1024)} %param.25) | copy-start | bytes 18436
  9.2 15.0 %copy-start.18 = (f32[1792]{0:T(1024)S(1)}, f32[1792]{0:T(1024)}, u32[]{:S(2)}) copy-start(f32[1792]{0:T(1024)} %param.21) | copy-start | bytes 21508
  9.2 15.6 %copy-start.20 = (f32[24]{0:T(128)S(1)}, f32[24]{0:T(128)}, u32[]{:S(2)}) copy-start(f32[24]{0:T(128)} %param.24) | copy-start | bytes 292
  9.2 17.0 %collective-permute-start.4 = (bf16[96,1920]{1,0:T(8,128)(2,1)S(1)}, bf16[96,1920]{1,0:T(8,128)(2,1)S(1)}, u32[]{:S(2)}, u32[]{:S(2)}) collective-permute-start(bf16[96,1920]{1,0:T(8,128)(2,1)S(1)} %fusion.2.refs_0_), channel_id=1, source_target_pairs={{0,16},{16,0},{32,48},{48,32},{64,80},{80,64},{96,112},{112,96},{1... | collective-permute-start | bytes 1105928 | tf_op jit(solution)/shard_map/ppermute | solution.py:912
  9.3 19.5 %collective-permute-start.2 = (bf16[96,1920]{1,0:T(8,128)(2,1)S(1)}, bf16[96,1920]{1,0:T(8,128)(2,1)S(1)}, u32[]{:S(2)}, u32[]{:S(2)}) collective-permute-start(bf16[96,1920]{1,0:T(8,128)(2,1)S(1)} %fusion.2.refs_0_), channel_id=1, source_target_pairs={{0,96},{16,112},{32,0},{48,16},{64,32},{80,48},{96,64},{112,80},{1... | collective-permute-start | bytes 1105928 | tf_op jit(solution)/shard_map/ppermute | solution.py:910
  12.5 16.4 %collective-permute-start.1 = (bf16[96,1920]{1,0:T(8,128)(2,1)S(1)}, bf16[96,1920]{1,0:T(8,128)(2,1)S(1)}, u32[]{:S(2)}, u32[]{:S(2)}) collective-permute-start(bf16[96,1920]{1,0:T(8,128)(2,1)S(1)} %fusion.2.refs_0_), channel_id=1, source_target_pairs={{0,64},{16,80},{32,96},{48,112},{64,0},{80,16},{96,32},{112,48},{1... | collective-permute-start | bytes 1105928 | tf_op jit(solution)/shard_map/ppermute | solution.py:910
  13.1 19.4 %collective-permute-start = (bf16[96,1920]{1,0:T(8,128)(2,1)S(1)}, bf16[96,1920]{1,0:T(8,128)(2,1)S(1)}, u32[]{:S(2)}, u32[]{:S(2)}) collective-permute-start(bf16[96,1920]{1,0:T(8,128)(2,1)S(1)} %fusion.2.refs_0_), channel_id=1, source_target_pairs={{0,32},{16,48},{32,64},{48,80},{64,96},{80,112},{96,0},{112,16},{1... | collective-permute-start | bytes 1105928 | tf_op jit(solution)/shard_map/ppermute | solution.py:910
  14.8 11.4 %collective-permute-start.3 = (bf16[16,768]{1,0:T(8,128)(2,1)S(1)}, bf16[16,768]{1,0:T(8,128)(2,1)S(1)}, u32[]{:S(2)}, u32[]{:S(2)}) collective-permute-start(bf16[16,768]{1,0:T(8,128)(2,1)S(1)} %slice_bitcast_fusion), channel_id=1, source_target_pairs={{0,1},{1,2},{2,3},{3,4},{4,5},{5,6},{6,7},{7,8},{8,9},{9,10},{10,1... | collective-permute-start | bytes 73736 | tf_op jit(solution)/shard_map/ppermute | solution.py:911
  26.2 9.2 %copy-start.16 = (bf16[16,768]{1,0:T(8,128)(2,1)}, bf16[16,768]{1,0:T(8,128)(2,1)S(1)}, u32[]{:S(2)}) copy-start(bf16[16,768]{1,0:T(8,128)(2,1)S(1)} %collective-permute-done.3.halo) | copy-start | bytes 73732
  26.2 9.2 %copy-start.8 = (bf16[96,1920]{1,0:T(8,128)(2,1)}, bf16[96,1920]{1,0:T(8,128)(2,1)S(1)}, u32[]{:S(2)}) copy-start(bf16[96,1920]{1,0:T(8,128)(2,1)S(1)} %collective-permute-done.4.refs_4_) | copy-start | bytes 1105924
  32.6 1.8 collective-permute-start.5
  32.7 2.2 collective-permute-start.6
  33.2 2.2 %collective-permute-start.7 = (bf16[96,1920]{1,0:T(8,128)(2,1)S(1)}, bf16[96,1920]{1,0:T(8,128)(2,1)S(1)}, u32[]{:S(2)}, u32[]{:S(2)}) collective-permute-start(bf16[96,1920]{1,0:T(8,128)(2,1)S(1)} %collective-permute-done.2.refs_3_), channel_id=1, source_target_pairs={{0,16},{16,0},{32,48},{48,32},{64,80},{80,64},{96,112},{112,96},{1... | collective-permute-start | bytes 1105928 | tf_op jit(solution)/shard_map/ppermute | solution.py:918
  47.1 20.4 %all-to-all-start = ((bf16[16,48,384]{2,1,0:T(8,128)(2,1)}), bf16[16,48,384]{2,1,0:T(8,128)(2,1)S(1)}, u32[]{:S(2)}, u32[]{:S(2)}) async-start(bf16[16,48,384]{2,1,0:T(8,128)(2,1)} %get-tuple-element.115), calls=%async_computation | async-start | bytes 1179648 | tf_op jit(solution)/shard_map/all_to_all | solution.py:882
  68.3 12.8 %all-to-all-start.1 = ((bf16[16,32,384]{2,1,0:T(8,128)(2,1)}), bf16[16,32,384]{2,1,0:T(8,128)(2,1)S(1)}, u32[]{:S(2)}, u32[]{:S(2)}) async-start(bf16[16,32,384]{2,1,0:T(8,128)(2,1)} %scan_states.1), calls=%async_computation.1 | async-start | bytes 786432 | tf_op jit(solution)/shard_map/all_to_all | solution.py:882
  91.5 16.1 %all-to-all-start.2 = ((bf16[16,48,384]{2,1,0:T(8,128)(2,1)}), bf16[16,48,384]{2,1,0:T(8,128)(2,1)S(1)}, u32[]{:S(2)}, u32[]{:S(2)}) async-start(bf16[16,48,384]{2,1,0:T(8,128)(2,1)} %get-tuple-element.125), calls=%async_computation.2 | async-start | bytes 1179648 | tf_op jit(solution)/shard_map/all_to_all | solution.py:882
  95.2 79.7 %reduce-scatter.2.cloned.1.call-start = ((), (), s32[]{:S(2)}) async-start(), calls=%async_computation.8 | async-start | bytes 5308416 | tf_op jit(solution)/shard_map/reduce_scatter | solution.py:994
  108.5 22.9 %all-to-all-start.3 = ((bf16[16,32,384]{2,1,0:T(8,128)(2,1)}), bf16[16,32,384]{2,1,0:T(8,128)(2,1)S(1)}, u32[]{:S(2)}, u32[]{:S(2)}) async-start(bf16[16,32,384]{2,1,0:T(8,128)(2,1)} %scan_adjoints.1), calls=%async_computation.3 | async-start | bytes 786432 | tf_op jit(solution)/shard_map/all_to_all | solution.py:882
  132.2 14.4 %copy-start = (bf16[272,768]{1,0:T(8,128)(2,1)S(1)}, bf16[272,768]{1,0:T(8,128)(2,1)}, u32[]{:S(2)}) copy-start(bf16[272,768]{1,0:T(8,128)(2,1)} %get-tuple-element.110.u) | copy-start | bytes 1253380
  132.2 14.4 %copy-start.2 = (s32[22]{0:T(128)S(1)}, s32[22]{0:T(128)}, u32[]{:S(2)}) copy-start(s32[22]{0:T(128)} %stack.85.ids) | copy-start | bytes 268
  152.0 3.5 %collective-permute-start.8 = (bf16[4,96,2048]{2,1,0:T(8,128)(2,1)S(1)}, bf16[4,96,2048]{2,1,0:T(8,128)(2,1)S(1)}, u32[]{:S(2)}, u32[]{:S(2)}) collective-permute-start(bf16[4,96,2048]{2,1,0:T(8,128)(2,1)S(1)} %get-tuple-element.147), channel_id=1, source_target_pairs={{0,16},{16,0},{32,48},{48,32},{64,80},{80,64},{96,112},{112,96},{1... | collective-permute-start | bytes 4718600 | tf_op jit(solution)/shard_map/ppermute | solution.py:1035
  156.4 7.4 %collective-permute-start.11 = (bf16[96,1024]{1,0:T(8,128)(2,1)S(1)}, bf16[96,1024]{1,0:T(8,128)(2,1)S(1)}, u32[]{:S(2)}, u32[]{:S(2)}) collective-permute-start(bf16[96,1024]{1,0:T(8,128)(2,1)S(1)} %get-tuple-element.151), channel_id=1, source_target_pairs={{0,1},{1,0},{2,3},{3,2},{4,5},{5,4},{6,7},{7,6},{8,9},{9,8},{10,11... | collective-permute-start | bytes 589832 | tf_op jit(solution)/shard_map/ppermute | solution.py:1043
  158.6 16.3 %collective-permute-start.9 = (bf16[96,2048]{1,0:T(8,128)(2,1)S(1)}, bf16[96,2048]{1,0:T(8,128)(2,1)S(1)}, u32[]{:S(2)}, u32[]{:S(2)}) collective-permute-start(bf16[96,2048]{1,0:T(8,128)(2,1)S(1)} %get-tuple-element.148), channel_id=1, source_target_pairs={{0,32},{16,48},{32,64},{48,80},{64,96},{80,112},{96,0},{112,16},{1... | collective-permute-start | bytes 1179656 | tf_op jit(solution)/shard_map/ppermute | solution.py:1044
  158.6 16.3 %collective-permute-start.10 = (bf16[96,2048]{1,0:T(8,128)(2,1)S(1)}, bf16[96,2048]{1,0:T(8,128)(2,1)S(1)}, u32[]{:S(2)}, u32[]{:S(2)}) collective-permute-start(bf16[96,2048]{1,0:T(8,128)(2,1)S(1)} %get-tuple-element.149), channel_id=1, source_target_pairs={{0,96},{16,112},{32,0},{48,16},{64,32},{80,48},{96,64},{112,80},{1... | collective-permute-start | bytes 1179656 | tf_op jit(solution)/shard_map/ppermute | solution.py:1044
  163.9 6.5 %collective-permute-start.13 = (f32[16,768]{1,0:T(8,128)S(1)}, f32[16,768]{1,0:T(8,128)S(1)}, u32[]{:S(2)}, u32[]{:S(2)}) collective-permute-start(f32[16,768]{1,0:T(8,128)S(1)} %copy-done.23), channel_id=1, source_target_pairs={{1,0},{2,1},{3,2},{4,3},{5,4},{6,5},{7,6},{8,7},{9,8},{10,9},{11,1... | collective-permute-start | bytes 147464 | tf_op jit(solution)/shard_map/ppermute | solution.py:1049
  165.2 8.7 %collective-permute-start.12 = (bf16[96,1024]{1,0:T(8,128)(2,1)S(1)}, bf16[96,1024]{1,0:T(8,128)(2,1)S(1)}, u32[]{:S(2)}, u32[]{:S(2)}) collective-permute-start(bf16[96,1024]{1,0:T(8,128)(2,1)S(1)} %add_tail_z.1), channel_id=1, source_target_pairs={{0,64},{16,80},{32,96},{48,112},{64,0},{80,16},{96,32},{112,48},{1... | collective-permute-start | bytes 589832 | tf_op jit(solution)/shard_map/ppermute | solution.py:1048
  (12 other events, 31.5 us)
Sparse Core Ops, SparseCore 0:
  32.7 34.1 all-gather.1
  107.7 38.3 reduce-scatter.1
